TPU v7x, 128 devices: a whole 4x4x4 slice. The times are simulated.
128 devices in a mesh: focus: 2 (over x_lo), gx: 4 (over x_hi, core), gy: 16 (over y, z).
Axes of the slice: x: 4 (x_hi: 2, x_lo: 2; x = x_hi * 2 + x_lo), y: 4, z: 4, core: 2. Of those that a mesh axis runs over, the one named last changes fastest.
Arguments:
- level_set: float32 [4096, 8192], P('gx', 'gy'), may hold values from -12 to 12
- focus_grads: float32 [4, 4096, 8192], P('focus', 'gx', 'gy'), may hold values from -6 to 6
- focus_weight: float32 [4], P('focus'), may hold values from 0.3 to 3
Outputs:
- level_out: float32 [4096, 8192], P('gx', 'gy')
- velocity: float32 [4096, 8192], P('gx', 'gy')
All inputs are finite; a program needn't handle non-finite values. Where the computation divides by a largest or mean magnitude, that divisor is 1e-20 or more.
Results may differ from a plain program's by a relative error of at most 0.00002.
Values sent between devices are 32-bit elements; how exact they have to be, the bound alone decides.
No kernel may reach another device: no remote copies, remote signals or barrier semaphores. Data moves between devices by JAX's collectives and lax.ppermute only.
A program may use at most 128 MiB of HBM per device.

v0:
```python
import jax
import jax.numpy as jnp
from jax import lax
from jax.sharding import PartitionSpec as P

EXT_SWEEPS = 8
REINIT_ITERS = 10


band_cells = 3.0
cfl_number = 0.5
pseudo_step = 0.5


def padded_2(cells, sides, width):
    for axis, dim in sides:
        count = lax.axis_size(axis)
        head = lax.slice_in_dim(cells, 0, width, axis=dim)
        tail = lax.slice_in_dim(cells, cells.shape[dim] - width, cells.shape[dim], axis=dim)
        cells = jnp.concatenate(
            [
                lax.ppermute(tail, axis, [(i, (i + 1) % count) for i in range(count)]),
                cells,
                lax.ppermute(head, axis, [((i + 1) % count, i) for i in range(count)]),
            ],
            axis=dim,
        )
    return cells


def jacobi(padded, source, band):
    beside = padded[2:, 1:-1] + padded[:-2, 1:-1] + padded[1:-1, 2:] + padded[1:-1, :-2]
    return (band * source + beside) / (band + 4.0)


def hamiltonian(padded, speed):
    center = padded[1:-1, 1:-1]
    dxm = center - padded[:-2, 1:-1]
    dxp = padded[2:, 1:-1] - center
    dym = center - padded[1:-1, :-2]
    dyp = padded[1:-1, 2:] - center
    gplus = jnp.sqrt(
        jnp.maximum(dxm, 0.0) ** 2
        + jnp.minimum(dxp, 0.0) ** 2
        + jnp.maximum(dym, 0.0) ** 2
        + jnp.minimum(dyp, 0.0) ** 2
    )
    gminus = jnp.sqrt(
        jnp.minimum(dxm, 0.0) ** 2
        + jnp.maximum(dxp, 0.0) ** 2
        + jnp.minimum(dym, 0.0) ** 2
        + jnp.maximum(dyp, 0.0) ** 2
    )
    return jnp.maximum(speed, 0.0) * gplus + jnp.minimum(speed, 0.0) * gminus


def per_device(level_set, focus_grads, focus_weight):
    local_sum = jnp.sum(focus_weight[:, None, None] * focus_grads, axis=0)
    source = lax.psum(local_sum, "focus")
    band = 1.0 / (1.0 + (level_set / band_cells) ** 2)
    velocity = source
    for sweep in range(EXT_SWEEPS):
        velocity = jacobi(padded_2(velocity, (("gx", 0), ("gy", 1)), 1), source, band)
    top = lax.pmax(jnp.max(jnp.abs(velocity)), ("gx", "gy"))
    step = cfl_number / (top + 1e-06)
    advanced = level_set - step * hamiltonian(
        padded_2(level_set, (("gx", 0), ("gy", 1)), 1), velocity
    )
    sign = advanced / jnp.sqrt(advanced * advanced + 1.0)
    level_out = advanced
    for sweep in range(REINIT_ITERS):
        level_out = level_out - pseudo_step * (
            hamiltonian(padded_2(level_out, (("gx", 0), ("gy", 1)), 1), sign) - sign
        )
    return (level_out, velocity)


def solution(mesh):
    in_specs = (P("gx", "gy"), P("focus", "gx", "gy"), P("focus"))
    out_specs = (P("gx", "gy"), P("gx", "gy"))
    return jax.shard_map(
        per_device, mesh=mesh, in_specs=in_specs, out_specs=out_specs, check_vma=False
    )
```

profile of v0, /device:TPU:1, one launch (start us, length us, event | category | flops | bytes accessed | tf_op | source)
XLA Modules:
  0.0 830.7 jit_solution(15202758720373901149)
XLA Ops:
  7.2 4.4 multiply_reduce_fusion
  11.6 72.8 %all-reduce.2.cloned.1.call-done = f32[1024,512]{1,0:T(8,128)} async-done(((f32[1024,512]{1,0:T(8,128)}), f32[1024,512]{1,0:T(8,128)}) %all-reduce.2.cloned.1.call-update) | async-done | bytes 2097168 | tf_op jit(solution)/shard_map/psum | solution.py:59
  89.7 8.2 concatenate.306
  99.7 4.9 collective-permute-start.2
  105.6 5.0 collective-permute-done.3
  110.9 7.1 fusion.81
  119.3 4.2 collective-permute-start.4
  125.3 8.2 concatenate.311
  141.4 6.7 fusion.76
  149.5 4.0 collective-permute-start.8
  155.2 8.2 concatenate.316
  167.8 3.9 collective-permute-done.11
  171.9 6.7 fusion.71
  180.0 4.0 collective-permute-start.12
  185.7 8.2 concatenate.321
  201.8 6.7 fusion.66
  209.9 4.0 collective-permute-start.16
  215.7 8.2 concatenate.326
  231.8 6.7 fusion.61
  239.9 4.0 collective-permute-start.20
  245.6 8.2 concatenate.331
  261.9 6.7 fusion.56
  270.0 4.0 collective-permute-start.24
  275.7 8.2 concatenate.336
  285.8 4.8 collective-permute-start.26
  295.7 7.1 concatenate.346
  303.3 6.6 fusion.51
  316.9 8.2 concatenate.341
  332.0 4.2 collective-permute-done.31
  337.2 8.7 %abs_reduce_fusion = (f32[]{:T(128)}, f32[1024,512]{1,0:T(8,128)}) fusion(f32[1026,512]{1,0:T(8,128)} %concatenate.341, f32[1026,1]{1,0:T(8,128)} %copy.49, f32[1026,1]{1,0:T(8,128)} %copy.47, f32[1024,512]{1,0:T(8,128)} %copy-done.15, f32[1,512]{1,0:T(1,128)S(1)} %collective-permute-done.29, f32[1,512]{1,0:T(1,128)S(1)} %collective-permute-done.28, ...), kind=kLoop, calls=%fused_computation.173 | loop fusion | flops 8912895 | bytes 10502164 | tf_op jit(solution)/shard_map/reduce_max | solution.py:64
  345.9 132.1 %pmax.7 = f32[]{:T(128)} all-reduce(f32[]{:T(128)} %get-tuple-element.4), channel_id=1, replica_groups=mesh['focus'=2,'gx'=4,'gy'=16] {'gx','gy'}, use_global_device_ids=true, to_apply=%region_3.0 | all-reduce | flops 1 | bytes 8 | tf_op jit(solution)/shard_map/pmax | solution.py:64
  478.7 10.3 %multiply_subtract_fusion.10 = f32[1024,512]{1,0:T(8,128)S(1)} fusion(f32[1024,512]{1,0:T(8,128)} %param.3, f32[1024,512]{1,0:T(8,128)} %get-tuple-element.5, f32[1026,1]{1,0:T(8,128)S(1)} %copy.53, f32[1026,512]{1,0:T(8,128)} %concatenate.346, f32[1026,1]{1,0:T(8,128)S(1)} %copy.51, f32[1,512]{1,0:T(1,128)S(1)} %collective-permute-done.33, ...), kind=kLoop, calls=%fused_computation.172 | loop fusion | flops 19398656 | bytes 8405012 | tf_op jit(solution)/shard_map/sub | solution.py:66
  489.0 34.5 %collective-permute-start.37 = (f32[1,512]{1,0:T(1,128)S(1)}, f32[1,512]{1,0:T(1,128)S(1)}, u32[]{:S(2)}, u32[]{:S(2)}) collective-permute-start(f32[1,512]{1,0:T(1,128)S(1)} %get-tuple-element.62), channel_id=1, source_target_pairs={{16,0},{32,16},{48,32},{0,48},{17,1},{33,17},{49,33},{1,49},{18,2}... | collective-permute-start | bytes 6152 | tf_op jit(solution)/shard_map/ppermute | solution.py:24
  525.2 7.1 concatenate.351
  534.6 4.5 collective-permute-start.39
  540.3 7.8 multiply_subtract_fusion.9
  549.5 4.0 collective-permute-start.41
  555.2 5.2 concatenate.356
  561.1 5.5 collective-permute-start.43
  567.6 10.2 %multiply_subtract_fusion.8 = f32[1024,512]{1,0:T(8,128)S(1)} fusion(f32[1024,512]{1,0:T(8,128)} %copy-done.14, f32[1026,1]{1,0:T(8,128)S(1)} %copy.61, f32[1026,512]{1,0:T(8,128)} %copy-done.22, f32[1026,1]{1,0:T(8,128)S(1)} %copy.59, f32[1,512]{1,0:T(1,128)S(1)} %collective-permute-done.41, f32[1,512]{1,0:T(1,128)S(1)} %collective-permute-done.40, ...), kind=kLoop, calls=%fused_computation.169 | loop fusion | flops 21495808 | bytes 8405008 | tf_op jit(solution)/shard_map/sub | solution.py:72
  583.4 7.1 concatenate.361
  592.4 5.4 collective-permute-start.47
  599.0 7.9 multiply_subtract_fusion.7
  613.7 8.2 concatenate.366
  623.9 5.3 collective-permute-start.51
  630.3 7.9 multiply_subtract_fusion.6
  645.0 8.2 concatenate.371
  655.2 5.3 collective-permute-start.55
  661.8 7.9 multiply_subtract_fusion.5
  676.5 8.2 concatenate.376
  686.7 5.4 collective-permute-start.59
  693.1 7.9 multiply_subtract_fusion.4
  707.8 8.2 concatenate.381
  718.1 5.4 collective-permute-start.63
  724.6 7.9 multiply_subtract_fusion.3
  739.4 8.2 concatenate.386
  749.6 5.4 collective-permute-start.67
  756.0 7.9 multiply_subtract_fusion.2
  770.7 5.2 concatenate.391
  776.6 5.4 collective-permute-start.71
  783.2 10.2 %multiply_subtract_fusion.1 = f32[1024,512]{1,0:T(8,128)S(1)} fusion(f32[1024,512]{1,0:T(8,128)} %copy-done.12, f32[1026,1]{1,0:T(8,128)S(1)} %copy.89, f32[1026,512]{1,0:T(8,128)} %copy-done.23, f32[1026,1]{1,0:T(8,128)S(1)} %copy.87, f32[1,512]{1,0:T(1,128)S(1)} %collective-permute-done.69, f32[1,512]{1,0:T(1,128)S(1)} %collective-permute-done.68, ...), kind=kLoop, calls=%fused_computation.162 | loop fusion | flops 21495808 | bytes 8405008 | tf_op jit(solution)/shard_map/sub | solution.py:72
  799.0 7.1 concatenate.396
  808.0 5.4 collective-permute-start.75
  814.4 8.9 %multiply_subtract_fusion = f32[1024,512]{1,0:T(8,128)} fusion(f32[1024,512]{1,0:T(8,128)S(1)} %multiply_subtract_fusion.1, f32[1026,1]{1,0:T(8,128)S(1)} %copy.93, f32[1026,512]{1,0:T(8,128)} %concatenate.396, f32[1026,1]{1,0:T(8,128)S(1)} %copy.91, f32[1,512]{1,0:T(1,128)S(1)} %collective-permute-done.73, f32[1,512]{1,0:T(1,128)S(1)} %collective-permute-done.72, ...), kind=kLoop, calls=%fused_computation.161 | loop fusion | flops 21495808 | bytes 8405008 | tf_op jit(solution)/shard_map/sub | solution.py:72
  (293 shorter events, 170.0 us)
Async XLA Ops:
  7.2 77.3 %all-reduce.2.cloned.1.call-start = ((), (), s32[]{:S(2)}) async-start(), calls=%async_computation | async-start | bytes 4194304 | tf_op jit(solution)/shard_map/psum | solution.py:59
  85.2 4.5 collective-permute-start
  85.9 3.8 collective-permute-start.1
  99.7 5.7 collective-permute-start.2
  104.8 5.8 collective-permute-start.3
  119.3 5.9 collective-permute-start.4
  135.1 2.5 collective-permute-start.6
  135.4 5.8 collective-permute-start.7
  149.5 5.7 collective-permute-start.8
  165.0 2.5 collective-permute-start.10
  165.3 6.4 collective-permute-start.11
  180.0 5.7 collective-permute-start.12
  195.5 2.5 collective-permute-start.14
  195.8 5.8 collective-permute-start.15
  209.9 5.7 collective-permute-start.16
  225.5 2.5 collective-permute-start.18
  225.7 5.8 collective-permute-start.19
  239.9 5.7 collective-permute-start.20
  255.4 2.5 collective-permute-start.22
  255.7 6.0 collective-permute-start.23
  270.0 5.7 collective-permute-start.24
  285.7 17.3 %collective-permute-start.27 = (f32[1026,1]{0,1:T(1,128)S(1)}, f32[1026,1]{0,1:T(1,128)S(1)}, u32[]{:S(2)}, u32[]{:S(2)}) collective-permute-start(f32[1026,1]{0,1:T(1,128)S(1)} %copy.44), channel_id=1, source_target_pairs={{0,1},{1,2},{2,3},{3,4},{4,5},{5,6},{6,7},{7,8},{8,9},{9,10},{10,1... | collective-permute-start | bytes 12320 | tf_op jit(solution)/shard_map/ppermute | solution.py:22
  285.8 17.0 %collective-permute-start.26 = (f32[1026,1]{0,1:T(1,128)S(1)}, f32[1026,1]{0,1:T(1,128)S(1)}, u32[]{:S(2)}, u32[]{:S(2)}) collective-permute-start(f32[1026,1]{0,1:T(1,128)S(1)} %copy.42), channel_id=1, source_target_pairs={{1,0},{2,1},{3,2},{4,3},{5,4},{6,5},{7,6},{8,7},{9,8},{10,9},{11,1... | collective-permute-start | bytes 12320 | tf_op jit(solution)/shard_map/ppermute | solution.py:24
  290.6 5.1 collective-permute-start.33
  311.3 5.5 collective-permute-start.28
  314.2 2.7 collective-permute-start.29
  315.3 15.3 %collective-permute-start.35 = (f32[1026,1]{0,1:T(1,128)S(1)}, f32[1026,1]{0,1:T(1,128)S(1)}, u32[]{:S(2)}, u32[]{:S(2)}) collective-permute-start(f32[1026,1]{0,1:T(1,128)S(1)} %copy.52), channel_id=1, source_target_pairs={{1,0},{2,1},{3,2},{4,3},{5,4},{6,5},{7,6},{8,7},{9,8},{10,9},{11,1... | collective-permute-start | bytes 12320 | tf_op jit(solution)/shard_map/ppermute | solution.py:24
  315.4 15.0 %collective-permute-start.34 = (f32[1026,1]{0,1:T(1,128)S(1)}, f32[1026,1]{0,1:T(1,128)S(1)}, u32[]{:S(2)}, u32[]{:S(2)}) collective-permute-start(f32[1026,1]{0,1:T(1,128)S(1)} %copy.50), channel_id=1, source_target_pairs={{0,1},{1,2},{2,3},{3,4},{4,5},{5,6},{6,7},{7,8},{8,9},{9,10},{10,1... | collective-permute-start | bytes 12320 | tf_op jit(solution)/shard_map/ppermute | solution.py:22
  326.7 4.2 collective-permute-start.30
  330.3 5.8 collective-permute-start.31
  489.0 36.2 %collective-permute-start.37 = (f32[1,512]{1,0:T(1,128)S(1)}, f32[1,512]{1,0:T(1,128)S(1)}, u32[]{:S(2)}, u32[]{:S(2)}) collective-permute-start(f32[1,512]{1,0:T(1,128)S(1)} %get-tuple-element.62), channel_id=1, source_target_pairs={{16,0},{32,16},{48,32},{0,48},{17,1},{33,17},{49,33},{1,49},{18,2}... | collective-permute-start | bytes 6152 | tf_op jit(solution)/shard_map/ppermute | solution.py:24
  523.5 1.7 collective-permute-start.36
  534.0 5.8 collective-permute-start.38
  534.6 5.4 collective-permute-start.39
  549.5 5.7 collective-permute-start.41
  553.5 1.7 collective-permute-start.40
  560.8 6.1 collective-permute-start.42
  561.1 6.3 collective-permute-start.43
  577.9 5.5 collective-permute-start.45
  581.7 1.7 collective-permute-start.44
  592.1 6.4 collective-permute-start.46
  592.4 6.3 collective-permute-start.47
  608.2 5.5 collective-permute-start.49
  623.7 6.1 collective-permute-start.50
  623.9 6.1 collective-permute-start.51
  639.6 5.5 collective-permute-start.53
  655.0 6.3 collective-permute-start.54
  655.2 6.3 collective-permute-start.55
  671.1 5.5 collective-permute-start.57
  686.5 6.1 collective-permute-start.58
  686.7 6.1 collective-permute-start.59
  702.4 5.5 collective-permute-start.61
  717.8 6.4 collective-permute-start.62
  718.1 6.3 collective-permute-start.63
  733.9 5.5 collective-permute-start.65
  749.3 6.1 collective-permute-start.66
  749.6 6.2 collective-permute-start.67
  765.3 5.4 collective-permute-start.69
  776.3 6.4 collective-permute-start.70
  776.6 6.3 collective-permute-start.71
  793.4 5.5 collective-permute-start.73
  797.3 1.7 collective-permute-start.72
  807.7 6.1 collective-permute-start.74
  808.0 6.2 collective-permute-start.75
  (37 other events, 172.8 us)
Sparse Core Ops, SparseCore 0:
  11.7 72.6 all-reduce.1
where the time goes:
time: 845 us; the launch traced here: 831 us
  local copies, waits for them, and re-layouts  206 us (24%)
  starting transfers between devices  189 us (22%)
  other arithmetic  156 us (18%)
  blocking collectives  132 us (16%)
  waiting for transfers between devices  131 us (16%)
  between operations  16.2 us (2%)
    ppermute x38, starting transfers between devices, padded_2(): lax.ppermute(head, axis, [((i + 1) % count, i) for i in range(count)])  166 us
    concatenate x19, local copies, waits for them, and re-layouts, padded_2(): jnp.concatenate([lax.ppermute(tail, axis, [(i, (i + 1) % count) for i in...  145 us
    pmax x1, blocking collectives, per_device(): top = lax.pmax(jnp.max(jnp.abs(velocity)), ('gx', 'gy'))  132 us
    sub x10, other arithmetic, per_device(): level_out - pseudo_step * (hamiltonian(padded_2(level_out, (('gx', 0), ('...  84.9 us
    psum x1, waiting for transfers between devices, per_device(): source = lax.psum(local_sum, 'focus')  72.8 us
    div x7, other arithmetic, jacobi(): return (band * source + beside) / (band + 4.0)  47.5 us
    ppermute x38, waiting for transfers between devices, padded_2(): lax.ppermute(tail, axis, [(i, (i + 1) % count) for i in range(count)])  32.8 us
    ppermute x38, waiting for transfers between devices, padded_2(): lax.ppermute(head, axis, [((i + 1) % count, i) for i in range(count)])  25.4 us
  transfers between devices with their start and end apart: 77, of which 44 were waited for; matrix products, arithmetic and copies ran while one was open for 3% of the time, Pallas kernels for 0%

commit v1 on v0

v1 whole, which is shorter than its diff:
```python
import functools

import jax
import jax.numpy as jnp
from jax import lax
from jax.experimental import pallas as pl
from jax.experimental.pallas import tpu as pltpu
from jax.sharding import PartitionSpec as P

EXT_SWEEPS = 8
REINIT_ITERS = 10
band_cells = 3.0
cfl_number = 0.5
pseudo_step = 0.5

HALO = 24
LANES = 128
TINY = 1e-18

VMEM = pl.BlockSpec(memory_space=pltpu.VMEM)
SMEM = pl.BlockSpec(memory_space=pltpu.SMEM)
ANY = pl.BlockSpec(memory_space=pl.ANY)


def call(body, out_shapes, in_specs, scratch=(), name=None, flops=0, out_specs=None, aliases=None):
    outs = [jax.ShapeDtypeStruct(s, jnp.float32) for s in out_shapes]
    return pl.pallas_call(
        body,
        out_shape=outs,
        in_specs=in_specs,
        out_specs=out_specs or [VMEM] * len(outs),
        scratch_shapes=list(scratch),
        name=name,
        input_output_aliases=aliases or {},
        compiler_params=pltpu.CompilerParams(vmem_limit_bytes=50 << 20),
        cost_estimate=pl.CostEstimate(flops=flops, bytes_accessed=1 << 20, transcendentals=0),
    )


def aligned(x, n=8):
    return pl.multiple_of(x, n)


def send_part(f_ref, w_ref, g_ref, send_ref, buf, sems):
    rows = send_ref.shape[0]
    start = aligned((1 - f_ref[0]) * (g_ref.shape[1] - rows))
    chunks = sems.shape[0]
    step = rows // 8 // chunks * 8
    spans = [(i * step, step if i < chunks - 1 else rows - i * step) for i in range(chunks)]
    copies = [
        pltpu.make_async_copy(
            g_ref.at[:, pl.ds(aligned(start + at), n), :], buf.at[:, pl.ds(at, n), :], sems.at[i]
        )
        for i, (at, n) in enumerate(spans)
    ]
    for copy in copies:
        copy.start()
    for copy, (at, n) in zip(copies, spans):
        copy.wait()
        send_ref[at : at + n, :] = w_ref[0] * buf[0, at : at + n, :] + w_ref[1] * buf[1, at : at + n, :]


def strips(w_ref, g_ref, ls_ref, p_ref, left_ref, right_ref):
    rows, cols = ls_ref.shape

    def chunk(i, _):
        at = pl.ds(aligned(i * LANES, LANES), LANES)
        p_ref[at, :] = w_ref[0] * g_ref[0, at, :] + w_ref[1] * g_ref[1, at, :]
        for n, ref in enumerate((p_ref, ls_ref)):
            to = slice(n * HALO, (n + 1) * HALO)
            left_ref[to, at] = ref[at, 0:LANES].T[0:HALO, :]
            right_ref[to, at] = ref[at, cols - LANES : cols].T[LANES - HALO :, :]
        return 0

    lax.fori_loop(0, rows // LANES, chunk, 0)


def turned(right, left):
    gap = jnp.zeros((LANES - 2 * HALO, right.shape[1]), jnp.float32)
    return jnp.concatenate([right, gap, left], axis=0).T


def row_messages(f_ref, right_ref, left_ref, p_ref, ls_ref, pcol_ref, lscol_ref, fs_ref, m1_ref, m2_ref):
    rows, cols = ls_ref.shape
    f = f_ref[0]

    def chunk(i, _):
        at = pl.ds(aligned(i * LANES, LANES), LANES)
        for n, ref in enumerate((pcol_ref, lscol_ref)):
            of = slice(n * HALO, (n + 1) * HALO)
            ref[at, :] = turned(right_ref[of, at], left_ref[of, at])
        return 0

    lax.fori_loop(0, rows // LANES, chunk, 0)
    width = fs_ref.shape[1]
    theirs = pl.ds(aligned((1 - f) * (rows - width), LANES), width)
    fs_ref[0:HALO, :] = right_ref[0:HALO, theirs]
    fs_ref[HALO:, :] = left_ref[0:HALO, theirs]
    outer = pl.ds(aligned((1 - f) * (rows - HALO)), HALO)
    inner = pl.ds(aligned(f * (rows - HALO)), HALO)
    m1_ref[0:HALO, 0:cols] = p_ref[outer, :]
    m1_ref[0:HALO, cols:] = pcol_ref[outer, :]
    m1_ref[HALO:, 0:cols] = ls_ref[outer, :]
    m1_ref[HALO:, cols:] = lscol_ref[outer, :]
    m2_ref[:, 0:cols] = p_ref[inner, :]
    m2_ref[:, cols:] = pcol_ref[inner, :]


def spread(nat, r, lo, width):
    return jnp.concatenate(
        [nat[c, pl.ds(lo, 8, stride=r), :] for c in range(width // LANES)], axis=1
    )


def unspread(nat, r, lo, value):
    for c in range(value.shape[1] // LANES):
        nat[c, pl.ds(lo, 8, stride=r), :] = value[:, c * LANES : (c + 1) * LANES]


def put(nat, rows, value, first=0):
    for c in range(value.shape[1] // LANES):
        nat[first + c, rows, :] = value[:, c * LANES : (c + 1) * LANES]


def half_setup(
    f_ref, p_ref, ls_ref, pcol_ref, lscol_ref, m1_ref, m2_ref, fs_ref, t_ref, lsx_ref, q_ref, rec_ref
):
    rows, cols = ls_ref.shape
    f = f_ref[0]
    ext = t_ref.shape[1]
    main = ext - HALO
    first = aligned((1 - f) * HALO)
    beside = pl.ds(aligned(f * main), HALO)
    put(t_ref, beside, m1_ref[0:HALO, :] + m2_ref[...])
    put(lsx_ref, beside, m1_ref[HALO:, :])
    width = fs_ref.shape[1]
    skip = aligned(f * (width - main))
    start = aligned(f * (rows - main))
    for i in range(main // 8):
        to = pl.ds(aligned(first + i * 8), 8)
        of = pl.ds(aligned(start + i * 8), 8)
        put(t_ref, to, p_ref[of, :])
        put(lsx_ref, to, ls_ref[of, :])
        put(t_ref, to, pcol_ref[of, :], cols // LANES)
        put(lsx_ref, to, lscol_ref[of, :], cols // LANES)
    theirs = turned(fs_ref[0:HALO, :], fs_ref[HALO:, :])
    last = cols // LANES

    @pl.when(f == 0)
    def _():
        t_ref[last, HALO : HALO + main, :] = t_ref[last, HALO : HALO + main, :] + theirs[0:main, :]

    @pl.when(f == 1)
    def _():
        t_ref[last, 0:main, :] = t_ref[last, 0:main, :] + theirs[width - main :, :]

    r = ext // 8

    def chunk(k, _):
        x = spread(lsx_ref, r, k, cols + LANES) * (1.0 / band_cells)
        u = x * x
        q = 1.0 / (5.0 + 4.0 * u)
        q_ref[k] = q
        rec_ref[k] = (1.0 + u) * q
        return 0

    lax.fori_loop(0, r, chunk, 0, unroll=2)


def wrap(ref, r):
    ref[0] = pltpu.roll(ref[r], 1, 0)
    ref[r + 1] = pltpu.roll(ref[1], 7, 0)


def sweep(src, r, body, unroll):
    def steps(i, carry):
        up, centre = carry
        for j in range(unroll):
            k = i * unroll + j
            down = src[k + 2]
            body(k, up, centre, down)
            up, centre = centre, down
        return up, centre

    lax.fori_loop(0, r // unroll, steps, (src[0], src[1]))


def divisor(r, most):
    return max(d for d in range(1, most + 1) if r % d == 0)


def half_velocity(f_ref, t_ref, rp_ref, q_ref, rec_ref, vx_ref, msg_ref, top_ref, sum_ref, a_ref, v0, v1):
    cols = rp_ref.shape[1]
    ext = t_ref.shape[1]
    r = ext // 8
    first = (1 - f_ref[0]) * HALO
    main = rp_ref.shape[0]

    def add(i, _):
        to = pl.ds(aligned(first + i * 8), 8)
        of = pl.ds(aligned(i * 8), 8)
        for c in range(cols // LANES):
            sum_ref[c, to, :] = t_ref[c, to, :] + rp_ref[of, c * LANES : (c + 1) * LANES]
        return 0

    lax.fori_loop(0, main // 8, add, 0, unroll=True)
    width = cols + LANES
    beside = pl.ds(aligned(f_ref[0] * main), HALO)
    for c in range(cols // LANES):
        sum_ref[c, beside, :] = t_ref[c, beside, :]

    def load(k, _):
        source = jnp.concatenate(
            [spread(sum_ref, r, k, cols), t_ref[cols // LANES, pl.ds(k, 8, stride=r), :]], axis=1
        )
        v0[k + 1] = source
        a_ref[k] = source * q_ref[k]
        return 0

    lax.fori_loop(0, r, load, 0, unroll=divisor(r, 10))
    wrap(v0, r)
    src, dst = v0, v1
    for s in range(EXT_SWEEPS):
        last = s == EXT_SWEEPS - 1

        def body(k, up, centre, down):
            beside = (up + down) + (pltpu.roll(centre, 1, 1) + pltpu.roll(centre, width - 1, 1))
            value = a_ref[k] + rec_ref[k] * beside
            if last:
                unspread(vx_ref, r, k, value)
            else:
                dst[k + 1] = value

        sweep(src, r, body, divisor(r, 10))
        if not last:
            wrap(dst, r)
        src, dst = dst, src
    half = msg_ref.shape[0] - 2 * HALO
    top = jnp.zeros((8, LANES), jnp.float32)
    for i in range(half // 8):
        for c in range(cols // LANES):
            value = vx_ref[c, HALO + i * 8 : HALO + i * 8 + 8, :]
            top = jnp.maximum(top, jnp.abs(value))
            msg_ref[i * 8 : i * 8 + 8, c * LANES : (c + 1) * LANES] = value
    for i in range(half // LANES):
        side = vx_ref[cols // LANES, HALO + i * LANES : HALO + (i + 1) * LANES, :].T
        msg_ref[half : half + HALO, i * LANES : (i + 1) * LANES] = side[0:HALO, :]
        msg_ref[half + HALO :, i * LANES : (i + 1) * LANES] = side[LANES - HALO :, :]
    top_ref[...] = jnp.full(top_ref.shape, jnp.max(top), jnp.float32)


def speeds(sigma, centre, up, down, left, right):
    a = jnp.maximum(sigma * (centre - up), TINY)
    b = jnp.maximum(sigma * (centre - down), 0.0)
    c = jnp.maximum(sigma * (centre - left), 0.0)
    d = jnp.maximum(sigma * (centre - right), 0.0)
    return (a * a + b * b) + (c * c + d * d)


def reinit(top_ref, ls_nat, v_nat, base, r, out_nat, p0, p1, h_ref, s_ref, width):
    step = cfl_number / (jnp.max(top_ref[...]) + 1e-06)
    unroll = divisor(r, 10)

    def load(k, _):
        p0[k + 1] = spread(ls_nat, r, base + k, width)
        return 0

    lax.fori_loop(0, r, load, 0, unroll=unroll)
    wrap(p0, r)

    def advance(k, up, centre, down):
        speed = spread(v_nat, r, base + k, width)
        sigma = jnp.where(speed >= 0.0, 1.0, -1.0)
        total = speeds(sigma, centre, up, down, pltpu.roll(centre, 1, 1), pltpu.roll(centre, width - 1, 1))
        advanced = centre - step * (speed * (total * lax.rsqrt(total)))
        p1[k + 1] = advanced
        h_ref[k] = pseudo_step * (advanced * lax.rsqrt(advanced * advanced + 1.0))
        s_ref[k] = jnp.where(advanced >= 0.0, 1.0, -1.0)

    sweep(p0, r, advance, unroll)
    wrap(p1, r)
    src, dst = p1, p0
    for it in range(REINIT_ITERS):
        last = it == REINIT_ITERS - 1

        def body(k, up, centre, down):
            total = speeds(
                s_ref[k], centre, up, down, pltpu.roll(centre, 1, 1), pltpu.roll(centre, width - 1, 1)
            )
            h = h_ref[k]
            value = (centre + h) - h * (total * lax.rsqrt(total))
            if last:
                unspread(out_nat, r, k, value[:, 0 : width - LANES])
            else:
                dst[k + 1] = value

        sweep(src, r, body, unroll)
        if not last:
            wrap(dst, r)
        src, dst = dst, src


def outer_part(f_ref, top_ref, lsx_ref, vx_ref, out_ref, nat, p0, p1, h_ref, s_ref):
    n, cols = out_ref.shape
    r = (n + 2 * HALO) // 8
    base = f_ref[0] * (lsx_ref.shape[1] - 8 * r)
    reinit(top_ref, lsx_ref, vx_ref, base, r, nat, p0, p1, h_ref, s_ref, cols + LANES)
    for c in range(cols // LANES):
        out_ref[:, c * LANES : (c + 1) * LANES] = nat[c, HALO : HALO + n, :]


def middle_part(
    f_ref, top_ref, vx_ref, msg_ref, got_ref, ls_ref, lscol_ref, mine_ref, level_ref, vel_ref,
    nat, lsn, vn, p0, p1, h_ref, s_ref,
):
    rows, cols = ls_ref.shape
    f = f_ref[0]
    ext = lsn.shape[1]
    r = ext // 8
    low = (rows - ext) // 2
    last = cols // LANES
    half = rows // 2
    side = turned(got_ref[half : half + HALO, :], got_ref[half + HALO :, :])
    for c in range(last + 1):
        for i in range(ext // 8):
            at = low + i * 8
            lanes = slice(c * LANES, (c + 1) * LANES)
            lsn[c, i * 8 : i * 8 + 8, :] = lscol_ref[at : at + 8, :] if c == last else ls_ref[at : at + 8, lanes]

    @pl.when(f == 0)
    def _():
        cut = half - low
        for c in range(last + 1):
            lanes = slice(c * LANES, (c + 1) * LANES)
            vn[c, 0:cut, :] = vx_ref[c, HALO + low : HALO + half, :]
            vn[c, cut:, :] = side[0 : ext - cut, :] if c == last else got_ref[0 : ext - cut, lanes]
        vel_ref[0:half, :] = msg_ref[0:half, :]
        vel_ref[half:, :] = got_ref[0:half, :]

    @pl.when(f == 1)
    def _():
        cut = half - low
        for c in range(last + 1):
            lanes = slice(c * LANES, (c + 1) * LANES)
            vn[c, 0:cut, :] = side[low:half, :] if c == last else got_ref[low:half, lanes]
            vn[c, cut:, :] = vx_ref[c, HALO : HALO + ext - cut, :]
        vel_ref[0:half, :] = got_ref[0:half, :]
        vel_ref[half:, :] = msg_ref[0:half, :]

    reinit(top_ref, lsn, vn, 0, r, nat, p0, p1, h_ref, s_ref, cols + LANES)
    n = mine_ref.shape[0]
    for c in range(last):
        level_ref[low + HALO : low + ext - HALO, c * LANES : (c + 1) * LANES] = nat[c, HALO : ext - HALO, :]
    level_ref[pl.ds(aligned(f * (rows - n)), n), :] = mine_ref[...]


def insert(f_ref, got_ref, _, level_ref, sem):
    n = got_ref.shape[0]
    to = pl.ds(aligned((1 - f_ref[0]) * (level_ref.shape[0] - n)), n)
    copy = pltpu.make_async_copy(got_ref, level_ref.at[to, :], sem)
    copy.start()
    copy.wait()


def shifted(n, by):
    return [(i, (i + by) % n) for i in range(n)]


def per_device(level_set, focus_grads, focus_weight):
    rows, cols = level_set.shape
    half = rows // 2
    gx, gy = lax.axis_size("gx"), lax.axis_size("gy")
    f = lax.axis_index("focus").reshape(1).astype(jnp.int32)
    planes = focus_grads.shape[0]
    assert planes == 2 and lax.axis_size("focus") == 2
    swap = [(0, 1), (1, 0)]
    main, ext, wide = half + HALO, half + 2 * HALO, cols + LANES
    slabs = wide // LANES

    (to_partner,) = call(
        send_part,
        [(main, cols)],
        [SMEM, SMEM, ANY],
        [pltpu.VMEM((planes, main, cols), jnp.float32), pltpu.SemaphoreType.DMA((4,))],
        "send_part",
    )(f, focus_weight, focus_grads)
    from_partner = lax.ppermute(to_partner, "focus", swap)

    p, left, right = call(
        strips, [(rows, cols), (2 * HALO, rows), (2 * HALO, rows)], [SMEM, VMEM, VMEM], (), "strips"
    )(focus_weight, focus_grads, level_set)
    from_right = lax.ppermute(left, "gy", shifted(gy, -1))
    from_left = lax.ppermute(right, "gy", shifted(gy, 1))
    side = -(-main // LANES) * LANES
    pcol, lscol, fs, m1, m2 = call(
        row_messages,
        [(rows, LANES), (rows, LANES), (2 * HALO, side), (2 * HALO, wide), (HALO, wide)],
        [SMEM, VMEM, VMEM, VMEM, VMEM],
        (),
        "row_messages",
    )(f, from_right, from_left, p, level_set)

    def place(f, x):
        return f * gx + x % gx

    same = [(place(0, x), place(0, x + 1)) for x in range(gx)] + [(place(1, x), place(1, x - 1)) for x in range(gx)]
    cross = [(place(0, x), place(1, x - 1)) for x in range(gx)] + [(place(1, x), place(0, x + 1)) for x in range(gx)]
    got1 = lax.ppermute(m1, ("focus", "gx"), same)
    got2 = lax.ppermute(m2, ("focus", "gx"), cross)
    got_fs = lax.ppermute(fs, "focus", swap)
    r = ext // 8
    t, lsx, q, rec = call(
        half_setup,
        [(slabs, ext, LANES), (slabs, ext, LANES), (r, 8, wide), (r, 8, wide)],
        [SMEM] + [VMEM] * 7,
        (),
        "half_setup",
    )(f, p, level_set, pcol, lscol, got1, got2, got_fs)
    devices = 2 * gx * gy
    vx, msg, top = call(
        half_velocity,
        [(slabs, ext, LANES), (half + 2 * HALO, cols), (devices, 8, LANES)],
        [SMEM] + [VMEM] * 4,
        [pltpu.VMEM((cols // LANES, ext, LANES), jnp.float32), pltpu.VMEM((r, 8, wide), jnp.float32)]
        + [pltpu.VMEM((r + 2, 8, wide), jnp.float32)] * 2,
        "half_velocity",
    )(f, t, from_partner, q, rec)
    got_msg = lax.ppermute(msg, "focus", swap)
    tops = lax.all_to_all(top, ("focus", "gx", "gy"), 0, 0)

    own = rows // 4
    r1 = (own + 2 * HALO) // 8
    (mine,) = call(
        outer_part,
        [(own, cols)],
        [SMEM] + [VMEM] * 3,
        [pltpu.VMEM((cols // LANES, 8 * r1, LANES), jnp.float32)]
        + [pltpu.VMEM((r1 + 2, 8, wide), jnp.float32)] * 2
        + [pltpu.VMEM((r1, 8, wide), jnp.float32)] * 2,
        "outer_part",
    )(f, tops, lsx, vx)
    theirs = lax.ppermute(mine, "focus", swap)
    mid = rows - 2 * own + 2 * HALO
    r2 = mid // 8
    level, velocity = call(
        middle_part,
        [(rows, cols), (rows, cols)],
        [SMEM] + [VMEM] * 7,
        [pltpu.VMEM((cols // LANES, mid, LANES), jnp.float32)]
        + [pltpu.VMEM((slabs, mid, LANES), jnp.float32)] * 2
        + [pltpu.VMEM((r2 + 2, 8, wide), jnp.float32)] * 2
        + [pltpu.VMEM((r2, 8, wide), jnp.float32)] * 2,
        "middle_part",
    )(f, tops, vx, msg, got_msg, level_set, lscol, mine)
    (level,) = call(
        insert,
        [(rows, cols)],
        [SMEM, VMEM, ANY],
        [pltpu.SemaphoreType.DMA(())],
        "insert",
        out_specs=[ANY],
        aliases={2: 0},
    )(f, theirs, level)
    return level, velocity


def solution(mesh):
    in_specs = (P("gx", "gy"), P("focus", "gx", "gy"), P("focus"))
    out_specs = (P("gx", "gy"), P("gx", "gy"))
    return jax.shard_map(
        per_device, mesh=mesh, in_specs=in_specs, out_specs=out_specs, check_vma=False
    )
```

time: 845 us -> 142 us (0.17); the launches traced: 831 us -> 142 us
  local copies, waits for them, and re-layouts: 206 us -> 3.11 us
  starting transfers between devices: 189 us -> 13.9 us
  other arithmetic: 156 us -> 0 us
  waiting for transfers between devices: 131 us -> 12.9 us
  blocking collectives: 132 us -> 37.9 us
  Pallas kernels: 0 us -> 73.5 us
  between operations: 16.2 us -> 0.7 us
    ppermute x76 -> x8, starting transfers between devices: 189 us -> 13.9 us  [the longest x1 6.28 us: per_device(): from_right = lax.ppermute(left, 'gy', shifted(gy, -1))]
    concatenate x19 -> x0, local copies, waits for them, and re-layouts: 145 us -> none  [padded_2(): jnp.concatenate([lax.ppermute(tail, axis, [(i, (i + 1) % count) for i in...]
    pmax x1 -> x0, blocking collectives: 132 us -> none  [per_device(): top = lax.pmax(jnp.max(jnp.abs(velocity)), ('gx', 'gy'))]
    sub x11 -> x0, other arithmetic: 95.2 us -> none  [the longest x10 84.9 us: per_device(): level_out - pseudo_step * (hamiltonian(padded_2(level_out, (('gx', 0), ('...]
    pallas_call x0 -> x8, Pallas kernels: none -> 73.5 us  [the longest x1 22.7 us: per_device(): call(outer_part, [(own, cols)], [SMEM] + [VMEM] * 3, [pltpu.VMEM((cols //...]
    psum x1 -> x0, waiting for transfers between devices: 72.8 us -> none  [per_device(): source = lax.psum(local_sum, 'focus')]
    div x7 -> x0, other arithmetic: 47.5 us -> none  [jacobi(): return (band * source + beside) / (band + 4.0)]
    ppermute x76 -> x8, waiting for transfers between devices: 58.2 us -> 12.9 us  [the longest x1 5.22 us: per_device(): from_left = lax.ppermute(right, 'gy', shifted(gy, 1))]
  transfers between devices with their start and end apart: 77 -> 8, of which waited for: 44 -> 4; matrix products, arithmetic and copies ran while one was open for 3% -> 0% of each run, Pallas kernels for 0% -> 40%
where the time goes in v1:
time: 142 us
  Pallas kernels  73.5 us (52%)
  blocking collectives  37.9 us (27%)
  starting transfers between devices  13.9 us (10%)
  waiting for transfers between devices  12.9 us (9%)
  local copies, waits for them, and re-layouts  3.11 us (2%)
    all_to_all x1, blocking collectives, per_device(): tops = lax.all_to_all(top, ('focus', 'gx', 'gy'), 0, 0)  37.9 us
    pallas_call x1, Pallas kernels, per_device(): call(outer_part, [(own, cols)], [SMEM] + [VMEM] * 3, [pltpu.VMEM((cols //...  22.7 us
    pallas_call x1, Pallas kernels, per_device(): call(middle_part, [(rows, cols), (rows, cols)], [SMEM] + [VMEM] * 7, [plt...  22.3 us
    pallas_call x1, Pallas kernels, per_device(): call(half_velocity, [(slabs, ext, LANES), (half + 2 * HALO, cols), (devic...  13.9 us
    ppermute x1, starting transfers between devices, per_device(): from_right = lax.ppermute(left, 'gy', shifted(gy, -1))  6.28 us
    pallas_call x1, Pallas kernels, per_device(): call(half_setup, [(slabs, ext, LANES), (slabs, ext, LANES), (r, 8, wide),...  5.28 us
    ppermute x1, waiting for transfers between devices, per_device(): from_left = lax.ppermute(right, 'gy', shifted(gy, 1))  5.22 us
    ppermute x1, starting transfers between devices, per_device(): got1 = lax.ppermute(m1, ('focus', 'gx'), same)  4.57 us
  transfers between devices with their start and end apart: 8, of which 4 were waited for; matrix products, arithmetic and copies ran while one was open for 0% of the time, Pallas kernels for 40%

profile of v1, /device:TPU:1, one launch (start us, length us, event | category | flops | bytes accessed | tf_op | source)
XLA Modules:
  0.0 142.0 jit_solution(1063972206008740941)
XLA Ops:
  0.6 0.0 copy-start.4
  0.6 0.6 copy-done.4
  1.3 2.2 %send_part.1 = f32[536,512]{1,0:T(8,128)S(1)} custom-call(s32[1]{0:T(128)} %bitcast.f_ref, f32[2]{0:T(128)S(1)} %copy-done.4, f32[2,1024,512]{2,1,0:T(8,128)} %g_ref.3), custom_call_target="tpu_custom_call" | custom-call | bytes 1048576 | tf_op jit(solution)/shard_map/send_part/pallas_call | solution.py:380
  3.5 2.1 %collective-permute-start.5 = (f32[536,512]{1,0:T(8,128)S(1)}, f32[536,512]{1,0:T(8,128)S(1)}, u32[]{:S(2)}, u32[]{:S(2)}) collective-permute-start(f32[536,512]{1,0:T(8,128)S(1)} %send_part.1), channel_id=1, source_target_pairs={{0,64},{64,0},{1,65},{65,1},{2,66},{66,2},{3,67},{67,3},{4,68},{68... | collective-permute-start | bytes 3293192 | tf_op jit(solution)/shard_map/ppermute | solution.py:387
  5.6 4.0 %strips.1 = (f32[1024,512]{1,0:T(8,128)S(1)}, f32[48,1024]{1,0:T(8,128)S(1)}, f32[48,1024]{1,0:T(8,128)S(1)}) custom-call(f32[2]{0:T(128)S(1)} %copy-done.4, f32[2,1024,512]{2,1,0:T(8,128)} %g_ref.3, f32[1024,512]{1,0:T(8,128)} %ls_ref.7), custom_call_target="tpu_custom_call" | custom-call | bytes 1048576 | tf_op jit(solution)/shard_map/strips/pallas_call | solution.py:389
  9.6 0.0 copy-start
  9.6 6.3 %collective-permute-start = (f32[48,1024]{1,0:T(8,128)S(1)}, f32[48,1024]{1,0:T(8,128)S(1)}, u32[]{:S(2)}, u32[]{:S(2)}) collective-permute-start(f32[48,1024]{1,0:T(8,128)S(1)} %get-tuple-element.20), channel_id=1, source_target_pairs={{0,15},{1,0},{2,1},{3,2},{4,3},{5,4},{6,5},{7,6},{8,7},{9,8},{10,9... | collective-permute-start | bytes 589832 | tf_op jit(solution)/shard_map/ppermute | solution.py:392
  15.9 0.0 collective-permute-start.1
  15.9 3.2 %collective-permute-done.right_ref = f32[48,1024]{1,0:T(8,128)S(1)} collective-permute-done((f32[48,1024]{1,0:T(8,128)S(1)}, f32[48,1024]{1,0:T(8,128)S(1)}, u32[]{:S(2)}, u32[]{:S(2)}) %collective-permute-start) | collective-permute-done | bytes 196640 | tf_op jit(solution)/shard_map/ppermute | solution.py:392
  19.1 5.2 %collective-permute-done.1.left_ref = f32[48,1024]{1,0:T(8,128)S(1)} collective-permute-done((f32[48,1024]{1,0:T(8,128)S(1)}, f32[48,1024]{1,0:T(8,128)S(1)}, u32[]{:S(2)}, u32[]{:S(2)}) %collective-permute-start.1) | collective-permute-done | bytes 196640 | tf_op jit(solution)/shard_map/ppermute | solution.py:393
  24.3 2.4 %row_messages.1 = (f32[1024,128]{1,0:T(8,128)S(1)}, f32[1024,128]{1,0:T(8,128)S(1)}, f32[48,640]{1,0:T(8,128)S(1)}, f32[48,640]{1,0:T(8,128)S(1)}, f32[24,640]{1,0:T(8,128)S(1)}) custom-call(s32[1]{0:T(128)} %bitcast.f_ref, f32[48,1024]{1,0:T(8,128)S(1)} %collective-permute-done.right_ref, f32[48,1024]{1,0:T(8,128)S(1)} %collective-permute-done.1.left_ref, ...), custom_call_target="tpu_custom_call" | custom-call | bytes 1048576 | tf_op jit(solution)/shard_map/row_messages/pallas_call | solution.py:395
  26.7 0.0 copy-done
  26.8 4.6 %collective-permute-start.2 = (f32[48,640]{1,0:T(8,128)S(1)}, f32[48,640]{1,0:T(8,128)S(1)}, u32[]{:S(2)}, u32[]{:S(2)}) collective-permute-start(f32[48,640]{1,0:T(8,128)S(1)} %get-tuple-element.24), channel_id=1, source_target_pairs={{0,16},{16,32},{32,48},{48,0},{64,112},{80,64},{96,80},{112,96},{1... | collective-permute-start | bytes 368648 | tf_op jit(solution)/shard_map/ppermute | solution.py:408
  31.3 0.0 collective-permute-start.4
  31.3 0.0 collective-permute-start.3
  31.3 4.3 %collective-permute-done.3.m2_ref = f32[24,640]{1,0:T(8,128)S(1)} collective-permute-done((f32[24,640]{1,0:T(8,128)S(1)}, f32[24,640]{1,0:T(8,128)S(1)}, u32[]{:S(2)}, u32[]{:S(2)}) %collective-permute-start.3) | collective-permute-done | bytes 61472 | tf_op jit(solution)/shard_map/ppermute | solution.py:409
  35.6 0.0 collective-permute-done.2.m1_ref
  35.6 0.1 collective-permute-done.4.fs_ref
  35.7 5.3 %half_setup.1 = (f32[5,560,128]{2,1,0:T(8,128)S(1)}, f32[5,560,128]{2,1,0:T(8,128)}, f32[70,8,640]{2,1,0:T(8,128)}, f32[70,8,640]{2,1,0:T(8,128)}) custom-call(s32[1]{0:T(128)} %bitcast.f_ref, f32[1024,512]{1,0:T(8,128)} %copy-done, f32[1024,512]{1,0:T(8,128)} %ls_ref.7, f32[1024,128]{1,0:T(8,128)S(1)} %get-tuple-element.22.pcol_ref, ...), custom_call_target="tpu_custom_call" | custom-call | bytes 1048576 | tf_op jit(solution)/shard_map/half_setup/pallas_call | solution.py:412
  41.0 0.0 copy-start.3
  41.0 1.1 copy-done.3
  42.1 0.0 collective-permute-done.5.rp_ref
  42.1 0.0 copy-start.2
  42.1 13.9 %half_velocity.1 = (f32[5,560,128]{2,1,0:T(8,128)}, f32[560,512]{1,0:T(8,128)S(1)}, f32[128,8,128]{2,1,0:T(8,128)S(1)}) custom-call(s32[1]{0:T(128)} %bitcast.f_ref, f32[5,560,128]{2,1,0:T(8,128)} %copy-done.3, f32[536,512]{1,0:T(8,128)S(1)} %collective-permute-done.5.rp_ref, f32[70,8,640]{2,1,0:T(8,128)} %get-tuple-element.28.q_ref, ...), custom_call_target="tpu_custom_call" | custom-call | bytes 1048576 | tf_op jit(solution)/shard_map/half_velocity/pallas_call | solution.py:420
  56.0 0.7 collective-permute-start.7
  56.7 37.9 %all_to_all.5.top_ref = f32[128,8,128]{2,1,0:T(8,128)S(1)} all-to-all(f32[128,8,128]{2,1,0:T(8,128)S(1)} %get-tuple-element.30), channel_id=1, replica_groups=mesh['focus'=2,'gx'=4,'gy'=16] {'focus','gx','gy'}, dimensions={0} | all-to-all | bytes 1048576 | tf_op jit(solution)/shard_map/all_to_all | solution.py:429
  94.6 0.0 copy-done.2
  94.6 0.0 copy-start.1
  94.6 1.4 copy-done.1
  95.9 22.7 %outer_part.1.mine_ref = f32[256,512]{1,0:T(8,128)S(1)} custom-call(s32[1]{0:T(128)} %bitcast.f_ref, f32[128,8,128]{2,1,0:T(8,128)S(1)} %all_to_all.5.top_ref, f32[5,560,128]{2,1,0:T(8,128)S(1)} %copy-done.2, f32[5,560,128]{2,1,0:T(8,128)S(1)} %copy-done.1), custom_call_target="tpu_custom_call" | custom-call | bytes 1048576 | tf_op jit(solution)/shard_map/outer_part/pallas_call | solution.py:433
  118.6 0.2 collective-permute-start.6
  118.9 0.0 collective-permute-done.7.got_ref
  118.9 22.3 %middle_part.1 = (f32[1024,512]{1,0:T(8,128)}, f32[1024,512]{1,0:T(8,128)}) custom-call(s32[1]{0:T(128)} %bitcast.f_ref, f32[128,8,128]{2,1,0:T(8,128)S(1)} %all_to_all.5.top_ref, f32[5,560,128]{2,1,0:T(8,128)} %get-tuple-element.32.vx_ref, f32[560,512]{1,0:T(8,128)S(1)} %get-tuple-element.33.msg_ref, f32[560,512]{1,0:T(8,128)S(1)} %collective-permute-done.7.got_ref, ...), custom_call_target="tpu_custom_call" | custom-call | bytes 1048576 | tf_op jit(solution)/shard_map/middle_part/pallas_call | solution.py:445
  141.2 0.0 collective-permute-done.6.got_ref
  141.2 0.8 insert.1
Async XLA Ops:
  0.6 0.7 copy-start.4
  3.5 38.6 %collective-permute-start.5 = (f32[536,512]{1,0:T(8,128)S(1)}, f32[536,512]{1,0:T(8,128)S(1)}, u32[]{:S(2)}, u32[]{:S(2)}) collective-permute-start(f32[536,512]{1,0:T(8,128)S(1)} %send_part.1), channel_id=1, source_target_pairs={{0,64},{64,0},{1,65},{65,1},{2,66},{66,2},{3,67},{67,3},{4,68},{68... | collective-permute-start | bytes 3293192 | tf_op jit(solution)/shard_map/ppermute | solution.py:387
  9.6 17.2 %copy-start = (f32[1024,512]{1,0:T(8,128)}, f32[1024,512]{1,0:T(8,128)S(1)}, u32[]{:S(2)}) copy-start(f32[1024,512]{1,0:T(8,128)S(1)} %get-tuple-element.19.p_ref) | copy-start | bytes 6291460
  9.6 9.5 %collective-permute-start = (f32[48,1024]{1,0:T(8,128)S(1)}, f32[48,1024]{1,0:T(8,128)S(1)}, u32[]{:S(2)}, u32[]{:S(2)}) collective-permute-start(f32[48,1024]{1,0:T(8,128)S(1)} %get-tuple-element.20), channel_id=1, source_target_pairs={{0,15},{1,0},{2,1},{3,2},{4,3},{5,4},{6,5},{7,6},{8,7},{9,8},{10,9... | collective-permute-start | bytes 589832 | tf_op jit(solution)/shard_map/ppermute | solution.py:392
  15.9 8.5 %collective-permute-start.1 = (f32[48,1024]{1,0:T(8,128)S(1)}, f32[48,1024]{1,0:T(8,128)S(1)}, u32[]{:S(2)}, u32[]{:S(2)}) collective-permute-start(f32[48,1024]{1,0:T(8,128)S(1)} %get-tuple-element.21), channel_id=1, source_target_pairs={{0,1},{1,2},{2,3},{3,4},{4,5},{5,6},{6,7},{7,8},{8,9},{9,10},{10,1... | collective-permute-start | bytes 589832 | tf_op jit(solution)/shard_map/ppermute | solution.py:393
  26.8 8.8 %collective-permute-start.2 = (f32[48,640]{1,0:T(8,128)S(1)}, f32[48,640]{1,0:T(8,128)S(1)}, u32[]{:S(2)}, u32[]{:S(2)}) collective-permute-start(f32[48,640]{1,0:T(8,128)S(1)} %get-tuple-element.24), channel_id=1, source_target_pairs={{0,16},{16,32},{32,48},{48,0},{64,112},{80,64},{96,80},{112,96},{1... | collective-permute-start | bytes 368648 | tf_op jit(solution)/shard_map/ppermute | solution.py:408
  31.3 4.4 %collective-permute-start.4 = (f32[48,640]{1,0:T(8,128)S(1)}, f32[48,640]{1,0:T(8,128)S(1)}, u32[]{:S(2)}, u32[]{:S(2)}) collective-permute-start(f32[48,640]{1,0:T(8,128)S(1)} %get-tuple-element.26), channel_id=1, source_target_pairs={{0,64},{64,0},{1,65},{65,1},{2,66},{66,2},{3,67},{67,3},{4,68},{68... | collective-permute-start | bytes 368648 | tf_op jit(solution)/shard_map/ppermute | solution.py:410
  31.3 4.3 %collective-permute-start.3 = (f32[24,640]{1,0:T(8,128)S(1)}, f32[24,640]{1,0:T(8,128)S(1)}, u32[]{:S(2)}, u32[]{:S(2)}) collective-permute-start(f32[24,640]{1,0:T(8,128)S(1)} %get-tuple-element.25), channel_id=1, source_target_pairs={{0,112},{16,64},{32,80},{48,96},{64,16},{80,32},{96,48},{112,0},{1... | collective-permute-start | bytes 184328 | tf_op jit(solution)/shard_map/ppermute | solution.py:409
  41.0 1.1 copy-start.3
  42.1 52.5 %copy-start.2 = (f32[5,560,128]{2,1,0:T(8,128)S(1)}, f32[5,560,128]{2,1,0:T(8,128)}, u32[]{:S(2)}) copy-start(f32[5,560,128]{2,1,0:T(8,128)} %get-tuple-element.31.lsx_ref) | copy-start | bytes 4300804
  56.0 62.9 %collective-permute-start.7 = (f32[560,512]{1,0:T(8,128)S(1)}, f32[560,512]{1,0:T(8,128)S(1)}, u32[]{:S(2)}, u32[]{:S(2)}) collective-permute-start(f32[560,512]{1,0:T(8,128)S(1)} %get-tuple-element.33.msg_ref), channel_id=1, source_target_pairs={{0,64},{64,0},{1,65},{65,1},{2,66},{66,2},{3,67},{67,3},{4,68},{68... | collective-permute-start | bytes 3440648 | tf_op jit(solution)/shard_map/ppermute | solution.py:428
  94.6 1.4 copy-start.1
  118.6 22.5 %collective-permute-start.6 = (f32[256,512]{1,0:T(8,128)S(1)}, f32[256,512]{1,0:T(8,128)S(1)}, u32[]{:S(2)}, u32[]{:S(2)}) collective-permute-start(f32[256,512]{1,0:T(8,128)S(1)} %outer_part.1.mine_ref), channel_id=1, source_target_pairs={{0,64},{64,0},{1,65},{65,1},{2,66},{66,2},{3,67},{67,3},{4,68},{68... | collective-permute-start | bytes 1572872 | tf_op jit(solution)/shard_map/ppermute | solution.py:442

commit v2 on v0

v2 whole, which is shorter than its diff:
```python
import jax
import jax.numpy as jnp
from jax import lax
from jax.experimental import pallas as pl
from jax.experimental.pallas import tpu as pltpu
from jax.sharding import PartitionSpec as P

EXT_SWEEPS = 8
REINIT_ITERS = 10
band_cells = 3.0
cfl_number = 0.5
pseudo_step = 0.5

HALO = 24
EDGE = 12
STAGED = 16
OWN_PARTS = (3, 16)
LANES = 128
TINY = 1e-18

VMEM = pl.BlockSpec(memory_space=pltpu.VMEM)
SMEM = pl.BlockSpec(memory_space=pltpu.SMEM)
ANY = pl.BlockSpec(memory_space=pl.ANY)
DMA = pltpu.SemaphoreType.DMA


def vmem(*shape):
    return pltpu.VMEM(shape, jnp.float32)


def call(body, out_shapes, in_specs, scratch=(), name=None, flops=0, out_specs=None, aliases=None, mib=24):
    outs = [jax.ShapeDtypeStruct(s, jnp.float32) for s in out_shapes]
    return pl.pallas_call(
        body,
        out_shape=outs,
        in_specs=in_specs,
        out_specs=out_specs or [VMEM] * len(outs),
        scratch_shapes=list(scratch),
        name=name,
        input_output_aliases=aliases or {},
        compiler_params=pltpu.CompilerParams(vmem_limit_bytes=mib << 20),
        cost_estimate=pl.CostEstimate(flops=flops, bytes_accessed=1 << 20, transcendentals=0),
    )


def aligned(x, n=8):
    return pl.multiple_of(x, n)


def lanes_of(c):
    return slice(c * LANES, (c + 1) * LANES)


def partner_rows(f, rows, main):
    return aligned((1 - f) * (rows - main))


def send_part(main, f_ref, w_ref, g_ref, send_ref, buf, sems):
    n = send_ref.shape[0]
    start = partner_rows(f_ref[0], g_ref.shape[1], main)
    chunks = sems.shape[0]
    step = n // 8 // chunks * 8
    spans = [(i * step, step if i < chunks - 1 else n - i * step) for i in range(chunks)]
    copies = [
        pltpu.make_async_copy(
            g_ref.at[:, pl.ds(aligned(start + at), n), :], buf.at[:, pl.ds(at, n), :], sems.at[i]
        )
        for i, (at, n) in enumerate(spans)
    ]
    for copy in copies:
        copy.start()
    for copy, (at, n) in zip(copies, spans):
        copy.wait()
        send_ref[at : at + n, :] = w_ref[0] * buf[0, at : at + n, :] + w_ref[1] * buf[1, at : at + n, :]


def strips(w_ref, g_ref, ls_ref, p_ref, left_ref, right_ref, buf, sems):
    rows, cols = ls_ref.shape
    n = rows // sems.shape[0]
    copies = [
        pltpu.make_async_copy(g_ref.at[:, pl.ds(i * n, n), :], buf.at[:, pl.ds(i * n, n), :], sems.at[i])
        for i in range(sems.shape[0])
    ]
    for copy in copies:
        copy.start()
    lane = lax.broadcasted_iota(jnp.int32, (LANES, LANES), 1)
    for i in range(rows // LANES):
        at = lanes_of(i)
        if i * LANES % n == 0:
            copies[i * LANES // n].wait()
        p_ref[at, :] = w_ref[0] * buf[0, at, :] + w_ref[1] * buf[1, at, :]
        first, last = slice(0, LANES), slice(cols - LANES, cols)
        packed = p_ref[at, first]
        for j, (ref, of) in enumerate(((ls_ref, first), (p_ref, last), (ls_ref, last)), 1):
            held = 0 if of.start == 0 else LANES - HALO
            moved = pltpu.roll(ref[at, of], (j * HALO - held) % LANES, 1)
            packed = jnp.where(lane < j * HALO, packed, moved)
        turned_ = packed.T
        left_ref[:, at] = turned_[0 : 2 * HALO, :]
        right_ref[:, at] = turned_[2 * HALO : 4 * HALO, :]


def turned(right, left):
    gap = jnp.zeros((LANES - 2 * HALO, right.shape[1]), jnp.float32)
    return jnp.concatenate([right, gap, left], axis=0).T


def row_messages(main, f_ref, right_ref, left_ref, p_ref, ls_ref, fs_ref, m1_ref, m2_ref, rest_ref):
    rows, cols = ls_ref.shape
    f = f_ref[0]
    width = fs_ref.shape[1]
    theirs = pl.ds(aligned((1 - f) * (rows - width), LANES), width)
    fs_ref[0:HALO, :] = right_ref[0:HALO, theirs]
    fs_ref[HALO:, :] = left_ref[0:HALO, theirs]

    def corner(of, bottom):
        at = pl.ds(aligned(bottom * (rows - LANES), LANES), LANES)
        return turned(right_ref[of, at], left_ref[of, at])

    def ends(block, bottom):
        return jnp.where(bottom == 1, block[LANES - HALO :, :], block[0:HALO, :])

    outer, inner = 1 - f, f
    p_part, ls_part = slice(0, HALO), slice(HALO, 2 * HALO)
    at_outer = pl.ds(aligned(outer * (rows - HALO)), HALO)
    at_inner = pl.ds(aligned(inner * (rows - HALO)), HALO)
    m1_ref[p_part, 0:cols] = p_ref[at_outer, :]
    m1_ref[p_part, cols:] = ends(corner(p_part, outer), outer)
    m1_ref[ls_part, 0:cols] = ls_ref[at_outer, :]
    m1_ref[ls_part, cols:] = ends(corner(ls_part, outer), outer)
    m2_ref[:, 0:cols] = p_ref[at_inner, :]
    m2_ref[:, cols:] = ends(corner(p_part, inner), inner)
    n = rest_ref.shape[0]
    rest_ref[...] = p_ref[pl.ds(aligned(partner_rows(f, rows, main) + main - n), n), :]


def spread(nat, r, lo, width):
    return jnp.concatenate(
        [nat[c, pl.ds(lo, 8, stride=r), :] for c in range(width // LANES)], axis=1
    )


def unspread(nat, r, lo, value):
    for c in range(value.shape[1] // LANES):
        nat[c, pl.ds(lo, 8, stride=r), :] = value[:, lanes_of(c)]


def put(nat, rows, value, first=0):
    for c in range(value.shape[1] // LANES):
        nat[first + c, rows, :] = value[:, lanes_of(c)]


def half_setup(
    f_ref, p_ref, ls_ref, right_ref, left_ref, m1_ref, m2_ref, fs_ref,
    t_ref, lsx_ref, q_ref, rec_ref, nat, pcol, lscol,
):
    rows, cols = ls_ref.shape
    f = f_ref[0]
    ext = lsx_ref.shape[1]
    main = ext - HALO
    first = aligned((1 - f) * HALO)
    beside = pl.ds(aligned(f * main), HALO)
    put(nat, beside, m1_ref[0:HALO, :] + m2_ref[...])
    put(lsx_ref, beside, m1_ref[HALO:, :])
    width = fs_ref.shape[1]
    skip = f * (width - main)
    lane0 = f * (rows - width)
    for i in range(width // LANES):
        at = pl.ds(aligned(lane0 + i * LANES, LANES), LANES)
        to = lanes_of(i)
        pcol[to, :] = turned(
            right_ref[0:HALO, at] + fs_ref[0:HALO, to], left_ref[0:HALO, at] + fs_ref[HALO:, to]
        )
        lscol[to, :] = turned(right_ref[HALO:, at], left_ref[HALO:, at])
    start = f * (rows - main)
    last = cols // LANES
    for i in range(main // 8):
        to = pl.ds(aligned(first + i * 8), 8)
        of = pl.ds(aligned(start + i * 8), 8)
        side = pl.ds(aligned(skip + i * 8), 8)
        put(nat, to, p_ref[of, :])
        put(lsx_ref, to, ls_ref[of, :])
        nat[last, to, :] = pcol[side, :]
        lsx_ref[last, to, :] = lscol[side, :]

    r = ext // 8
    for k in range(r):
        x = spread(lsx_ref, r, k, cols + LANES) * (1.0 / band_cells)
        u = x * x
        q = 1.0 / (5.0 + 4.0 * u)
        q_ref[k] = q
        rec_ref[k] = (1.0 + u) * q
        t_ref[k] = spread(nat, r, k, cols + LANES)


def wrap(ref, r):
    ref[0] = pltpu.roll(ref[r], 1, 0)
    ref[r + 1] = pltpu.roll(ref[1], 7, 0)


def sweep(src, r, body):
    up, centre = src[0], src[1]
    for k in range(r):
        down = src[k + 2]
        body(k, up, centre, down)
        up, centre = centre, down


def half_velocity(f_ref, t_ref, rp1_ref, rp2_ref, q_ref, rec_ref, vs_ref, top_ref, nat, a_ref, v0, v1):
    cols = rp1_ref.shape[1]
    r, _, width = t_ref.shape
    ext = 8 * r
    f = f_ref[0]
    at = aligned((1 - f) * HALO)
    main = ext - HALO
    for c in range(cols // LANES):
        nat[c, pl.ds(aligned(f * main), HALO), :] = jnp.zeros((HALO, LANES), jnp.float32)
    n1, n2 = rp1_ref.shape[0], rp2_ref.shape[0]
    put(nat, pl.ds(at, n1), rp1_ref[...])
    put(nat, pl.ds(aligned(at + n1), n2), rp2_ref[...])
    for k in range(r):
        t = t_ref[k]
        source = jnp.concatenate([t[:, 0:cols] + spread(nat, r, k, cols), t[:, cols:]], axis=1)
        v0[k + 1] = source
        a_ref[k] = source * q_ref[k]
    wrap(v0, r)

    def relax(k, up, centre, down):
        beside = (up + down) + (pltpu.roll(centre, 1, 1) + pltpu.roll(centre, width - 1, 1))
        return a_ref[k] + rec_ref[k] * beside

    def one(src, dst):
        def body(k, *cells):
            dst[k + 1] = relax(k, *cells)

        sweep(src, r, body)
        wrap(dst, r)

    def pair(i, _):
        one(v0, v1)
        one(v1, v0)
        return 0

    assert EXT_SWEEPS % 2 == 0
    lax.fori_loop(0, EXT_SWEEPS // 2 - 1, pair, 0)
    one(v0, v1)
    sub = lax.broadcasted_iota(jnp.int32, (8, cols), 0)
    tops = [jnp.zeros((8, cols), jnp.float32)] * 2

    def final(k, *cells):
        value = relax(k, *cells)
        vs_ref[k] = value
        size = jnp.abs(value[:, 0:cols])
        row = sub * r + k
        if k < HALO or 7 * r + k >= ext - HALO:
            size = jnp.where((row >= HALO) & (row < ext - HALO), size, 0.0)
        tops[k % 2] = jnp.maximum(tops[k % 2], size)

    sweep(v1, r, final)
    top_ref[...] = jnp.full(top_ref.shape, jnp.max(jnp.maximum(*tops)), jnp.float32)


def velocity_messages(f_ref, vs_ref, vx_ref, near_ref, far_ref):
    slabs, ext, _ = vx_ref.shape
    r = ext // 8
    for k in range(r):
        unspread(vx_ref, r, k, vs_ref[k])
    far = far_ref.shape[0]
    near = near_ref.shape[0] - 2 * HALO
    half = far + near
    f = f_ref[0]
    at_near = pl.ds(aligned(HALO + (1 - f) * far), near)
    at_far = pl.ds(aligned(HALO + f * near), far)
    for c in range(slabs - 1):
        near_ref[0:near, lanes_of(c)] = vx_ref[c, at_near, :]
        far_ref[:, lanes_of(c)] = vx_ref[c, at_far, :]
    for i in range(half // LANES):
        side = vx_ref[slabs - 1, HALO + i * LANES : HALO + (i + 1) * LANES, :].T
        near_ref[near : near + HALO, lanes_of(i)] = side[0:HALO, :]
        near_ref[near + HALO :, lanes_of(i)] = side[LANES - HALO :, :]


def speeds(sigma, centre, up, down, left, right):
    a = jnp.maximum(sigma * (centre - up), TINY)
    b = jnp.maximum(sigma * (centre - down), 0.0)
    c = jnp.maximum(sigma * (centre - left), 0.0)
    d = jnp.maximum(sigma * (centre - right), 0.0)
    return (a * a + b * b) + (c * c + d * d)


def reinit(top_ref, ls_nat, v_nat, base, r, out_nat, shift, p0, p1, h_ref, s_ref, width):
    step = cfl_number / (jnp.max(top_ref[...]) + 1e-06)
    for k in range(r):
        p0[k + 1] = spread(ls_nat, r, base + k, width)
    wrap(p0, r)

    def beside(centre):
        return pltpu.roll(centre, 1, 1), pltpu.roll(centre, width - 1, 1)

    def advance(k, up, centre, down):
        speed = spread(v_nat, r, base + k, width)
        sigma = jnp.where(speed >= 0.0, 1.0, -1.0)
        total = speeds(sigma, centre, up, down, *beside(centre))
        advanced = centre - step * (speed * (total * lax.rsqrt(total)))
        p1[k + 1] = advanced
        h_ref[k] = pseudo_step * (advanced * lax.rsqrt(advanced * advanced + 1.0))
        s_ref[k] = jnp.where(advanced >= 0.0, 1.0, -1.0)

    sweep(p0, r, advance)
    wrap(p1, r)

    def one(src, dst):
        def body(k, up, centre, down):
            total = speeds(s_ref[k], centre, up, down, *beside(centre))
            h = h_ref[k]
            dst[k + 1] = (centre + h) - h * (total * lax.rsqrt(total))

        sweep(src, r, body)
        wrap(dst, r)

    def pair(i, _):
        one(p1, p0)
        one(p0, p1)
        return 0

    assert REINIT_ITERS % 2 == 0
    lax.fori_loop(0, REINIT_ITERS // 2 - 1, pair, 0)
    one(p1, p0)
    cols = width - LANES

    def final(k, up, centre, down):
        left, right = beside(centre)
        c = centre[:, 0:cols]
        total = speeds(s_ref[k][:, 0:cols], c, up[:, 0:cols], down[:, 0:cols], left[:, 0:cols], right[:, 0:cols])
        h = h_ref[k][:, 0:cols]
        unspread(out_nat, r, k + shift, (c + h) - h * (total * lax.rsqrt(total)))

    sweep(p0, r, final)


def outer_part(f_ref, top_ref, lsx_ref, vx_ref, out_ref, nat, p0, p1, h_ref, s_ref):
    n, cols = out_ref.shape
    r = (n + 2 * EDGE) // 8
    base = HALO - EDGE + f_ref[0] * (lsx_ref.shape[1] - 2 * HALO - n)
    reinit(top_ref, lsx_ref, vx_ref, base, r, nat, STAGED - EDGE, p0, p1, h_ref, s_ref, cols + LANES)
    for c in range(cols // LANES):
        out_ref[:, lanes_of(c)] = nat[c, STAGED : STAGED + n, :]


def middle_part(
    f_ref, top_ref, vx_ref, near_ref, ls_ref, right_ref, left_ref, mine_ref, level_ref, vel_ref,
    nat, lsn, vn, p0, p1, h_ref, s_ref, sems,
):
    rows, cols = ls_ref.shape
    f = f_ref[0]
    staged = lsn.shape[1]
    n = staged - 2 * STAGED
    r = (n + 2 * EDGE) // 8
    low = (rows - staged) // 2
    last = cols // LANES
    half = rows // 2
    near = near_ref.shape[0] - 2 * HALO
    own = mine_ref.shape[0]
    ready = [
        pltpu.make_async_copy(
            vx_ref.at[c, pl.ds(HALO, half), :],
            vel_ref.at[pl.ds(aligned(f * half), half), pl.ds(c * LANES, LANES)],
            sems.at[c],
        )
        for c in range(last)
    ]
    ready.append(
        pltpu.make_async_copy(
            near_ref.at[pl.ds(0, near), :],
            vel_ref.at[pl.ds(aligned((1 - f) * half + f * (half - near)), near), :],
            sems.at[last],
        )
    )
    ready.append(
        pltpu.make_async_copy(
            mine_ref, level_ref.at[pl.ds(aligned(f * (rows - own)), own), :], sems.at[last + 1]
        )
    )
    for copy in ready:
        copy.start()
    for c in range(last):
        lsn[c] = ls_ref[low : low + staged, lanes_of(c)]
    cut = half - low
    for i in range(rows // LANES):
        at = i * LANES
        begin, end = max(at, low), min(at + LANES, low + staged)
        if begin < end:
            block = turned(right_ref[HALO:, at : at + LANES], left_ref[HALO:, at : at + LANES])
            lsn[last, begin - low : end - low, :] = block[begin - at : end - at, :]
        if at < half:
            block = turned(near_ref[near : near + HALO, at : at + LANES], near_ref[near + HALO :, at : at + LANES])

            @pl.when(f == 0)
            def _():
                end = min(at + LANES, staged - cut)
                if at < end:
                    vn[last, cut + at : cut + end, :] = block[0 : end - at, :]

            @pl.when(f == 1)
            def _():
                begin = max(at, low)
                if begin < at + LANES:
                    vn[last, begin - low : at + LANES - low, :] = block[begin - at :, :]

    @pl.when(f == 0)
    def _():
        vn[:, 0:cut, :] = vx_ref[:, HALO + low : HALO + half, :]
        put(vn, slice(cut, staged), near_ref[0 : staged - cut, :])

    @pl.when(f == 1)
    def _():
        put(vn, slice(0, cut), near_ref[near - cut : near, :])
        vn[:, cut:, :] = vx_ref[:, HALO : HALO + staged - cut, :]

    reinit(top_ref, lsn, vn, STAGED - EDGE, r, nat, STAGED - EDGE, p0, p1, h_ref, s_ref, cols + LANES)
    results = [
        pltpu.make_async_copy(
            nat.at[c, pl.ds(STAGED, n), :],
            level_ref.at[pl.ds(low + STAGED, n), pl.ds(c * LANES, LANES)],
            sems.at[last + 2 + c],
        )
        for c in range(last)
    ]
    for copy in results:
        copy.start()
    for copy in ready + results:
        copy.wait()


def insert(f_ref, theirs_ref, far_ref, _, __, level_ref, vel_ref, sems):
    rows = level_ref.shape[0]
    n, far = theirs_ref.shape[0], far_ref.shape[0]
    f = f_ref[0]
    copies = [
        pltpu.make_async_copy(
            theirs_ref, level_ref.at[pl.ds(aligned((1 - f) * (rows - n)), n), :], sems.at[0]
        ),
        pltpu.make_async_copy(
            far_ref, vel_ref.at[pl.ds(aligned((1 - f) * (rows - far)), far), :], sems.at[1]
        ),
    ]
    for copy in copies:
        copy.start()
    for copy in copies:
        copy.wait()


def shifted(n, by):
    return [(i, (i + by) % n) for i in range(n)]


def per_device(level_set, focus_grads, focus_weight):
    rows, cols = level_set.shape
    half = rows // 2
    gx, gy = lax.axis_size("gx"), lax.axis_size("gy")
    f = lax.axis_index("focus").reshape(1).astype(jnp.int32)
    planes = focus_grads.shape[0]
    assert planes == 2 and lax.axis_size("focus") == 2
    swap = [(0, 1), (1, 0)]
    main, ext, wide = half + HALO, half + 2 * HALO, cols + LANES
    slabs = wide // LANES
    part = main * 3 // 4 // 16 * 16

    (to_partner,) = call(
        lambda *refs: send_part(main, *refs),
        [(part, cols)],
        [SMEM, SMEM, ANY],
        [vmem(planes, part, cols), DMA((4,))],
        "send_part",
    )(f, focus_weight, focus_grads)
    from_partner = lax.ppermute(to_partner, "focus", swap)

    p, left, right = call(
        strips,
        [(rows, cols), (2 * HALO, rows), (2 * HALO, rows)],
        [SMEM, ANY, VMEM],
        [vmem(planes, rows, cols), DMA((4,))],
        "strips",
    )(focus_weight, focus_grads, level_set)
    from_right = lax.ppermute(left, "gy", shifted(gy, -1))
    from_left = lax.ppermute(right, "gy", shifted(gy, 1))
    side = -(-main // LANES) * LANES
    fs, m1, m2, to_partner2 = call(
        lambda *refs: row_messages(main, *refs),
        [(2 * HALO, side), (2 * HALO, wide), (HALO, wide), (main - part, cols)],
        [SMEM, VMEM, VMEM, VMEM, VMEM],
        (),
        "row_messages",
    )(f, from_right, from_left, p, level_set)

    def place(f, x):
        return f * gx + x % gx

    same = [(place(0, x), place(0, x + 1)) for x in range(gx)] + [(place(1, x), place(1, x - 1)) for x in range(gx)]
    cross = [(place(0, x), place(1, x - 1)) for x in range(gx)] + [(place(1, x), place(0, x + 1)) for x in range(gx)]
    got1 = lax.ppermute(m1, ("focus", "gx"), same)
    got2 = lax.ppermute(m2, ("focus", "gx"), cross)
    got_fs = lax.ppermute(fs, "focus", swap)
    from_partner2 = lax.ppermute(to_partner2, "focus", swap)
    r = ext // 8
    t, lsx, q, rec = call(
        half_setup,
        [(r, 8, wide), (slabs, ext, LANES), (r, 8, wide), (r, 8, wide)],
        [SMEM] + [VMEM] * 7,
        [vmem(slabs, ext, LANES), vmem(side, LANES), vmem(side, LANES)],
        "half_setup",
    )(f, p, level_set, from_right, from_left, got1, got2, got_fs)
    devices = 2 * gx * gy
    vs, top = call(
        half_velocity,
        [(r, 8, wide), (devices, LANES)],
        [SMEM] + [VMEM] * 5,
        [vmem(slabs - 1, ext, LANES), vmem(r, 8, wide), vmem(r + 2, 8, wide), vmem(r + 2, 8, wide)],
        "half_velocity",
    )(f, t, from_partner, from_partner2, q, rec)
    tops = lax.all_to_all(top, ("focus", "gx", "gy"), 0, 0)

    own = rows * OWN_PARTS[0] // OWN_PARTS[1]
    near = half - own + STAGED
    vx, to_near, to_far = call(
        velocity_messages,
        [(slabs, ext, LANES), (near + 2 * HALO, cols), (half - near, cols)],
        [SMEM, VMEM],
        (),
        "velocity_messages",
    )(f, vs)
    got_near = lax.ppermute(to_near, "focus", swap)
    got_far = lax.ppermute(to_far, "focus", swap)

    def work(n):
        r = (n + 2 * EDGE) // 8
        return [vmem(r + 2, 8, wide)] * 2 + [vmem(r, 8, wide)] * 2

    (mine,) = call(
        outer_part,
        [(own, cols)],
        [SMEM] + [VMEM] * 3,
        [vmem(slabs - 1, own + 2 * STAGED, LANES)] + work(own),
        "outer_part",
    )(f, tops, lsx, vx)
    theirs = lax.ppermute(mine, "focus", swap)
    mid = rows - 2 * own
    staged = mid + 2 * STAGED
    level, velocity = call(
        middle_part,
        [(rows, cols), (rows, cols)],
        [SMEM] + [VMEM] * 7,
        [vmem(slabs - 1, staged, LANES), vmem(slabs, staged, LANES), vmem(slabs, staged, LANES)]
        + work(mid)
        + [DMA((2 * slabs,))],
        "middle_part",
        out_specs=[ANY, ANY],
        mib=32,
    )(f, tops, vx, got_near, level_set, from_right, from_left, mine)
    level, velocity = call(
        insert,
        [(rows, cols), (rows, cols)],
        [SMEM, VMEM, VMEM, ANY, ANY],
        [DMA((2,))],
        "insert",
        out_specs=[ANY, ANY],
        aliases={3: 0, 4: 1},
    )(f, theirs, got_far, level, velocity)
    return level, velocity


def solution(mesh):
    in_specs = (P("gx", "gy"), P("focus", "gx", "gy"), P("focus"))
    out_specs = (P("gx", "gy"), P("gx", "gy"))
    return jax.shard_map(
        per_device, mesh=mesh, in_specs=in_specs, out_specs=out_specs, check_vma=False
    )
```

time: 845 us -> 99.2 us (0.12); the launches traced: 831 us -> 99.1 us
  local copies, waits for them, and re-layouts: 206 us -> 2.84 us
  starting transfers between devices: 189 us -> 15.6 us
  other arithmetic: 156 us -> 0 us
  waiting for transfers between devices: 131 us -> 16.1 us
  blocking collectives: 132 us -> 26.8 us
  Pallas kernels: 0 us -> 36.7 us
  between operations: 16.2 us -> 0.91 us
    ppermute x76 -> x10, starting transfers between devices: 189 us -> 15.6 us  [the longest x1 6.28 us: per_device(): from_right = lax.ppermute(left, 'gy', shifted(gy, -1))]
    concatenate x19 -> x0, local copies, waits for them, and re-layouts: 145 us -> none  [padded_2(): jnp.concatenate([lax.ppermute(tail, axis, [(i, (i + 1) % count) for i in...]
    pmax x1 -> x0, blocking collectives: 132 us -> none  [per_device(): top = lax.pmax(jnp.max(jnp.abs(velocity)), ('gx', 'gy'))]
    sub x11 -> x0, other arithmetic: 95.2 us -> none  [the longest x10 84.9 us: per_device(): level_out - pseudo_step * (hamiltonian(padded_2(level_out, (('gx', 0), ('...]
    psum x1 -> x0, waiting for transfers between devices: 72.8 us -> none  [per_device(): source = lax.psum(local_sum, 'focus')]
    div x7 -> x0, other arithmetic: 47.5 us -> none  [jacobi(): return (band * source + beside) / (band + 4.0)]
    ppermute x76 -> x10, waiting for transfers between devices: 58.2 us -> 16.1 us  [the longest x1 7.66 us: per_device(): got2 = lax.ppermute(m2, ('focus', 'gx'), cross)]
    pallas_call x0 -> x9, Pallas kernels: none -> 36.7 us  [the longest x1 18.3 us: per_device(): call(middle_part, [(rows, cols), (rows, cols)], [SMEM] + [VMEM] * 7, [vme...]
  transfers between devices with their start and end apart: 77 -> 10, of which waited for: 44 -> 3; matrix products, arithmetic and copies ran while one was open for 3% -> 0% of each run, Pallas kernels for 0% -> 28%
where the time goes in v2:
time: 99.2 us; the launch traced here: 99.1 us
  Pallas kernels  36.7 us (37%)
  blocking collectives  26.8 us (27%)
  waiting for transfers between devices  16.1 us (16%)
  starting transfers between devices  15.6 us (16%)
  local copies, waits for them, and re-layouts  2.84 us (3%)
    all_to_all x1, blocking collectives, per_device(): tops = lax.all_to_all(top, ('focus', 'gx', 'gy'), 0, 0)  26.8 us
    pallas_call x1, Pallas kernels, per_device(): call(middle_part, [(rows, cols), (rows, cols)], [SMEM] + [VMEM] * 7, [vme...  18.3 us
    ppermute x1, waiting for transfers between devices, per_device(): got2 = lax.ppermute(m2, ('focus', 'gx'), cross)  7.66 us
    pallas_call x1, Pallas kernels, per_device(): call(half_velocity, [(r, 8, wide), (devices, LANES)], [SMEM] + [VMEM] * 5...  7.07 us
    ppermute x1, starting transfers between devices, per_device(): from_right = lax.ppermute(left, 'gy', shifted(gy, -1))  6.28 us
    pallas_call x1, Pallas kernels, per_device(): call(outer_part, [(own, cols)], [SMEM] + [VMEM] * 3, [vmem(slabs - 1, own...  5.63 us
    ppermute x1, waiting for transfers between devices, per_device(): from_left = lax.ppermute(right, 'gy', shifted(gy, 1))  5.23 us
    ppermute x1, starting transfers between devices, per_device(): got1 = lax.ppermute(m1, ('focus', 'gx'), same)  4.87 us
  transfers between devices with their start and end apart: 10, of which 3 were waited for; matrix products, arithmetic and copies ran while one was open for 0% of the time, Pallas kernels for 28%

profile of v2, /device:TPU:1, one launch (start us, length us, event | category | flops | bytes accessed | tf_op | source)
XLA Modules:
  0.0 99.1 jit_solution(1120714596485965341)
XLA Ops:
  0.6 0.0 copy-start.1
  0.6 2.2 %copy-done.1 = f32[2,1024,512]{2,1,0:T(8,128)S(1)} copy-done((f32[2,1024,512]{2,1,0:T(8,128)S(1)}, f32[2,1024,512]{2,1,0:T(8,128)}, u32[]{:S(2)}) %copy-start.1) | copy-done | bytes 4194328
  2.8 0.0 copy-start.2
  2.8 0.7 copy-done.2
  3.5 0.0 copy-start
  3.5 1.1 %send_part.1 = f32[400,512]{1,0:T(8,128)S(1)} custom-call(s32[1]{0:T(128)} %bitcast.refs_0_.f_ref, f32[2]{0:T(128)S(1)} %copy-done.2, f32[2,1024,512]{2,1,0:T(8,128)S(1)} %copy-done.1), custom_call_target="tpu_custom_call" | custom-call | bytes 1048576 | tf_op jit(solution)/shard_map/send_part/pallas_call | solution.py:469
  4.6 2.1 %collective-permute-start.5 = (f32[400,512]{1,0:T(8,128)S(1)}, f32[400,512]{1,0:T(8,128)S(1)}, u32[]{:S(2)}, u32[]{:S(2)}) collective-permute-start(f32[400,512]{1,0:T(8,128)S(1)} %send_part.1), channel_id=1, source_target_pairs={{0,64},{64,0},{1,65},{65,1},{2,66},{66,2},{3,67},{67,3},{4,68},{68... | collective-permute-start | bytes 2457608 | tf_op jit(solution)/shard_map/ppermute | solution.py:476
  6.8 0.0 copy-done
  6.8 2.1 %strips.1 = (f32[1024,512]{1,0:T(8,128)S(1)}, f32[48,1024]{1,0:T(8,128)S(1)}, f32[48,1024]{1,0:T(8,128)S(1)}) custom-call(f32[2]{0:T(128)S(1)} %copy-done.2, f32[2,1024,512]{2,1,0:T(8,128)S(1)} %copy-done.1, f32[1024,512]{1,0:T(8,128)S(1)} %copy-done), custom_call_target="tpu_custom_call" | custom-call | bytes 1048576 | tf_op jit(solution)/shard_map/strips/pallas_call | solution.py:478
  8.8 6.3 %collective-permute-start = (f32[48,1024]{1,0:T(8,128)S(1)}, f32[48,1024]{1,0:T(8,128)S(1)}, u32[]{:S(2)}, u32[]{:S(2)}) collective-permute-start(f32[48,1024]{1,0:T(8,128)S(1)} %get-tuple-element.21), channel_id=1, source_target_pairs={{0,15},{1,0},{2,1},{3,2},{4,3},{5,4},{6,5},{7,6},{8,7},{9,8},{10,9... | collective-permute-start | bytes 589832 | tf_op jit(solution)/shard_map/ppermute | solution.py:485
  15.1 0.0 collective-permute-start.1
  15.1 3.2 %collective-permute-done.refs_1_.right_ref = f32[48,1024]{1,0:T(8,128)S(1)} collective-permute-done((f32[48,1024]{1,0:T(8,128)S(1)}, f32[48,1024]{1,0:T(8,128)S(1)}, u32[]{:S(2)}, u32[]{:S(2)}) %collective-permute-start) | collective-permute-done | bytes 196640 | tf_op jit(solution)/shard_map/ppermute | solution.py:485
  18.4 5.2 %collective-permute-done.1.refs_2_.left_ref = f32[48,1024]{1,0:T(8,128)S(1)} collective-permute-done((f32[48,1024]{1,0:T(8,128)S(1)}, f32[48,1024]{1,0:T(8,128)S(1)}, u32[]{:S(2)}, u32[]{:S(2)}) %collective-permute-start.1) | collective-permute-done | bytes 196640 | tf_op jit(solution)/shard_map/ppermute | solution.py:486
  23.6 0.1 row_messages.1
  23.7 0.5 collective-permute-start.6
  24.3 4.9 %collective-permute-start.2 = (f32[48,640]{1,0:T(8,128)S(1)}, f32[48,640]{1,0:T(8,128)S(1)}, u32[]{:S(2)}, u32[]{:S(2)}) collective-permute-start(f32[48,640]{1,0:T(8,128)S(1)} %get-tuple-element.23), channel_id=1, source_target_pairs={{0,16},{16,32},{32,48},{48,0},{64,112},{80,64},{96,80},{112,96},{1... | collective-permute-start | bytes 368648 | tf_op jit(solution)/shard_map/ppermute | solution.py:501
  29.1 0.0 collective-permute-start.4
  29.1 0.0 collective-permute-start.3
  29.2 7.7 %collective-permute-done.3.m2_ref = f32[24,640]{1,0:T(8,128)S(1)} collective-permute-done((f32[24,640]{1,0:T(8,128)S(1)}, f32[24,640]{1,0:T(8,128)S(1)}, u32[]{:S(2)}, u32[]{:S(2)}) %collective-permute-start.3) | collective-permute-done | bytes 61472 | tf_op jit(solution)/shard_map/ppermute | solution.py:502
  36.8 0.0 collective-permute-done.2.m1_ref
  36.8 0.0 collective-permute-done.4.fs_ref
  36.8 1.1 %half_setup.1 = (f32[70,8,640]{2,1,0:T(8,128)S(1)}, f32[5,560,128]{2,1,0:T(8,128)S(1)}, f32[70,8,640]{2,1,0:T(8,128)S(1)}, f32[70,8,640]{2,1,0:T(8,128)S(1)}) custom-call(s32[1]{0:T(128)} %bitcast.refs_0_.f_ref, f32[1024,512]{1,0:T(8,128)S(1)} %get-tuple-element.20.refs_3_.p_ref, f32[1024,512]{1,0:T(8,128)S(1)} %copy-done, ...), custom_call_target="tpu_custom_call" | custom-call | bytes 1048576 | tf_op jit(solution)/shard_map/half_setup/pallas_call | solution.py:506
  37.9 0.0 collective-permute-done.6.rp2_ref
  37.9 0.0 collective-permute-done.5.rp1_ref
  37.9 7.1 %half_velocity.1 = (f32[70,8,640]{2,1,0:T(8,128)S(1)}, f32[128,128]{1,0:T(8,128)S(1)}) custom-call(s32[1]{0:T(128)} %bitcast.refs_0_.f_ref, f32[70,8,640]{2,1,0:T(8,128)S(1)} %get-tuple-element.26.t_ref, f32[400,512]{1,0:T(8,128)S(1)} %collective-permute-done.5.rp1_ref, f32[136,512]{1,0:T(8,128)S(1)} %collective-permute-done.6.rp2_ref, ...), custom_call_target="tpu_custom_call" | custom-call | bytes 1048576 | tf_op jit(solution)/shard_map/half_velocity/pallas_call | solution.py:514
  45.0 0.3 velocity_messages.1
  45.4 0.1 collective-permute-start.9
  45.4 26.8 %all_to_all.11 = f32[128,1,128]{2,1,0:T(1,128)S(1)} all-to-all(f32[128,1,128]{2,1,0:T(1,128)S(1)} %bitcast.7), channel_id=1, replica_groups=mesh['focus'=2,'gx'=4,'gy'=16] {'focus','gx','gy'}, dimensions={0} | all-to-all | bytes 131072 | tf_op jit(solution)/shard_map/all_to_all | solution.py:521
  72.3 5.6 %outer_part.1.mine_ref = f32[192,512]{1,0:T(8,128)S(1)} custom-call(s32[1]{0:T(128)} %bitcast.refs_0_.f_ref, f32[128,128]{1,0:T(8,128)S(1)} %bitcast.5, f32[5,560,128]{2,1,0:T(8,128)S(1)} %get-tuple-element.31.lsx_ref, f32[5,560,128]{2,1,0:T(8,128)S(1)} %get-tuple-element.33.vx_ref), custom_call_target="tpu_custom_call" | custom-call | bytes 1048576 | tf_op jit(solution)/shard_map/outer_part/pallas_call | solution.py:539
  77.9 0.7 collective-permute-start.7
  78.7 1.0 collective-permute-start.8
  79.6 0.0 collective-permute-done.9.near_ref
  79.6 18.3 %middle_part.1 = (f32[1024,512]{1,0:T(8,128)}, f32[1024,512]{1,0:T(8,128)}) custom-call(s32[1]{0:T(128)} %bitcast.refs_0_.f_ref, f32[128,128]{1,0:T(8,128)S(1)} %bitcast.6, f32[5,560,128]{2,1,0:T(8,128)S(1)} %get-tuple-element.33.vx_ref, f32[384,512]{1,0:T(8,128)S(1)} %collective-permute-done.9.near_ref, f32[1024,512]{1,0:T(8,128)S(1)} %copy-done, ...), custom_call_target="tpu_custom_call" | custom-call | bytes 1048576 | tf_op jit(solution)/shard_map/middle_part/pallas_call | solution.py:549
  98.0 0.0 collective-permute-done.8.far_ref
  98.0 0.0 collective-permute-done.7.theirs_ref
  98.0 0.9 insert.1
Async XLA Ops:
  0.6 2.2 %copy-start.1 = (f32[2,1024,512]{2,1,0:T(8,128)S(1)}, f32[2,1024,512]{2,1,0:T(8,128)}, u32[]{:S(2)}) copy-start(f32[2,1024,512]{2,1,0:T(8,128)} %refs_2_.1) | copy-start | bytes 12582916
  2.8 0.7 copy-start.2
  3.5 3.3 %copy-start = (f32[1024,512]{1,0:T(8,128)S(1)}, f32[1024,512]{1,0:T(8,128)}, u32[]{:S(2)}) copy-start(f32[1024,512]{1,0:T(8,128)} %ls_ref.5) | copy-start | bytes 6291460
  4.6 33.3 %collective-permute-start.5 = (f32[400,512]{1,0:T(8,128)S(1)}, f32[400,512]{1,0:T(8,128)S(1)}, u32[]{:S(2)}, u32[]{:S(2)}) collective-permute-start(f32[400,512]{1,0:T(8,128)S(1)} %send_part.1), channel_id=1, source_target_pairs={{0,64},{64,0},{1,65},{65,1},{2,66},{66,2},{3,67},{67,3},{4,68},{68... | collective-permute-start | bytes 2457608 | tf_op jit(solution)/shard_map/ppermute | solution.py:476
  8.8 9.5 %collective-permute-start = (f32[48,1024]{1,0:T(8,128)S(1)}, f32[48,1024]{1,0:T(8,128)S(1)}, u32[]{:S(2)}, u32[]{:S(2)}) collective-permute-start(f32[48,1024]{1,0:T(8,128)S(1)} %get-tuple-element.21), channel_id=1, source_target_pairs={{0,15},{1,0},{2,1},{3,2},{4,3},{5,4},{6,5},{7,6},{8,7},{9,8},{10,9... | collective-permute-start | bytes 589832 | tf_op jit(solution)/shard_map/ppermute | solution.py:485
  15.1 8.5 %collective-permute-start.1 = (f32[48,1024]{1,0:T(8,128)S(1)}, f32[48,1024]{1,0:T(8,128)S(1)}, u32[]{:S(2)}, u32[]{:S(2)}) collective-permute-start(f32[48,1024]{1,0:T(8,128)S(1)} %get-tuple-element.22), channel_id=1, source_target_pairs={{0,1},{1,2},{2,3},{3,4},{4,5},{5,6},{6,7},{7,8},{8,9},{9,10},{10,1... | collective-permute-start | bytes 589832 | tf_op jit(solution)/shard_map/ppermute | solution.py:486
  23.7 14.2 %collective-permute-start.6 = (f32[136,512]{1,0:T(8,128)S(1)}, f32[136,512]{1,0:T(8,128)S(1)}, u32[]{:S(2)}, u32[]{:S(2)}) collective-permute-start(f32[136,512]{1,0:T(8,128)S(1)} %get-tuple-element.27), channel_id=1, source_target_pairs={{0,64},{64,0},{1,65},{65,1},{2,66},{66,2},{3,67},{67,3},{4,68},{68... | collective-permute-start | bytes 835592 | tf_op jit(solution)/shard_map/ppermute | solution.py:504
  24.3 12.5 %collective-permute-start.2 = (f32[48,640]{1,0:T(8,128)S(1)}, f32[48,640]{1,0:T(8,128)S(1)}, u32[]{:S(2)}, u32[]{:S(2)}) collective-permute-start(f32[48,640]{1,0:T(8,128)S(1)} %get-tuple-element.23), channel_id=1, source_target_pairs={{0,16},{16,32},{32,48},{48,0},{64,112},{80,64},{96,80},{112,96},{1... | collective-permute-start | bytes 368648 | tf_op jit(solution)/shard_map/ppermute | solution.py:501
  29.1 7.7 %collective-permute-start.4 = (f32[48,640]{1,0:T(8,128)S(1)}, f32[48,640]{1,0:T(8,128)S(1)}, u32[]{:S(2)}, u32[]{:S(2)}) collective-permute-start(f32[48,640]{1,0:T(8,128)S(1)} %get-tuple-element.25), channel_id=1, source_target_pairs={{0,64},{64,0},{1,65},{65,1},{2,66},{66,2},{3,67},{67,3},{4,68},{68... | collective-permute-start | bytes 368648 | tf_op jit(solution)/shard_map/ppermute | solution.py:503
  29.1 7.7 %collective-permute-start.3 = (f32[24,640]{1,0:T(8,128)S(1)}, f32[24,640]{1,0:T(8,128)S(1)}, u32[]{:S(2)}, u32[]{:S(2)}) collective-permute-start(f32[24,640]{1,0:T(8,128)S(1)} %get-tuple-element.24), channel_id=1, source_target_pairs={{0,112},{16,64},{32,80},{48,96},{64,16},{80,32},{96,48},{112,0},{1... | collective-permute-start | bytes 184328 | tf_op jit(solution)/shard_map/ppermute | solution.py:502
  45.4 34.3 %collective-permute-start.9 = (f32[384,512]{1,0:T(8,128)S(1)}, f32[384,512]{1,0:T(8,128)S(1)}, u32[]{:S(2)}, u32[]{:S(2)}) collective-permute-start(f32[384,512]{1,0:T(8,128)S(1)} %get-tuple-element.35), channel_id=1, source_target_pairs={{0,64},{64,0},{1,65},{65,1},{2,66},{66,2},{3,67},{67,3},{4,68},{68... | collective-permute-start | bytes 2359304 | tf_op jit(solution)/shard_map/ppermute | solution.py:532
  77.9 20.1 %collective-permute-start.7 = (f32[192,512]{1,0:T(8,128)S(1)}, f32[192,512]{1,0:T(8,128)S(1)}, u32[]{:S(2)}, u32[]{:S(2)}) collective-permute-start(f32[192,512]{1,0:T(8,128)S(1)} %outer_part.1.mine_ref), channel_id=1, source_target_pairs={{0,64},{64,0},{1,65},{65,1},{2,66},{66,2},{3,67},{67,3},{4,68},{68... | collective-permute-start | bytes 1179656 | tf_op jit(solution)/shard_map/ppermute | solution.py:546
  78.7 19.3 %collective-permute-start.8 = (f32[176,512]{1,0:T(8,128)S(1)}, f32[176,512]{1,0:T(8,128)S(1)}, u32[]{:S(2)}, u32[]{:S(2)}) collective-permute-start(f32[176,512]{1,0:T(8,128)S(1)} %get-tuple-element.34), channel_id=1, source_target_pairs={{0,64},{64,0},{1,65},{65,1},{2,66},{66,2},{3,67},{67,3},{4,68},{68... | collective-permute-start | bytes 1081352 | tf_op jit(solution)/shard_map/ppermute | solution.py:533

commit v3 on v2

v3 whole, which is shorter than its diff:
```python
import jax
import jax.numpy as jnp
from jax import lax
from jax.experimental import pallas as pl
from jax.experimental.pallas import tpu as pltpu
from jax.sharding import PartitionSpec as P

EXT_SWEEPS = 8
REINIT_ITERS = 10
band_cells = 3.0
cfl_number = 0.5
pseudo_step = 0.5

HALO = 24
SIDE = 20
EDGE = 12
STAGED = 16
OWN_PARTS = (1, 4)
FIRST_PARTS = (26, 35)
EARLY = 128
LANES = 128
TINY = 1e-18

VMEM = pl.BlockSpec(memory_space=pltpu.VMEM)
SMEM = pl.BlockSpec(memory_space=pltpu.SMEM)
HBM = pl.BlockSpec(memory_space=pl.ANY)
DMA = pltpu.SemaphoreType.DMA


def vmem(*shape):
    return pltpu.VMEM(shape, jnp.float32)


def call(body, out_shapes, in_specs, scratch=(), name=None, out_specs=None, aliases=None, mib=16, us=1):
    out_specs = out_specs or [VMEM] * len(out_shapes)
    outs = [
        pltpu.HBM(s, jnp.float32) if spec is HBM else jax.ShapeDtypeStruct(s, jnp.float32)
        for s, spec in zip(out_shapes, out_specs)
    ]
    kernel = pl.pallas_call(
        body,
        out_shape=outs,
        in_specs=in_specs,
        out_specs=out_specs,
        scratch_shapes=list(scratch),
        name=name,
        input_output_aliases=aliases or {},
        compiler_params=pltpu.CompilerParams(vmem_limit_bytes=mib << 20),
        cost_estimate=pl.CostEstimate(flops=int(us * 1e9), bytes_accessed=0, transcendentals=0),
    )

    def run(*args):
        return kernel(
            *(pltpu.with_memory_space_constraint(x, pltpu.HBM) if spec is HBM else x for x, spec in zip(args, in_specs))
        )

    return run


def aligned(x, n=8):
    return pl.multiple_of(x, n)


def lanes_of(c):
    return slice(c * LANES, (c + 1) * LANES)


def blank(nat, f, main):
    for c in range(nat.shape[0]):
        nat[c, pl.ds(aligned(f * main), HALO), :] = jnp.zeros((HALO, LANES), jnp.float32)


def send_part(f_ref, w_hbm, g_ref, send_ref, buf, nat, w_ref, sems):
    n, main, cols = send_ref.shape[0], buf.shape[1], buf.shape[2]
    f = f_ref[0]
    start = (1 - f) * (g_ref.shape[1] - main)
    chunks = sems.shape[0] - 1
    weights = pltpu.make_async_copy(w_hbm, w_ref, sems.at[chunks])
    weights.start()
    step = main // 8 // chunks * 8
    spans = [(i * step, step if i < chunks - 1 else main - i * step) for i in range(chunks)]
    copies = [
        pltpu.make_async_copy(
            g_ref.at[:, pl.ds(aligned(start + at), n), :], buf.at[:, pl.ds(at, n), :], sems.at[i]
        )
        for i, (at, n) in enumerate(spans)
    ]
    for copy in copies:
        copy.start()
    blank(nat, 1 - f, main)
    weights.wait()
    for copy, (at, rows) in zip(copies, spans):
        copy.wait()
        part = w_ref[0] * buf[0, at : at + rows, :] + w_ref[1] * buf[1, at : at + rows, :]
        put(nat, pl.ds(aligned(f * HALO + at), rows), part)
    for k in range(n):
        send_ref[k] = spread(nat, nat.shape[1] // 8, k, cols)


def send_rest(main, f_ref, p_ref, _, send_ref, nat):
    rows, cols = p_ref.shape
    f = f_ref[0]
    r = nat.shape[1] // 8
    blank(nat, 1 - f, main)
    put(nat, pl.ds(aligned(f * HALO), main), p_ref[pl.ds(aligned((1 - f) * (rows - main)), main), :])
    for k in range(send_ref.shape[0]):
        send_ref[k] = spread(nat, r, r - send_ref.shape[0] + k, cols)


def strips(w_hbm, g_ref, ls_ref, p_ref, left_ref, right_ref, buf, w_ref, sems):
    rows, cols = ls_ref.shape
    chunks = sems.shape[0] - 1
    n = rows // chunks
    weights = pltpu.make_async_copy(w_hbm, w_ref, sems.at[chunks])
    weights.start()
    copies = [
        pltpu.make_async_copy(g_ref.at[:, pl.ds(i * n, n), :], buf.at[:, pl.ds(i * n, n), :], sems.at[i])
        for i in range(chunks)
    ]
    for copy in copies:
        copy.start()
    weights.wait()
    lane = lax.broadcasted_iota(jnp.int32, (LANES, LANES), 1)
    for i in range(rows // LANES):
        at = lanes_of(i)
        if i * LANES % n == 0:
            copies[i * LANES // n].wait()
        p_ref[at, :] = w_ref[0] * buf[0, at, :] + w_ref[1] * buf[1, at, :]
        first, last = slice(0, LANES), slice(cols - LANES, cols)
        packed = p_ref[at, first]
        for j, (ref, of) in enumerate(((ls_ref, first), (p_ref, last), (ls_ref, last)), 1):
            held = 0 if of.start == 0 else LANES - SIDE
            moved = pltpu.roll(ref[at, of], (j * SIDE - held) % LANES, 1)
            packed = jnp.where(lane < j * SIDE, packed, moved)
        turned_ = packed.T
        left_ref[:, at] = turned_[0 : 2 * SIDE, :]
        right_ref[:, at] = turned_[2 * SIDE : 4 * SIDE, :]


def turned(right, left):
    gap = jnp.zeros((LANES - 2 * SIDE, right.shape[1]), jnp.float32)
    return jnp.concatenate([right, gap, left], axis=0).T


def row_messages(f_ref, right_ref, left_ref, p_ref, ls_ref, fs_ref, m1_ref, m2_ref):
    rows, cols = ls_ref.shape
    f = f_ref[0]
    width = fs_ref.shape[1]
    theirs = pl.ds(aligned((1 - f) * (rows - width), LANES), width)
    fs_ref[0:SIDE, :] = right_ref[0:SIDE, theirs]
    fs_ref[SIDE:, :] = left_ref[0:SIDE, theirs]

    def corner(of, bottom):
        at = pl.ds(aligned(bottom * (rows - LANES), LANES), LANES)
        return turned(right_ref[of, at], left_ref[of, at])

    def ends(block, bottom):
        return jnp.where(bottom == 1, block[LANES - HALO :, :], block[0:HALO, :])

    outer, inner = 1 - f, f
    p_cols, ls_cols = slice(0, SIDE), slice(SIDE, 2 * SIDE)
    p_part, ls_part = slice(0, HALO), slice(HALO, 2 * HALO)
    at_outer = pl.ds(aligned(outer * (rows - HALO)), HALO)
    at_inner = pl.ds(aligned(inner * (rows - HALO)), HALO)
    m1_ref[p_part, 0:cols] = p_ref[at_outer, :]
    m1_ref[p_part, cols:] = ends(corner(p_cols, outer), outer)
    m1_ref[ls_part, 0:cols] = ls_ref[at_outer, :]
    m1_ref[ls_part, cols:] = ends(corner(ls_cols, outer), outer)
    m2_ref[:, 0:cols] = p_ref[at_inner, :]
    m2_ref[:, cols:] = ends(corner(p_cols, inner), inner)


def spread(nat, r, lo, width):
    return jnp.concatenate(
        [nat[c, pl.ds(lo, 8, stride=r), :] for c in range(width // LANES)], axis=1
    )


def unspread(nat, r, lo, value):
    for c in range(value.shape[1] // LANES):
        nat[c, pl.ds(lo, 8, stride=r), :] = value[:, lanes_of(c)]


def put(nat, rows, value, first=0):
    for c in range(value.shape[1] // LANES):
        nat[first + c, rows, :] = value[:, lanes_of(c)]


def half_setup(
    f_ref, p_ref, ls_ref, right_ref, left_ref, m1_ref, m2_ref, fs_ref,
    t_ref, q_ref, rec_ref, nat, lsx, pcol, lscol,
):
    rows, cols = ls_ref.shape
    f = f_ref[0]
    ext = lsx.shape[1]
    main = ext - HALO
    first = aligned((1 - f) * HALO)
    beside = pl.ds(aligned(f * main), HALO)
    put(nat, beside, m1_ref[0:HALO, :] + m2_ref[...])
    put(lsx, beside, m1_ref[HALO:, :])
    width = fs_ref.shape[1]
    skip = f * (width - main)
    lane0 = f * (rows - width)
    for i in range(width // LANES):
        at = pl.ds(aligned(lane0 + i * LANES, LANES), LANES)
        to = lanes_of(i)
        pcol[to, :] = turned(
            right_ref[0:SIDE, at] + fs_ref[0:SIDE, to], left_ref[0:SIDE, at] + fs_ref[SIDE:, to]
        )
        lscol[to, :] = turned(right_ref[SIDE:, at], left_ref[SIDE:, at])
    start = f * (rows - main)
    last = cols // LANES
    for i in range(main // 8):
        to = pl.ds(aligned(first + i * 8), 8)
        of = pl.ds(aligned(start + i * 8), 8)
        side = pl.ds(aligned(skip + i * 8), 8)
        put(nat, to, p_ref[of, :])
        put(lsx, to, ls_ref[of, :])
        nat[last, to, :] = pcol[side, :]
        lsx[last, to, :] = lscol[side, :]

    r = ext // 8
    for k in range(r):
        x = spread(lsx, r, k, cols + LANES) * (1.0 / band_cells)
        u = x * x
        q = 1.0 / (5.0 + 4.0 * u)
        q_ref[k] = q
        rec_ref[k] = (1.0 + u) * q
        t_ref[k] = spread(nat, r, k, cols + LANES)


def wrap(ref, r):
    ref[0] = pltpu.roll(ref[r], 1, 0)
    ref[r + 1] = pltpu.roll(ref[1], 7, 0)


def sweep(src, r, body, first=0):
    up, centre = src[first], src[first + 1]
    for k in range(first, r):
        down = src[k + 2]
        body(k, up, centre, down)
        up, centre = centre, down


def relaxed(a_ref, rec_ref, width):
    def relax(k, up, centre, down):
        beside = (up + down) + (pltpu.roll(centre, 1, 1) + pltpu.roll(centre, width - 1, 1))
        return a_ref[k] + rec_ref[k] * beside

    return relax


def add_part(t, part):
    cols = part.shape[1]
    return jnp.concatenate([t[:, 0:cols] + part, t[:, cols:]], axis=1)


def velocity_begun(t_ref, rp1_ref, q_ref, rec_ref, v0, v1, a_ref):
    n = rp1_ref.shape[0]
    for k in range(n):
        source = add_part(t_ref[k], rp1_ref[k])
        v0[k + 1] = source
        a_ref[k] = source * q_ref[k]
    relax = relaxed(a_ref, rec_ref, t_ref.shape[2])
    for level in range(1, EXT_SWEEPS + 1):
        src, dst = (v0, v1) if level % 2 else (v1, v0)

        def body(k, *cells):
            dst[k + 1] = relax(k, *cells)

        sweep(src, n - level, body, level)


def velocity_ended(
    f_ref, t_ref, rp1_ref, rp2_ref, q_ref, rec_ref, b0_ref, b1_ref, vs_hbm, early_ref, near_ref, top_ref,
    nat, a_ref, v0, v1, vs_ref, sems,
):
    n, _, cols = rp1_ref.shape
    r, _, width = t_ref.shape
    ext = 8 * r
    f = f_ref[0]
    group = r // sems.shape[0]
    copies = [
        pltpu.make_async_copy(vs_ref.at[pl.ds(i * group, group)], vs_hbm.at[pl.ds(i * group, group)], sems.at[i])
        for i in range(sems.shape[0])
    ]
    sub = lax.broadcasted_iota(jnp.int32, (8, cols), 0)
    tops = [jnp.zeros((8, cols), jnp.float32)] * 2
    done = set()

    def final(k, value):
        vs_ref[k] = value
        unspread(nat, r, k, value)
        done.add(k)
        i = k // group
        if all(i * group + j in done for j in range(group)):
            copies[i].start()
        size = jnp.abs(value[:, 0:cols])
        row = sub * r + k
        if k < HALO or 7 * r + k >= ext - HALO:
            size = jnp.where((row >= HALO) & (row < ext - HALO), size, 0.0)
        tops[k % 2] = jnp.maximum(tops[k % 2], size)

    edge = EXT_SWEEPS + 1
    for k in (*range(edge), *range(n - edge, n)):
        v0[k + 1] = b0_ref[k + 1]
        v1[k + 1] = b1_ref[k + 1]
    for k in (*range(EXT_SWEEPS), *range(n - EXT_SWEEPS, r)):
        source = add_part(t_ref[k], rp1_ref[k] if k < n else rp2_ref[k - n])
        a_ref[k] = source * q_ref[k]
        if k >= n:
            v0[k + 1] = source
    assert EXT_SWEEPS % 2 == 0
    for k in range(EXT_SWEEPS, n - EXT_SWEEPS):
        final(k, b0_ref[k + 1])
    wrap(v0, r)
    relax = relaxed(a_ref, rec_ref, width)
    for level in range(1, EXT_SWEEPS + 1):
        src, dst = (v0, v1) if level % 2 else (v1, v0)

        def body(k, *cells):
            value = relax(k, *cells)
            if level == EXT_SWEEPS:
                final(k, value)
            else:
                dst[k + 1] = value

        sweep(src, r, body, n - level)
        sweep(src, level, body)
        if level < EXT_SWEEPS:
            wrap(dst, r)
    near = near_ref.shape[0] - 2 * SIDE
    half = ext - 2 * HALO
    early = early_ref.shape[0]
    at_early = pl.ds(aligned(HALO + (1 - f) * (half - early)), early)
    at_near = pl.ds(aligned(HALO + (1 - f) * (half - early - near) + f * early), near)
    for c in range(cols // LANES):
        early_ref[:, lanes_of(c)] = nat[c, at_early, :]
        near_ref[0:near, lanes_of(c)] = nat[c, at_near, :]
    for i in range(half // LANES):
        side = nat[cols // LANES, HALO + i * LANES : HALO + (i + 1) * LANES, :].T
        near_ref[near : near + SIDE, lanes_of(i)] = side[0:SIDE, :]
        near_ref[near + SIDE :, lanes_of(i)] = side[LANES - SIDE :, :]
    for copy in copies:
        copy.wait()
    top_ref[...] = jnp.full(top_ref.shape, jnp.max(jnp.maximum(*tops)), jnp.float32)


def velocity_rows(f_ref, vs_hbm, early_ref, vx_hbm, far_hbm, vel_hbm, vs_ref, nat, sems):
    slabs, ext, _ = nat.shape
    last = slabs - 1
    r = ext // 8
    parts = 2
    group = r // parts
    used = iter(range(sems.shape[0]))

    def begin(src, dst):
        copy = pltpu.make_async_copy(src, dst, sems.at[next(used)])
        copy.start()
        return copy

    loads = [
        begin(vs_hbm.at[pl.ds(i * group, group)], vs_ref.at[pl.ds(i * group, group)]) for i in range(parts)
    ]
    for k in range(r):
        if k % group == 0:
            loads[k // group].wait()
        unspread(nat, r, k, vs_ref[k])
    far = far_hbm.shape[0]
    half = ext - 2 * HALO
    f = f_ref[0]
    at_far = pl.ds(aligned(HALO + f * (half - far)), far)
    lanes = [pl.ds(c * LANES, LANES) for c in range(last)]
    copies = [begin(nat.at[c, at_far, :], far_hbm.at[:, lanes[c]]) for c in range(last)]
    copies.append(begin(nat, vx_hbm))
    early = early_ref.shape[0]
    theirs = vel_hbm.at[pl.ds(aligned((1 - f) * half + f * (half - early)), early), :]
    copies.append(begin(early_ref, theirs))
    for c in range(last):
        mine = vel_hbm.at[pl.ds(aligned(f * half), half), lanes[c]]
        copies.append(begin(nat.at[c, pl.ds(HALO, half), :], mine))
    for copy in copies:
        copy.wait()


def speeds(sigma, centre, up, down, left, right):
    a = jnp.maximum(sigma * (centre - up), TINY)
    b = jnp.maximum(sigma * (centre - down), 0.0)
    c = jnp.maximum(sigma * (centre - left), 0.0)
    d = jnp.maximum(sigma * (centre - right), 0.0)
    return (a * a + b * b) + (c * c + d * d)


def reinit(top_ref, ls_nat, v_nat, base, r, out_nat, shift, p0, p1, h_ref, s_ref, width):
    step = cfl_number / (jnp.max(top_ref[...]) + 1e-06)
    for k in range(r):
        p0[k + 1] = spread(ls_nat, r, base + k, width)
    wrap(p0, r)

    def beside(centre):
        return pltpu.roll(centre, 1, 1), pltpu.roll(centre, width - 1, 1)

    def advance(k, up, centre, down):
        speed = spread(v_nat, r, base + k, width)
        sigma = jnp.where(speed >= 0.0, 1.0, -1.0)
        total = speeds(sigma, centre, up, down, *beside(centre))
        advanced = centre - step * (speed * (total * lax.rsqrt(total)))
        p1[k + 1] = advanced
        h_ref[k] = pseudo_step * (advanced * lax.rsqrt(advanced * advanced + 1.0))
        s_ref[k] = jnp.where(advanced >= 0.0, 1.0, -1.0)

    sweep(p0, r, advance)
    wrap(p1, r)

    def one(src, dst):
        def body(k, up, centre, down):
            total = speeds(s_ref[k], centre, up, down, *beside(centre))
            h = h_ref[k]
            dst[k + 1] = (centre + h) - h * (total * lax.rsqrt(total))

        sweep(src, r, body)
        wrap(dst, r)

    def pair(i, _):
        one(p1, p0)
        one(p0, p1)
        return 0

    assert REINIT_ITERS % 2 == 0
    lax.fori_loop(0, REINIT_ITERS // 2 - 1, pair, 0)
    one(p1, p0)
    cols = width - LANES

    def final(k, up, centre, down):
        left, right = beside(centre)
        c = centre[:, 0:cols]
        total = speeds(s_ref[k][:, 0:cols], c, up[:, 0:cols], down[:, 0:cols], left[:, 0:cols], right[:, 0:cols])
        h = h_ref[k][:, 0:cols]
        unspread(out_nat, r, k + shift, (c + h) - h * (total * lax.rsqrt(total)))

    sweep(p0, r, final)


def outer_part(
    f_ref, top_ref, ls_hbm, right_ref, left_ref, m1_ref, vx_hbm, out_ref,
    nat, lsn, vn, lscol, p0, p1, h_ref, s_ref, sems,
):
    n, cols = out_ref.shape
    rows = ls_hbm.shape[0]
    f = f_ref[0]
    staged = lsn.shape[1]
    last = cols // LANES
    inside = n + HALO
    first = aligned((1 - f) * HALO)
    start = aligned(f * (rows - inside))
    copies = [
        pltpu.make_async_copy(
            ls_hbm.at[pl.ds(start, inside), pl.ds(c * LANES, LANES)], lsn.at[c, pl.ds(first, inside), :], sems.at[c]
        )
        for c in range(last)
    ]
    from_ext = aligned(f * (vx_hbm.shape[1] - staged))
    copies.append(pltpu.make_async_copy(vx_hbm.at[:, pl.ds(from_ext, staged), :], vn, sems.at[last]))
    for copy in copies:
        copy.start()
    put(lsn, pl.ds(aligned(f * inside), HALO), m1_ref[HALO:, :])
    width = lscol.shape[0]
    for i in range(width // LANES):
        at = pl.ds(aligned(f * (rows - width) + i * LANES, LANES), LANES)
        lscol[lanes_of(i), :] = turned(right_ref[SIDE:, at], left_ref[SIDE:, at])
    lsn[last, pl.ds(first, inside), :] = lscol[pl.ds(aligned(f * (width - inside)), inside), :]
    for copy in copies:
        copy.wait()
    r = (n + 2 * EDGE) // 8
    reinit(top_ref, lsn, vn, HALO - EDGE, r, nat, STAGED - EDGE, p0, p1, h_ref, s_ref, cols + LANES)
    for c in range(last):
        out_ref[:, lanes_of(c)] = nat[c, STAGED : STAGED + n, :]


def middle_part(
    f_ref, top_ref, vx_hbm, early_ref, near_ref, ls_hbm, right_ref, left_ref, mine_ref, _, level_ref, vel_ref,
    nat, lsn, vn, p0, p1, h_ref, s_ref, sems,
):
    rows, cols = ls_hbm.shape
    f = f_ref[0]
    staged = lsn.shape[1]
    n = staged - 2 * STAGED
    r = (n + 2 * EDGE) // 8
    low = (rows - staged) // 2
    last = cols // LANES
    half = rows // 2
    cut = half - low
    near = near_ref.shape[0] - 2 * SIDE
    early = early_ref.shape[0]
    own = mine_ref.shape[0]
    used = iter(range(sems.shape[0]))

    def begin(src, dst):
        copy = pltpu.make_async_copy(src, dst, sems.at[next(used)])
        copy.start()
        return copy

    needed = [
        begin(
            vx_hbm.at[:, pl.ds(aligned(HALO + (1 - f) * low), cut), :],
            vn.at[:, pl.ds(aligned(f * cut), cut), :],
        )
    ]
    for c in range(last):
        needed.append(begin(ls_hbm.at[pl.ds(low, staged), pl.ds(c * LANES, LANES)], lsn.at[c]))
    ready = [
        begin(near_ref.at[pl.ds(0, near), :], vel_ref.at[pl.ds(aligned((1 - f) * (half + early) + f * low), near), :]),
        begin(mine_ref, level_ref.at[pl.ds(aligned(f * (rows - own)), own), :]),
    ]
    put(vn, pl.ds(aligned((1 - f) * cut + f * near), early), early_ref[...])
    put(vn, pl.ds(aligned((1 - f) * (cut + early)), near), near_ref[0:near, :])
    for i in range(rows // LANES):
        at = i * LANES
        first, end = max(at, low), min(at + LANES, low + staged)
        if first < end:
            block = turned(right_ref[SIDE:, at : at + LANES], left_ref[SIDE:, at : at + LANES])
            lsn[last, first - low : end - low, :] = block[first - at : end - at, :]
    for i in range(half // LANES):
        at = i * LANES
        block = turned(near_ref[near : near + SIDE, at : at + LANES], near_ref[near + SIDE :, at : at + LANES])

        @pl.when(f == 0)
        def _():
            end = min(at + LANES, staged - cut)
            if at < end:
                vn[last, cut + at : cut + end, :] = block[0 : end - at, :]

        @pl.when(f == 1)
        def _():
            first = max(at, low)
            if first < at + LANES:
                vn[last, first - low : at + LANES - low, :] = block[first - at :, :]

    for copy in needed:
        copy.wait()
    reinit(top_ref, lsn, vn, STAGED - EDGE, r, nat, STAGED - EDGE, p0, p1, h_ref, s_ref, cols + LANES)
    for c in range(last):
        ready.append(
            begin(nat.at[c, pl.ds(STAGED, n), :], level_ref.at[pl.ds(low + STAGED, n), pl.ds(c * LANES, LANES)])
        )
    for copy in ready:
        copy.wait()


def insert(f_ref, theirs_ref, far_ref, _, __, level_ref, vel_ref, sems):
    rows = level_ref.shape[0]
    n, far = theirs_ref.shape[0], far_ref.shape[0]
    f = f_ref[0]
    copies = [
        pltpu.make_async_copy(
            theirs_ref, level_ref.at[pl.ds(aligned((1 - f) * (rows - n)), n), :], sems.at[0]
        ),
        pltpu.make_async_copy(
            far_ref, vel_ref.at[pl.ds(aligned((1 - f) * (rows - far)), far), :], sems.at[1]
        ),
    ]
    for copy in copies:
        copy.start()
    for copy in copies:
        copy.wait()


def shifted(n, by):
    return [(i, (i + by) % n) for i in range(n)]


def per_device(level_set, focus_grads, focus_weight):
    rows, cols = level_set.shape
    half = rows // 2
    gx, gy = lax.axis_size("gx"), lax.axis_size("gy")
    f = lax.axis_index("focus").reshape(1).astype(jnp.int32)
    planes = focus_grads.shape[0]
    assert planes == 2 and lax.axis_size("focus") == 2
    swap = [(0, 1), (1, 0)]
    main, ext, wide = half + HALO, half + 2 * HALO, cols + LANES
    slabs = wide // LANES
    r = ext // 8
    part = r * FIRST_PARTS[0] // FIRST_PARTS[1]
    weights = pltpu.SMEM(focus_weight.shape, jnp.float32)

    (to_partner,) = call(
        send_part,
        [(part, 8, cols)],
        [SMEM, HBM, HBM],
        [vmem(planes, main, cols), vmem(slabs - 1, ext, LANES), weights, DMA((5,))],
        "send_part",
    )(f, focus_weight, focus_grads)
    from_partner = lax.ppermute(to_partner, "focus", swap)

    p, left, right = call(
        strips,
        [(rows, cols), (2 * SIDE, rows), (2 * SIDE, rows)],
        [HBM, HBM, VMEM],
        [vmem(planes, rows, cols), weights, DMA((5,))],
        "strips",
        mib=16,
        us=2,
    )(focus_weight, focus_grads, level_set)
    from_right = lax.ppermute(left, "gy", shifted(gy, -1))
    from_left = lax.ppermute(right, "gy", shifted(gy, 1))
    side = -(-main // LANES) * LANES
    fs, m1, m2 = call(
        row_messages,
        [(2 * SIDE, side), (2 * HALO, wide), (HALO, wide)],
        [SMEM, VMEM, VMEM, VMEM, VMEM],
        (),
        "row_messages",
    )(f, from_right, from_left, p, level_set)

    def place(f, x):
        return f * gx + x % gx

    same = [(place(0, x), place(0, x + 1)) for x in range(gx)] + [(place(1, x), place(1, x - 1)) for x in range(gx)]
    cross = [(place(0, x), place(1, x - 1)) for x in range(gx)] + [(place(1, x), place(0, x + 1)) for x in range(gx)]
    got1 = lax.ppermute(m1, ("focus", "gx"), same)
    got2 = lax.ppermute(m2, ("focus", "gx"), cross)
    got_fs = lax.ppermute(fs, "focus", swap)
    (to_partner2,) = call(
        lambda *refs: send_rest(main, *refs),
        [(r - part, 8, cols)],
        [SMEM, VMEM, VMEM],
        [vmem(slabs - 1, ext, LANES)],
        "send_rest",
    )(f, p, got2)
    from_partner2 = lax.ppermute(to_partner2, "focus", swap)
    t, q, rec = call(
        half_setup,
        [(r, 8, wide)] * 3,
        [SMEM] + [VMEM] * 7,
        [vmem(slabs, ext, LANES), vmem(slabs, ext, LANES), vmem(side, LANES), vmem(side, LANES)],
        "half_setup",
        us=2,
        mib=20,
    )(f, p, level_set, from_right, from_left, got1, got2, got_fs)
    devices = 2 * gx * gy
    own = rows * OWN_PARTS[0] // OWN_PARTS[1]
    far = own - STAGED
    near = half - far - EARLY
    b0, b1 = call(
        velocity_begun,
        [(r + 2, 8, wide)] * 2,
        [VMEM] * 4,
        [vmem(part, 8, wide)],
        "velocity_begun",
        us=4,
    )(t, from_partner, q, rec)
    vs, to_early, to_near, top = call(
        velocity_ended,
        [(r, 8, wide), (EARLY, cols), (near + 2 * SIDE, cols), (devices, LANES)],
        [SMEM] + [VMEM] * 7,
        [
            vmem(slabs, ext, LANES), vmem(r, 8, wide), vmem(r + 2, 8, wide), vmem(r + 2, 8, wide),
            vmem(r, 8, wide), DMA((7,)),
        ],
        "velocity_ended",
        us=5,
        out_specs=[HBM, VMEM, VMEM, VMEM],
        mib=24,
    )(f, t, from_partner, from_partner2, q, rec, b0, b1)
    got_early = lax.ppermute(to_early, "focus", swap)
    tops = lax.all_to_all(top, ("focus", "gx", "gy"), 0, 0)
    got_near = lax.ppermute(to_near, "focus", swap)
    vx, to_far, velocity = call(
        velocity_rows,
        [(slabs, ext, LANES), (far, cols), (rows, cols)],
        [SMEM, HBM, VMEM],
        [vmem(r, 8, wide), vmem(slabs, ext, LANES), DMA((2 * slabs + 2,))],
        "velocity_rows",
        us=60,
        out_specs=[HBM, HBM, HBM],
    )(f, vs, got_early)
    got_far = lax.ppermute(to_far, "focus", swap)

    def work(n):
        r = (n + 2 * EDGE) // 8
        return [vmem(r + 2, 8, wide)] * 2 + [vmem(r, 8, wide)] * 2

    staged = own + 2 * HALO
    (mine,) = call(
        outer_part,
        [(own, cols)],
        [SMEM, VMEM, HBM, VMEM, VMEM, VMEM, HBM],
        [vmem(slabs - 1, own + 2 * STAGED, LANES), vmem(slabs, staged, LANES), vmem(slabs, staged, LANES)]
        + [vmem(-(-(own + HALO) // LANES) * LANES, LANES)]
        + work(own)
        + [DMA((slabs,))],
        "outer_part",
        us=8,
    )(f, tops, level_set, from_right, from_left, got1, vx)
    theirs = lax.ppermute(mine, "focus", swap)
    mid = rows - 2 * own
    staged = mid + 2 * STAGED
    level, velocity = call(
        middle_part,
        [(rows, cols), (rows, cols)],
        [SMEM, VMEM, HBM, VMEM, VMEM, HBM, VMEM, VMEM, VMEM, HBM],
        [vmem(slabs - 1, staged, LANES), vmem(slabs, staged, LANES), vmem(slabs, staged, LANES)]
        + work(mid)
        + [DMA((2 * slabs + 1,))],
        "middle_part",
        us=20,
        out_specs=[HBM, HBM],
        aliases={9: 1},
        mib=20,
    )(f, tops, vx, got_early, got_near, level_set, from_right, from_left, mine, velocity)
    level, velocity = call(
        insert,
        [(rows, cols), (rows, cols)],
        [SMEM, VMEM, VMEM, HBM, HBM],
        [DMA((2,))],
        "insert",
        out_specs=[HBM, HBM],
        aliases={3: 0, 4: 1},
    )(f, theirs, got_far, level, velocity)
    return level, velocity


def solution(mesh):
    in_specs = (P("gx", "gy"), P("focus", "gx", "gy"), P("focus"))
    out_specs = (P("gx", "gy"), P("gx", "gy"))
    return jax.shard_map(
        per_device, mesh=mesh, in_specs=in_specs, out_specs=out_specs, check_vma=False
    )
```

time: 99.2 us -> 87 us (0.88)
  blocking collectives: 26.8 us -> 0 us
  starting transfers between devices: 15.6 us -> 26.1 us
  Pallas kernels: 36.7 us -> 42.7 us
  local copies, waits for them, and re-layouts: 2.84 us -> 0.01 us
    all_to_all x1 -> x0, blocking collectives: 26.8 us -> none  [per_device(): tops = lax.all_to_all(top, ('focus', 'gx', 'gy'), 0, 0)]
    all_to_all x0 -> x1, starting transfers between devices: none -> 8.06 us  [per_device(): tops = lax.all_to_all(top, ('focus', 'gx', 'gy'), 0, 0)]
    ppermute x1, waiting for transfers between devices: 7.66 us -> 0.01 us  [per_device(): got2 = lax.ppermute(m2, ('focus', 'gx'), cross)]
    pallas_call x9 -> x11, Pallas kernels: 36.7 us -> 42.7 us  [run(): kernel(*(pltpu.with_memory_space_constraint(x, pltpu.HBM) if spec is HBM...]
    all_to_all x0 -> x1, waiting for transfers between devices: none -> 4.83 us  [per_device(): tops = lax.all_to_all(top, ('focus', 'gx', 'gy'), 0, 0)]
    ppermute x1, waiting for transfers between devices: 0.01 us -> 2.92 us  [per_device(): got_fs = lax.ppermute(fs, 'focus', swap)]
    unnamed x6 -> x2, local copies, waits for them, and re-layouts: 2.84 us -> 0.01 us
    ppermute x1, starting transfers between devices: 0.01 us -> 2.71 us  [per_device(): got2 = lax.ppermute(m2, ('focus', 'gx'), cross)]
  transfers between devices with their start and end apart: 10 -> 12, of which waited for: 3 -> 5; matrix products, arithmetic and copies ran while one was open for 0% -> 0% of each run, Pallas kernels for 28% -> 41%
where the time goes in v3:
time: 87 us; the launch traced here: 86.7 us
  Pallas kernels  42.7 us (49%)
  starting transfers between devices  26.1 us (30%)
  waiting for transfers between devices  17 us (20%)
  between operations  0.92 us (1%)
    pallas_call x11, Pallas kernels, run(): kernel(*(pltpu.with_memory_space_constraint(x, pltpu.HBM) if spec is HBM...  42.7 us
    all_to_all x1, starting transfers between devices, per_device(): tops = lax.all_to_all(top, ('focus', 'gx', 'gy'), 0, 0)  8.06 us
    ppermute x1, starting transfers between devices, per_device(): from_right = lax.ppermute(left, 'gy', shifted(gy, -1))  6.28 us
    ppermute x1, waiting for transfers between devices, per_device(): from_left = lax.ppermute(right, 'gy', shifted(gy, 1))  4.94 us
    all_to_all x1, waiting for transfers between devices, per_device(): tops = lax.all_to_all(top, ('focus', 'gx', 'gy'), 0, 0)  4.83 us
    ppermute x1, waiting for transfers between devices, per_device(): got_fs = lax.ppermute(fs, 'focus', swap)  2.92 us
    ppermute x1, starting transfers between devices, per_device(): got2 = lax.ppermute(m2, ('focus', 'gx'), cross)  2.71 us
    ppermute x1, waiting for transfers between devices, per_device(): from_right = lax.ppermute(left, 'gy', shifted(gy, -1))  2.55 us
  transfers between devices with their start and end apart: 12, of which 5 were waited for; matrix products, arithmetic and copies ran while one was open for 0% of the time, Pallas kernels for 41%

profile of v3, /device:TPU:1, one launch (start us, length us, event | category | flops | bytes accessed | tf_op | source)
XLA Modules:
  0.0 86.7 jit_solution(8818187340949550438)
XLA Ops:
  0.6 0.0 copy-start
  0.6 1.8 %send_part.1 = f32[52,8,512]{2,1,0:T(8,128)S(1)} custom-call(s32[1]{0:T(128)} %bitcast.f_ref.refs_0_, f32[2]{0:T(128)} %w_hbm.3, f32[2,1024,512]{2,1,0:T(8,128)} %g_ref.3), custom_call_target="tpu_custom_call" | custom-call | flops 1000000000 | tf_op jit(solution)/shard_map/send_part/pallas_call | solution.py:53
  2.5 2.1 %collective-permute-start.5 = (f32[52,8,512]{2,1,0:T(8,128)S(1)}, f32[52,8,512]{2,1,0:T(8,128)S(1)}, u32[]{:S(2)}, u32[]{:S(2)}) collective-permute-start(f32[52,8,512]{2,1,0:T(8,128)S(1)} %send_part.1), channel_id=1, source_target_pairs={{0,64},{64,0},{1,65},{65,1},{2,66},{66,2},{3,67},{67,3},{4,68},{68... | collective-permute-start | bytes 2555912 | tf_op jit(solution)/shard_map/ppermute | solution.py:593
  4.6 0.0 copy-done
  4.6 2.5 %strips.1 = (f32[1024,512]{1,0:T(8,128)S(1)}, f32[40,1024]{1,0:T(8,128)S(1)}, f32[40,1024]{1,0:T(8,128)S(1)}) custom-call(f32[2]{0:T(128)} %w_hbm.3, f32[2,1024,512]{2,1,0:T(8,128)} %g_ref.3, f32[1024,512]{1,0:T(8,128)S(1)} %copy-done), custom_call_target="tpu_custom_call" | custom-call | flops 2000000000 | tf_op jit(solution)/shard_map/strips/pallas_call | solution.py:53
  7.1 6.3 %collective-permute-start = (f32[40,1024]{1,0:T(8,128)S(1)}, f32[40,1024]{1,0:T(8,128)S(1)}, u32[]{:S(2)}, u32[]{:S(2)}) collective-permute-start(f32[40,1024]{1,0:T(8,128)S(1)} %get-tuple-element.23), channel_id=1, source_target_pairs={{0,15},{1,0},{2,1},{3,2},{4,3},{5,4},{6,5},{7,6},{8,7},{9,8},{10,9... | collective-permute-start | bytes 491528 | tf_op jit(solution)/shard_map/ppermute | solution.py:604
  13.4 0.0 collective-permute-start.1
  13.4 2.5 %collective-permute-done.right_ref = f32[40,1024]{1,0:T(8,128)S(1)} collective-permute-done((f32[40,1024]{1,0:T(8,128)S(1)}, f32[40,1024]{1,0:T(8,128)S(1)}, u32[]{:S(2)}, u32[]{:S(2)}) %collective-permute-start) | collective-permute-done | bytes 163872 | tf_op jit(solution)/shard_map/ppermute | solution.py:604
  16.0 4.9 %collective-permute-done.1.left_ref = f32[40,1024]{1,0:T(8,128)S(1)} collective-permute-done((f32[40,1024]{1,0:T(8,128)S(1)}, f32[40,1024]{1,0:T(8,128)S(1)}, u32[]{:S(2)}, u32[]{:S(2)}) %collective-permute-start.1) | collective-permute-done | bytes 163872 | tf_op jit(solution)/shard_map/ppermute | solution.py:605
  20.9 0.1 row_messages.1
  21.0 2.7 %collective-permute-start.3 = (f32[24,640]{1,0:T(8,128)S(1)}, f32[24,640]{1,0:T(8,128)S(1)}, u32[]{:S(2)}, u32[]{:S(2)}) collective-permute-start(f32[24,640]{1,0:T(8,128)S(1)} %get-tuple-element.26), channel_id=1, source_target_pairs={{0,112},{16,64},{32,80},{48,96},{64,16},{80,32},{96,48},{112,0},{1... | collective-permute-start | bytes 184328 | tf_op jit(solution)/shard_map/ppermute | solution.py:621
  23.8 2.2 %collective-permute-start.2 = (f32[48,640]{1,0:T(8,128)S(1)}, f32[48,640]{1,0:T(8,128)S(1)}, u32[]{:S(2)}, u32[]{:S(2)}) collective-permute-start(f32[48,640]{1,0:T(8,128)S(1)} %get-tuple-element.25), channel_id=1, source_target_pairs={{0,16},{16,32},{32,48},{48,0},{64,112},{80,64},{96,80},{112,96},{1... | collective-permute-start | bytes 368648 | tf_op jit(solution)/shard_map/ppermute | solution.py:620
  26.0 0.0 collective-permute-start.4
  26.0 0.0 collective-permute-done.3.m2_ref.refs_2_
  26.0 0.1 send_rest.1
  26.1 1.6 %collective-permute-start.6 = (f32[18,8,512]{2,1,0:T(8,128)S(1)}, f32[18,8,512]{2,1,0:T(8,128)S(1)}, u32[]{:S(2)}, u32[]{:S(2)}) collective-permute-start(f32[18,8,512]{2,1,0:T(8,128)S(1)} %send_rest.1), channel_id=1, source_target_pairs={{0,64},{64,0},{1,65},{65,1},{2,66},{66,2},{3,67},{67,3},{4,68},{68... | collective-permute-start | bytes 884744 | tf_op jit(solution)/shard_map/ppermute | solution.py:630
  27.7 2.9 %collective-permute-done.4.fs_ref = f32[40,640]{1,0:T(8,128)S(1)} collective-permute-done((f32[40,640]{1,0:T(8,128)S(1)}, f32[40,640]{1,0:T(8,128)S(1)}, u32[]{:S(2)}, u32[]{:S(2)}) %collective-permute-start.4) | collective-permute-done | bytes 102432 | tf_op jit(solution)/shard_map/ppermute | solution.py:622
  30.6 0.0 collective-permute-done.2.m1_ref
  30.6 1.1 %half_setup.1 = (f32[70,8,640]{2,1,0:T(8,128)S(1)}, f32[70,8,640]{2,1,0:T(8,128)S(1)}, f32[70,8,640]{2,1,0:T(8,128)S(1)}) custom-call(s32[1]{0:T(128)} %bitcast.f_ref.refs_0_, f32[1024,512]{1,0:T(8,128)S(1)} %get-tuple-element.22.p_ref.refs_1_, f32[1024,512]{1,0:T(8,128)S(1)} %copy-done, f32[40,1024]{1,0:T(8,128)S(1)} %collective-permute-done.right_ref, ...), custom_call_target="tpu_custom_call" | custom-call | flops 2000000000 | tf_op jit(solution)/shard_map/half_setup/pallas_call | solution.py:53
  31.7 0.0 collective-permute-done.5.rp1_ref
  31.7 3.8 %velocity_begun.1 = (f32[72,8,640]{2,1,0:T(8,128)S(1)}, f32[72,8,640]{2,1,0:T(8,128)S(1)}) custom-call(f32[70,8,640]{2,1,0:T(8,128)S(1)} %get-tuple-element.28.t_ref, f32[52,8,512]{2,1,0:T(8,128)S(1)} %collective-permute-done.5.rp1_ref, f32[70,8,640]{2,1,0:T(8,128)S(1)} %get-tuple-element.29.q_ref, f32[70,8,640]{2,1,0:T(8,128)S(1)} %get-tuple-element.30.rec_ref), custom_call_target="tpu_custom_call" | custom-call | flops 4000000000 | tf_op jit(solution)/shard_map/velocity_begun/pallas_call | solution.py:53
  35.5 1.7 %collective-permute-done.6.rp2_ref = f32[18,8,512]{2,1,0:T(8,128)S(1)} collective-permute-done((f32[18,8,512]{2,1,0:T(8,128)S(1)}, f32[18,8,512]{2,1,0:T(8,128)S(1)}, u32[]{:S(2)}, u32[]{:S(2)}) %collective-permute-start.6) | collective-permute-done | bytes 294944 | tf_op jit(solution)/shard_map/ppermute | solution.py:630
  37.2 4.2 %velocity_ended.1 = (f32[70,8,640]{2,1,0:T(8,128)}, f32[128,512]{1,0:T(8,128)S(1)}, f32[184,512]{1,0:T(8,128)S(1)}, f32[128,128]{1,0:T(8,128)}) custom-call(s32[1]{0:T(128)} %bitcast.f_ref.refs_0_, f32[70,8,640]{2,1,0:T(8,128)S(1)} %get-tuple-element.28.t_ref, f32[52,8,512]{2,1,0:T(8,128)S(1)} %collective-permute-done.5.rp1_ref, ...), custom_call_target="tpu_custom_call" | custom-call | flops 5000000000 | tf_op jit(solution)/shard_map/velocity_ended/pallas_call | solution.py:53
  41.4 1.1 %collective-permute-start.7 = (f32[128,512]{1,0:T(8,128)S(1)}, f32[128,512]{1,0:T(8,128)S(1)}, u32[]{:S(2)}, u32[]{:S(2)}) collective-permute-start(f32[128,512]{1,0:T(8,128)S(1)} %get-tuple-element.35), channel_id=1, source_target_pairs={{0,64},{64,0},{1,65},{65,1},{2,66},{66,2},{3,67},{67,3},{4,68},{68... | collective-permute-start | bytes 786440 | tf_op jit(solution)/shard_map/ppermute | solution.py:665
  42.4 8.1 %all-to-all-start = ((f32[128,1,128]{2,1,0:T(1,128)}), f32[128,1,128]{2,1,0:T(1,128)S(1)}, u32[]{:S(2)}, u32[]{:S(2)}) async-start(f32[128,1,128]{2,1,0:T(1,128)} %bitcast.2), calls=%async_computation | async-start | bytes 131072 | tf_op jit(solution)/shard_map/all_to_all | solution.py:666
  50.5 1.5 %collective-permute-start.10 = (f32[184,512]{1,0:T(8,128)S(1)}, f32[184,512]{1,0:T(8,128)S(1)}, u32[]{:S(2)}, u32[]{:S(2)}) collective-permute-start(f32[184,512]{1,0:T(8,128)S(1)} %get-tuple-element.38), channel_id=1, source_target_pairs={{0,64},{64,0},{1,65},{65,1},{2,66},{66,2},{3,67},{67,3},{4,68},{68... | collective-permute-start | bytes 1130504 | tf_op jit(solution)/shard_map/ppermute | solution.py:667
  52.0 0.0 collective-permute-done.7.early_ref
  52.0 3.2 %velocity_rows.1 = (f32[5,560,128]{2,1,0:T(8,128)}, f32[240,512]{1,0:T(8,128)}, f32[1024,512]{1,0:T(8,128)}) custom-call(s32[1]{0:T(128)} %bitcast.f_ref.refs_0_, f32[70,8,640]{2,1,0:T(8,128)} %get-tuple-element.34.vs_hbm, f32[128,512]{1,0:T(8,128)S(1)} %collective-permute-done.7.early_ref), custom_call_target="tpu_custom_call" | custom-call | flops 60000002048 | tf_op jit(solution)/shard_map/velocity_rows/pallas_call | solution.py:53
  55.1 0.2 collective-permute-start.9
  55.3 4.8 %all-to-all-done = f32[128,1,128]{2,1,0:T(1,128)S(1)} async-done(((f32[128,1,128]{2,1,0:T(1,128)}), f32[128,1,128]{2,1,0:T(1,128)S(1)}, u32[]{:S(2)}, u32[]{:S(2)}) %all-to-all-start) | async-done | bytes 65568 | tf_op jit(solution)/shard_map/all_to_all | solution.py:666
  60.1 8.7 %outer_part.1.mine_ref = f32[256,512]{1,0:T(8,128)S(1)} custom-call(s32[1]{0:T(128)} %bitcast.f_ref.refs_0_, f32[128,128]{1,0:T(8,128)S(1)} %bitcast.5, f32[1024,512]{1,0:T(8,128)} %ls_hbm.3, f32[40,1024]{1,0:T(8,128)S(1)} %collective-permute-done.right_ref, f32[40,1024]{1,0:T(8,128)S(1)} %collective-permute-done.1.left_ref, ...), custom_call_target="tpu_custom_call" | custom-call | flops 8000000000 | tf_op jit(solution)/shard_map/outer_part/pallas_call | solution.py:53
  68.9 0.4 collective-permute-start.8
  69.3 0.0 collective-permute-done.10.near_ref
  69.3 16.3 %middle_part.1 = (f32[1024,512]{1,0:T(8,128)}, f32[1024,512]{1,0:T(8,128)}) custom-call(s32[1]{0:T(128)} %bitcast.f_ref.refs_0_, f32[128,128]{1,0:T(8,128)S(1)} %bitcast.6, f32[5,560,128]{2,1,0:T(8,128)} %get-tuple-element.36.vx_hbm, f32[128,512]{1,0:T(8,128)S(1)} %collective-permute-done.7.early_ref, ...), custom_call_target="tpu_custom_call", output_to_operand_aliasing={{1}: (9, {})} | custom-call | flops 20000000000 | tf_op jit(solution)/shard_map/middle_part/pallas_call | solution.py:53
  85.6 0.0 collective-permute-done.9.far_ref
  85.6 0.0 collective-permute-done.8.theirs_ref
  85.6 1.0 %insert.1 = (f32[1024,512]{1,0:T(8,128)}, f32[1024,512]{1,0:T(8,128)}) custom-call(s32[1]{0:T(128)} %bitcast.f_ref.refs_0_, f32[256,512]{1,0:T(8,128)S(1)} %collective-permute-done.8.theirs_ref, f32[240,512]{1,0:T(8,128)S(1)} %collective-permute-done.9.far_ref, f32[1024,512]{1,0:T(8,128)} %get-tuple-element.40._, ...), custom_call_target="tpu_custom_call", output_to_operand_aliasing={{0}: (3, {}), {1}: (4, {})} | custom-call | flops 1000000000 | tf_op jit(solution)/shard_map/insert/pallas_call | solution.py:53
Async XLA Ops:
  0.6 4.0 %copy-start = (f32[1024,512]{1,0:T(8,128)S(1)}, f32[1024,512]{1,0:T(8,128)}, u32[]{:S(2)}) copy-start(f32[1024,512]{1,0:T(8,128)} %ls_hbm.3) | copy-start | bytes 6291460
  2.5 29.2 %collective-permute-start.5 = (f32[52,8,512]{2,1,0:T(8,128)S(1)}, f32[52,8,512]{2,1,0:T(8,128)S(1)}, u32[]{:S(2)}, u32[]{:S(2)}) collective-permute-start(f32[52,8,512]{2,1,0:T(8,128)S(1)} %send_part.1), channel_id=1, source_target_pairs={{0,64},{64,0},{1,65},{65,1},{2,66},{66,2},{3,67},{67,3},{4,68},{68... | collective-permute-start | bytes 2555912 | tf_op jit(solution)/shard_map/ppermute | solution.py:593
  7.1 8.8 %collective-permute-start = (f32[40,1024]{1,0:T(8,128)S(1)}, f32[40,1024]{1,0:T(8,128)S(1)}, u32[]{:S(2)}, u32[]{:S(2)}) collective-permute-start(f32[40,1024]{1,0:T(8,128)S(1)} %get-tuple-element.23), channel_id=1, source_target_pairs={{0,15},{1,0},{2,1},{3,2},{4,3},{5,4},{6,5},{7,6},{8,7},{9,8},{10,9... | collective-permute-start | bytes 491528 | tf_op jit(solution)/shard_map/ppermute | solution.py:604
  13.4 7.5 %collective-permute-start.1 = (f32[40,1024]{1,0:T(8,128)S(1)}, f32[40,1024]{1,0:T(8,128)S(1)}, u32[]{:S(2)}, u32[]{:S(2)}) collective-permute-start(f32[40,1024]{1,0:T(8,128)S(1)} %get-tuple-element.24), channel_id=1, source_target_pairs={{0,1},{1,2},{2,3},{3,4},{4,5},{5,6},{6,7},{7,8},{8,9},{9,10},{10,1... | collective-permute-start | bytes 491528 | tf_op jit(solution)/shard_map/ppermute | solution.py:605
  21.0 4.9 %collective-permute-start.3 = (f32[24,640]{1,0:T(8,128)S(1)}, f32[24,640]{1,0:T(8,128)S(1)}, u32[]{:S(2)}, u32[]{:S(2)}) collective-permute-start(f32[24,640]{1,0:T(8,128)S(1)} %get-tuple-element.26), channel_id=1, source_target_pairs={{0,112},{16,64},{32,80},{48,96},{64,16},{80,32},{96,48},{112,0},{1... | collective-permute-start | bytes 184328 | tf_op jit(solution)/shard_map/ppermute | solution.py:621
  23.8 6.8 %collective-permute-start.2 = (f32[48,640]{1,0:T(8,128)S(1)}, f32[48,640]{1,0:T(8,128)S(1)}, u32[]{:S(2)}, u32[]{:S(2)}) collective-permute-start(f32[48,640]{1,0:T(8,128)S(1)} %get-tuple-element.25), channel_id=1, source_target_pairs={{0,16},{16,32},{32,48},{48,0},{64,112},{80,64},{96,80},{112,96},{1... | collective-permute-start | bytes 368648 | tf_op jit(solution)/shard_map/ppermute | solution.py:620
  26.0 4.6 %collective-permute-start.4 = (f32[40,640]{1,0:T(8,128)S(1)}, f32[40,640]{1,0:T(8,128)S(1)}, u32[]{:S(2)}, u32[]{:S(2)}) collective-permute-start(f32[40,640]{1,0:T(8,128)S(1)} %get-tuple-element.27), channel_id=1, source_target_pairs={{0,64},{64,0},{1,65},{65,1},{2,66},{66,2},{3,67},{67,3},{4,68},{68... | collective-permute-start | bytes 307208 | tf_op jit(solution)/shard_map/ppermute | solution.py:622
  26.1 11.1 %collective-permute-start.6 = (f32[18,8,512]{2,1,0:T(8,128)S(1)}, f32[18,8,512]{2,1,0:T(8,128)S(1)}, u32[]{:S(2)}, u32[]{:S(2)}) collective-permute-start(f32[18,8,512]{2,1,0:T(8,128)S(1)} %send_rest.1), channel_id=1, source_target_pairs={{0,64},{64,0},{1,65},{65,1},{2,66},{66,2},{3,67},{67,3},{4,68},{68... | collective-permute-start | bytes 884744 | tf_op jit(solution)/shard_map/ppermute | solution.py:630
  41.4 10.6 %collective-permute-start.7 = (f32[128,512]{1,0:T(8,128)S(1)}, f32[128,512]{1,0:T(8,128)S(1)}, u32[]{:S(2)}, u32[]{:S(2)}) collective-permute-start(f32[128,512]{1,0:T(8,128)S(1)} %get-tuple-element.35), channel_id=1, source_target_pairs={{0,64},{64,0},{1,65},{65,1},{2,66},{66,2},{3,67},{67,3},{4,68},{68... | collective-permute-start | bytes 786440 | tf_op jit(solution)/shard_map/ppermute | solution.py:665
  42.4 17.7 %all-to-all-start = ((f32[128,1,128]{2,1,0:T(1,128)}), f32[128,1,128]{2,1,0:T(1,128)S(1)}, u32[]{:S(2)}, u32[]{:S(2)}) async-start(f32[128,1,128]{2,1,0:T(1,128)} %bitcast.2), calls=%async_computation | async-start | bytes 131072 | tf_op jit(solution)/shard_map/all_to_all | solution.py:666
  50.5 18.8 %collective-permute-start.10 = (f32[184,512]{1,0:T(8,128)S(1)}, f32[184,512]{1,0:T(8,128)S(1)}, u32[]{:S(2)}, u32[]{:S(2)}) collective-permute-start(f32[184,512]{1,0:T(8,128)S(1)} %get-tuple-element.38), channel_id=1, source_target_pairs={{0,64},{64,0},{1,65},{65,1},{2,66},{66,2},{3,67},{67,3},{4,68},{68... | collective-permute-start | bytes 1130504 | tf_op jit(solution)/shard_map/ppermute | solution.py:667
  55.1 30.4 %collective-permute-start.9 = (f32[240,512]{1,0:T(8,128)}, f32[240,512]{1,0:T(8,128)S(1)}, u32[]{:S(2)}, u32[]{:S(2)}) collective-permute-start(f32[240,512]{1,0:T(8,128)} %get-tuple-element.37), channel_id=1, source_target_pairs={{0,64},{64,0},{1,65},{65,1},{2,66},{66,2},{3,67},{67,3},{4,68},{68... | collective-permute-start | bytes 1474568 | tf_op jit(solution)/shard_map/ppermute | solution.py:677
  68.9 16.7 %collective-permute-start.8 = (f32[256,512]{1,0:T(8,128)S(1)}, f32[256,512]{1,0:T(8,128)S(1)}, u32[]{:S(2)}, u32[]{:S(2)}) collective-permute-start(f32[256,512]{1,0:T(8,128)S(1)} %outer_part.1.mine_ref), channel_id=1, source_target_pairs={{0,64},{64,0},{1,65},{65,1},{2,66},{66,2},{3,67},{67,3},{4,68},{68... | collective-permute-start | bytes 1572872 | tf_op jit(solution)/shard_map/ppermute | solution.py:695

commit v4 on v3

--- a/solution.py
+++ b/solution.py
@@ -16,8 +16,8 @@
 EDGE = 12
 STAGED = 16
 OWN_PARTS = (1, 4)
-FIRST_PARTS = (26, 35)
-EARLY = 128
+FIRST_PARTS = (27, 35)
+EARLY = 208
 LANES = 128
 TINY = 1e-18
 
@@ -341,9 +341,9 @@
         side = nat[cols // LANES, HALO + i * LANES : HALO + (i + 1) * LANES, :].T
         near_ref[near : near + SIDE, lanes_of(i)] = side[0:SIDE, :]
         near_ref[near + SIDE :, lanes_of(i)] = side[LANES - SIDE :, :]
+    top_ref[...] = jnp.full(top_ref.shape, jnp.max(jnp.maximum(*tops)), jnp.float32)
     for copy in copies:
         copy.wait()
-    top_ref[...] = jnp.full(top_ref.shape, jnp.max(jnp.maximum(*tops)), jnp.float32)
 
 
 def velocity_rows(f_ref, vs_hbm, early_ref, vx_hbm, far_hbm, vel_hbm, vs_ref, nat, sems):
@@ -383,42 +383,55 @@
         copy.wait()
 
 
-def speeds(sigma, centre, up, down, left, right):
-    a = jnp.maximum(sigma * (centre - up), TINY)
-    b = jnp.maximum(sigma * (centre - down), 0.0)
-    c = jnp.maximum(sigma * (centre - left), 0.0)
-    d = jnp.maximum(sigma * (centre - right), 0.0)
+def speeds(sigma, above, below, before, after):
+    a = jnp.maximum(sigma * above, TINY)
+    b = jnp.minimum(sigma * below, 0.0)
+    c = jnp.maximum(sigma * before, 0.0)
+    d = jnp.minimum(sigma * after, 0.0)
     return (a * a + b * b) + (c * c + d * d)
 
 
-def reinit(top_ref, ls_nat, v_nat, base, r, out_nat, shift, p0, p1, h_ref, s_ref, width):
+def differences(src, r, width, body):
+    centre = src[1]
+    above = centre - src[0]
+    for k in range(r):
+        down = src[k + 2]
+        below = down - centre
+        before = centre - pltpu.roll(centre, 1, 1)
+        after = pltpu.roll(centre, width - 1, 1) - centre
+        body(k, centre, above, below, before, after)
+        centre, above = down, below
+
+
+def reinit(top_ref, ls_nat, v_nat, base, r, out_nat, shift, p0, p1, h_ref, s_ref, width, coming=(), later=()):
     step = cfl_number / (jnp.max(top_ref[...]) + 1e-06)
     for k in range(r):
         p0[k + 1] = spread(ls_nat, r, base + k, width)
     wrap(p0, r)
-
-    def beside(centre):
-        return pltpu.roll(centre, 1, 1), pltpu.roll(centre, width - 1, 1)
-
-    def advance(k, up, centre, down):
+    for copy in coming:
+        copy.wait()
+    for copy in later:
+        copy.start()
+
+    def advance(k, centre, *steps):
         speed = spread(v_nat, r, base + k, width)
         sigma = jnp.where(speed >= 0.0, 1.0, -1.0)
-        total = speeds(sigma, centre, up, down, *beside(centre))
+        total = speeds(sigma, *steps)
         advanced = centre - step * (speed * (total * lax.rsqrt(total)))
         p1[k + 1] = advanced
         h_ref[k] = pseudo_step * (advanced * lax.rsqrt(advanced * advanced + 1.0))
         s_ref[k] = jnp.where(advanced >= 0.0, 1.0, -1.0)
 
-    sweep(p0, r, advance)
+    differences(p0, r, width, advance)
     wrap(p1, r)
 
     def one(src, dst):
-        def body(k, up, centre, down):
-            total = speeds(s_ref[k], centre, up, down, *beside(centre))
+        def body(k, centre, *steps):
+            total = speeds(s_ref[k], *steps)
             h = h_ref[k]
             dst[k + 1] = (centre + h) - h * (total * lax.rsqrt(total))
 
-        sweep(src, r, body)
+        differences(src, r, width, body)
         wrap(dst, r)
 
     def pair(i, _):
@@ -431,18 +444,16 @@
     one(p1, p0)
     cols = width - LANES
 
-    def final(k, up, centre, down):
-        left, right = beside(centre)
-        c = centre[:, 0:cols]
-        total = speeds(s_ref[k][:, 0:cols], c, up[:, 0:cols], down[:, 0:cols], left[:, 0:cols], right[:, 0:cols])
+    def final(k, centre, *steps):
+        total = speeds(s_ref[k][:, 0:cols], *(x[:, 0:cols] for x in steps))
         h = h_ref[k][:, 0:cols]
-        unspread(out_nat, r, k + shift, (c + h) - h * (total * lax.rsqrt(total)))
-
-    sweep(p0, r, final)
+        unspread(out_nat, r, k + shift, (centre[:, 0:cols] + h) - h * (total * lax.rsqrt(total)))
+
+    differences(p0, r, width, final)
 
 
 def outer_part(
-    f_ref, top_ref, ls_hbm, right_ref, left_ref, m1_ref, vx_hbm, out_ref,
+    f_ref, top_ref, ls_hbm, right_ref, left_ref, m1_ref, vx_hbm, out_ref, lsm_ref, vm_ref,
     nat, lsn, vn, lscol, p0, p1, h_ref, s_ref, sems,
 ):
     n, cols = out_ref.shape
@@ -463,25 +474,49 @@
     copies.append(pltpu.make_async_copy(vx_hbm.at[:, pl.ds(from_ext, staged), :], vn, sems.at[last]))
     for copy in copies:
         copy.start()
+    middle, cut = lsm_ref.shape[1], vm_ref.shape[1]
+    low = (rows - middle) // 2
+    later = [
+        pltpu.make_async_copy(
+            ls_hbm.at[pl.ds(low, middle), pl.ds(c * LANES, LANES)], lsm_ref.at[c], sems.at[last + 1 + c]
+        )
+        for c in range(last)
+    ]
+    later.append(
+        pltpu.make_async_copy(
+            vx_hbm.at[:, pl.ds(aligned(HALO + (1 - f) * low), cut), :], vm_ref, sems.at[2 * last + 1]
+        )
+    )
     put(lsn, pl.ds(aligned(f * inside), HALO), m1_ref[HALO:, :])
     width = lscol.shape[0]
     for i in range(width // LANES):
         at = pl.ds(aligned(f * (rows - width) + i * LANES, LANES), LANES)
         lscol[lanes_of(i), :] = turned(right_ref[SIDE:, at], left_ref[SIDE:, at])
     lsn[last, pl.ds(first, inside), :] = lscol[pl.ds(aligned(f * (width - inside)), inside), :]
-    for copy in copies:
+    for copy in copies[:last]:
         copy.wait()
     r = (n + 2 * EDGE) // 8
-    reinit(top_ref, lsn, vn, HALO - EDGE, r, nat, STAGED - EDGE, p0, p1, h_ref, s_ref, cols + LANES)
+    reinit(
+        top_ref, lsn, vn, HALO - EDGE, r, nat, STAGED - EDGE, p0, p1, h_ref, s_ref, cols + LANES,
+        copies[last:], later,
+    )
     for c in range(last):
         out_ref[:, lanes_of(c)] = nat[c, STAGED : STAGED + n, :]
+    for i in range(rows // LANES):
+        at = i * LANES
+        first, end = max(at, low), min(at + LANES, low + middle)
+        if first < end:
+            block = turned(right_ref[SIDE:, at : at + LANES], left_ref[SIDE:, at : at + LANES])
+            lsm_ref[last, first - low : end - low, :] = block[first - at : end - at, :]
+    for copy in later:
+        copy.wait()
 
 
 def middle_part(
-    f_ref, top_ref, vx_hbm, early_ref, near_ref, ls_hbm, right_ref, left_ref, mine_ref, _, level_ref, vel_ref,
-    nat, lsn, vn, p0, p1, h_ref, s_ref, sems,
+    f_ref, top_ref, vm_ref, early_ref, near_ref, lsn, mine_ref, _, level_ref, vel_ref,
+    nat, vn, p0, p1, h_ref, s_ref, sems,
 ):
-    rows, cols = ls_hbm.shape
+    rows, cols = level_ref.shape
     f = f_ref[0]
     staged = lsn.shape[1]
     n = staged - 2 * STAGED
@@ -500,26 +535,14 @@
         copy.start()
         return copy
 
-    needed = [
-        begin(
-            vx_hbm.at[:, pl.ds(aligned(HALO + (1 - f) * low), cut), :],
-            vn.at[:, pl.ds(aligned(f * cut), cut), :],
-        )
-    ]
-    for c in range(last):
-        needed.append(begin(ls_hbm.at[pl.ds(low, staged), pl.ds(c * LANES, LANES)], lsn.at[c]))
     ready = [
         begin(near_ref.at[pl.ds(0, near), :], vel_ref.at[pl.ds(aligned((1 - f) * (half + early) + f * low), near), :]),
         begin(mine_ref, level_ref.at[pl.ds(aligned(f * (rows - own)), own), :]),
     ]
+    for c in range(last + 1):
+        vn[c, pl.ds(aligned(f * cut), cut), :] = vm_ref[c]
     put(vn, pl.ds(aligned((1 - f) * cut + f * near), early), early_ref[...])
     put(vn, pl.ds(aligned((1 - f) * (cut + early)), near), near_ref[0:near, :])
-    for i in range(rows // LANES):
-        at = i * LANES
-        first, end = max(at, low), min(at + LANES, low + staged)
-        if first < end:
-            block = turned(right_ref[SIDE:, at : at + LANES], left_ref[SIDE:, at : at + LANES])
-            lsn[last, first - low : end - low, :] = block[first - at : end - at, :]
     for i in range(half // LANES):
         at = i * LANES
         block = turned(near_ref[near : near + SIDE, at : at + LANES], near_ref[near + SIDE :, at : at + LANES])
@@ -536,8 +559,6 @@
             if first < at + LANES:
                 vn[last, first - low : at + LANES - low, :] = block[first - at :, :]
 
-    for copy in needed:
-        copy.wait()
     reinit(top_ref, lsn, vn, STAGED - EDGE, r, nat, STAGED - EDGE, p0, p1, h_ref, s_ref, cols + LANES)
     for c in range(last):
         ready.append(
@@ -587,7 +608,7 @@
         send_part,
         [(part, 8, cols)],
         [SMEM, HBM, HBM],
-        [vmem(planes, main, cols), vmem(slabs - 1, ext, LANES), weights, DMA((5,))],
+        [vmem(planes, main, cols), vmem(slabs - 1, ext, LANES), weights, DMA((9,))],
         "send_part",
     )(f, focus_weight, focus_grads)
     from_partner = lax.ppermute(to_partner, "focus", swap)
@@ -681,33 +702,33 @@
         return [vmem(r + 2, 8, wide)] * 2 + [vmem(r, 8, wide)] * 2
 
     staged = own + 2 * HALO
-    (mine,) = call(
+    mid = rows - 2 * own
+    middle = mid + 2 * STAGED
+    mine, ls_mid, v_mid = call(
         outer_part,
-        [(own, cols)],
+        [(own, cols), (slabs, middle, LANES), (slabs, middle // 2, LANES)],
         [SMEM, VMEM, HBM, VMEM, VMEM, VMEM, HBM],
         [vmem(slabs - 1, own + 2 * STAGED, LANES), vmem(slabs, staged, LANES), vmem(slabs, staged, LANES)]
         + [vmem(-(-(own + HALO) // LANES) * LANES, LANES)]
         + work(own)
-        + [DMA((slabs,))],
+        + [DMA((2 * slabs,))],
         "outer_part",
         us=8,
     )(f, tops, level_set, from_right, from_left, got1, vx)
     theirs = lax.ppermute(mine, "focus", swap)
-    mid = rows - 2 * own
-    staged = mid + 2 * STAGED
     level, velocity = call(
         middle_part,
         [(rows, cols), (rows, cols)],
-        [SMEM, VMEM, HBM, VMEM, VMEM, HBM, VMEM, VMEM, VMEM, HBM],
-        [vmem(slabs - 1, staged, LANES), vmem(slabs, staged, LANES), vmem(slabs, staged, LANES)]
+        [SMEM] + [VMEM] * 6 + [HBM],
+        [vmem(slabs - 1, middle, LANES), vmem(slabs, middle, LANES)]
         + work(mid)
-        + [DMA((2 * slabs + 1,))],
+        + [DMA((slabs + 1,))],
         "middle_part",
         us=20,
         out_specs=[HBM, HBM],
-        aliases={9: 1},
+        aliases={7: 1},
         mib=20,
-    )(f, tops, vx, got_early, got_near, level_set, from_right, from_left, mine, velocity)
+    )(f, tops, v_mid, got_early, got_near, ls_mid, mine, velocity)
     level, velocity = call(
         insert,
         [(rows, cols), (rows, cols)],

time: 87 us -> 84.4 us (0.970)
  Pallas kernels: 42.7 us -> 40.4 us
  waiting for transfers between devices: 17 us -> 15.9 us
    pallas_call x11, Pallas kernels: 42.7 us -> 40.4 us  [run(): kernel(*(pltpu.with_memory_space_constraint(x, pltpu.HBM) if spec is HBM...]
  transfers between devices with their start and end apart: 12 -> 12, of which waited for: 5 -> 5; matrix products, arithmetic and copies ran while one was open for 0% -> 0% of each run, Pallas kernels for 41% -> 40%
where the time goes in v4:
time: 84.4 us; the launch traced here: 84.2 us
  Pallas kernels  40.4 us (48%)
  starting transfers between devices  26.9 us (32%)
  waiting for transfers between devices  15.9 us (19%)
  between operations  0.92 us (1%)
    pallas_call x11, Pallas kernels, run(): kernel(*(pltpu.with_memory_space_constraint(x, pltpu.HBM) if spec is HBM...  40.4 us
    all_to_all x1, starting transfers between devices, per_device(): tops = lax.all_to_all(top, ('focus', 'gx', 'gy'), 0, 0)  8.76 us
    ppermute x1, starting transfers between devices, per_device(): from_right = lax.ppermute(left, 'gy', shifted(gy, -1))  6.28 us
    ppermute x1, waiting for transfers between devices, per_device(): from_left = lax.ppermute(right, 'gy', shifted(gy, 1))  4.94 us
    all_to_all x1, waiting for transfers between devices, per_device(): tops = lax.all_to_all(top, ('focus', 'gx', 'gy'), 0, 0)  4.63 us
    ppermute x1, waiting for transfers between devices, per_device(): got_fs = lax.ppermute(fs, 'focus', swap)  2.92 us
    ppermute x1, starting transfers between devices, per_device(): got2 = lax.ppermute(m2, ('focus', 'gx'), cross)  2.71 us
    ppermute x1, waiting for transfers between devices, per_device(): from_right = lax.ppermute(left, 'gy', shifted(gy, -1))  2.55 us
  transfers between devices with their start and end apart: 12, of which 5 were waited for; matrix products, arithmetic and copies ran while one was open for 0% of the time, Pallas kernels for 40%

profile of v4, /device:TPU:1, one launch (start us, length us, event | category | flops | bytes accessed | tf_op | source)
XLA Modules:
  0.0 84.2 jit_solution(4619141650957201592)
XLA Ops:
  0.6 0.0 copy-start
  0.6 1.9 %send_part.1 = f32[54,8,512]{2,1,0:T(8,128)S(1)} custom-call(s32[1]{0:T(128)} %bitcast.f_ref.refs_0_, f32[2]{0:T(128)} %w_hbm.3, f32[2,1024,512]{2,1,0:T(8,128)} %g_ref.3), custom_call_target="tpu_custom_call" | custom-call | flops 1000000000 | tf_op jit(solution)/shard_map/send_part/pallas_call | solution.py:53
  2.5 2.1 %collective-permute-start.5 = (f32[54,8,512]{2,1,0:T(8,128)S(1)}, f32[54,8,512]{2,1,0:T(8,128)S(1)}, u32[]{:S(2)}, u32[]{:S(2)}) collective-permute-start(f32[54,8,512]{2,1,0:T(8,128)S(1)} %send_part.1), channel_id=1, source_target_pairs={{0,64},{64,0},{1,65},{65,1},{2,66},{66,2},{3,67},{67,3},{4,68},{68... | collective-permute-start | bytes 2654216 | tf_op jit(solution)/shard_map/ppermute | solution.py:614
  4.6 0.0 copy-done
  4.6 2.5 %strips.1 = (f32[1024,512]{1,0:T(8,128)S(1)}, f32[40,1024]{1,0:T(8,128)S(1)}, f32[40,1024]{1,0:T(8,128)S(1)}) custom-call(f32[2]{0:T(128)} %w_hbm.3, f32[2,1024,512]{2,1,0:T(8,128)} %g_ref.3, f32[1024,512]{1,0:T(8,128)S(1)} %copy-done), custom_call_target="tpu_custom_call" | custom-call | flops 2000000000 | tf_op jit(solution)/shard_map/strips/pallas_call | solution.py:53
  7.1 6.3 %collective-permute-start = (f32[40,1024]{1,0:T(8,128)S(1)}, f32[40,1024]{1,0:T(8,128)S(1)}, u32[]{:S(2)}, u32[]{:S(2)}) collective-permute-start(f32[40,1024]{1,0:T(8,128)S(1)} %get-tuple-element.26), channel_id=1, source_target_pairs={{0,15},{1,0},{2,1},{3,2},{4,3},{5,4},{6,5},{7,6},{8,7},{9,8},{10,9... | collective-permute-start | bytes 491528 | tf_op jit(solution)/shard_map/ppermute | solution.py:625
  13.4 0.0 collective-permute-start.1
  13.4 2.5 %collective-permute-done.right_ref = f32[40,1024]{1,0:T(8,128)S(1)} collective-permute-done((f32[40,1024]{1,0:T(8,128)S(1)}, f32[40,1024]{1,0:T(8,128)S(1)}, u32[]{:S(2)}, u32[]{:S(2)}) %collective-permute-start) | collective-permute-done | bytes 163872 | tf_op jit(solution)/shard_map/ppermute | solution.py:625
  16.0 4.9 %collective-permute-done.1.left_ref = f32[40,1024]{1,0:T(8,128)S(1)} collective-permute-done((f32[40,1024]{1,0:T(8,128)S(1)}, f32[40,1024]{1,0:T(8,128)S(1)}, u32[]{:S(2)}, u32[]{:S(2)}) %collective-permute-start.1) | collective-permute-done | bytes 163872 | tf_op jit(solution)/shard_map/ppermute | solution.py:626
  20.9 0.1 row_messages.1
  21.0 2.7 %collective-permute-start.3 = (f32[24,640]{1,0:T(8,128)S(1)}, f32[24,640]{1,0:T(8,128)S(1)}, u32[]{:S(2)}, u32[]{:S(2)}) collective-permute-start(f32[24,640]{1,0:T(8,128)S(1)} %get-tuple-element.29), channel_id=1, source_target_pairs={{0,112},{16,64},{32,80},{48,96},{64,16},{80,32},{96,48},{112,0},{1... | collective-permute-start | bytes 184328 | tf_op jit(solution)/shard_map/ppermute | solution.py:642
  23.8 2.2 %collective-permute-start.2 = (f32[48,640]{1,0:T(8,128)S(1)}, f32[48,640]{1,0:T(8,128)S(1)}, u32[]{:S(2)}, u32[]{:S(2)}) collective-permute-start(f32[48,640]{1,0:T(8,128)S(1)} %get-tuple-element.28), channel_id=1, source_target_pairs={{0,16},{16,32},{32,48},{48,0},{64,112},{80,64},{96,80},{112,96},{1... | collective-permute-start | bytes 368648 | tf_op jit(solution)/shard_map/ppermute | solution.py:641
  26.0 0.0 collective-permute-start.4
  26.0 0.0 collective-permute-done.3.m2_ref.refs_2_
  26.0 0.1 send_rest.1
  26.1 1.6 %collective-permute-start.6 = (f32[16,8,512]{2,1,0:T(8,128)S(1)}, f32[16,8,512]{2,1,0:T(8,128)S(1)}, u32[]{:S(2)}, u32[]{:S(2)}) collective-permute-start(f32[16,8,512]{2,1,0:T(8,128)S(1)} %send_rest.1), channel_id=1, source_target_pairs={{0,64},{64,0},{1,65},{65,1},{2,66},{66,2},{3,67},{67,3},{4,68},{68... | collective-permute-start | bytes 786440 | tf_op jit(solution)/shard_map/ppermute | solution.py:651
  27.7 2.9 %collective-permute-done.4.fs_ref = f32[40,640]{1,0:T(8,128)S(1)} collective-permute-done((f32[40,640]{1,0:T(8,128)S(1)}, f32[40,640]{1,0:T(8,128)S(1)}, u32[]{:S(2)}, u32[]{:S(2)}) %collective-permute-start.4) | collective-permute-done | bytes 102432 | tf_op jit(solution)/shard_map/ppermute | solution.py:643
  30.6 0.0 collective-permute-done.2.m1_ref
  30.6 1.1 %half_setup.1 = (f32[70,8,640]{2,1,0:T(8,128)S(1)}, f32[70,8,640]{2,1,0:T(8,128)S(1)}, f32[70,8,640]{2,1,0:T(8,128)S(1)}) custom-call(s32[1]{0:T(128)} %bitcast.f_ref.refs_0_, f32[1024,512]{1,0:T(8,128)S(1)} %get-tuple-element.25.p_ref.refs_1_, f32[1024,512]{1,0:T(8,128)S(1)} %copy-done, f32[40,1024]{1,0:T(8,128)S(1)} %collective-permute-done.right_ref, ...), custom_call_target="tpu_custom_call" | custom-call | flops 2000000000 | tf_op jit(solution)/shard_map/half_setup/pallas_call | solution.py:53
  31.7 0.0 collective-permute-done.5.rp1_ref
  31.7 3.9 %velocity_begun.1 = (f32[72,8,640]{2,1,0:T(8,128)S(1)}, f32[72,8,640]{2,1,0:T(8,128)S(1)}) custom-call(f32[70,8,640]{2,1,0:T(8,128)S(1)} %get-tuple-element.31.t_ref, f32[54,8,512]{2,1,0:T(8,128)S(1)} %collective-permute-done.5.rp1_ref, f32[70,8,640]{2,1,0:T(8,128)S(1)} %get-tuple-element.32.q_ref, f32[70,8,640]{2,1,0:T(8,128)S(1)} %get-tuple-element.33.rec_ref), custom_call_target="tpu_custom_call" | custom-call | flops 4000000000 | tf_op jit(solution)/shard_map/velocity_begun/pallas_call | solution.py:53
  35.6 0.9 %collective-permute-done.6.rp2_ref = f32[16,8,512]{2,1,0:T(8,128)S(1)} collective-permute-done((f32[16,8,512]{2,1,0:T(8,128)S(1)}, f32[16,8,512]{2,1,0:T(8,128)S(1)}, u32[]{:S(2)}, u32[]{:S(2)}) %collective-permute-start.6) | collective-permute-done | bytes 262176 | tf_op jit(solution)/shard_map/ppermute | solution.py:651
  36.5 3.9 %velocity_ended.1 = (f32[70,8,640]{2,1,0:T(8,128)}, f32[208,512]{1,0:T(8,128)S(1)}, f32[104,512]{1,0:T(8,128)S(1)}, f32[128,128]{1,0:T(8,128)}) custom-call(s32[1]{0:T(128)} %bitcast.f_ref.refs_0_, f32[70,8,640]{2,1,0:T(8,128)S(1)} %get-tuple-element.31.t_ref, f32[54,8,512]{2,1,0:T(8,128)S(1)} %collective-permute-done.5.rp1_ref, ...), custom_call_target="tpu_custom_call" | custom-call | flops 5000000000 | tf_op jit(solution)/shard_map/velocity_ended/pallas_call | solution.py:53
  40.4 1.1 %collective-permute-start.7 = (f32[208,512]{1,0:T(8,128)S(1)}, f32[208,512]{1,0:T(8,128)S(1)}, u32[]{:S(2)}, u32[]{:S(2)}) collective-permute-start(f32[208,512]{1,0:T(8,128)S(1)} %get-tuple-element.38), channel_id=1, source_target_pairs={{0,64},{64,0},{1,65},{65,1},{2,66},{66,2},{3,67},{67,3},{4,68},{68... | collective-permute-start | bytes 1277960 | tf_op jit(solution)/shard_map/ppermute | solution.py:686
  41.5 8.8 %all-to-all-start = ((f32[128,1,128]{2,1,0:T(1,128)}), f32[128,1,128]{2,1,0:T(1,128)S(1)}, u32[]{:S(2)}, u32[]{:S(2)}) async-start(f32[128,1,128]{2,1,0:T(1,128)} %bitcast.2), calls=%async_computation | async-start | bytes 131072 | tf_op jit(solution)/shard_map/all_to_all | solution.py:687
  50.2 1.5 %collective-permute-start.10 = (f32[104,512]{1,0:T(8,128)S(1)}, f32[104,512]{1,0:T(8,128)S(1)}, u32[]{:S(2)}, u32[]{:S(2)}) collective-permute-start(f32[104,512]{1,0:T(8,128)S(1)} %get-tuple-element.43), channel_id=1, source_target_pairs={{0,64},{64,0},{1,65},{65,1},{2,66},{66,2},{3,67},{67,3},{4,68},{68... | collective-permute-start | bytes 638984 | tf_op jit(solution)/shard_map/ppermute | solution.py:688
  51.7 0.0 collective-permute-done.7.early_ref
  51.7 3.2 %velocity_rows.1 = (f32[5,560,128]{2,1,0:T(8,128)}, f32[240,512]{1,0:T(8,128)}, f32[1024,512]{1,0:T(8,128)}) custom-call(s32[1]{0:T(128)} %bitcast.f_ref.refs_0_, f32[70,8,640]{2,1,0:T(8,128)} %get-tuple-element.37.vs_hbm, f32[208,512]{1,0:T(8,128)S(1)} %collective-permute-done.7.early_ref), custom_call_target="tpu_custom_call" | custom-call | flops 60000002048 | tf_op jit(solution)/shard_map/velocity_rows/pallas_call | solution.py:53
  54.9 0.3 collective-permute-start.9
  55.2 4.6 %all-to-all-done = f32[128,1,128]{2,1,0:T(1,128)S(1)} async-done(((f32[128,1,128]{2,1,0:T(1,128)}), f32[128,1,128]{2,1,0:T(1,128)S(1)}, u32[]{:S(2)}, u32[]{:S(2)}) %all-to-all-start) | async-done | bytes 65568 | tf_op jit(solution)/shard_map/all_to_all | solution.py:687
  59.9 8.5 %outer_part.1 = (f32[256,512]{1,0:T(8,128)S(1)}, f32[5,544,128]{2,1,0:T(8,128)S(1)}, f32[5,272,128]{2,1,0:T(8,128)S(1)}) custom-call(s32[1]{0:T(128)} %bitcast.f_ref.refs_0_, f32[128,128]{1,0:T(8,128)S(1)} %bitcast.5, f32[1024,512]{1,0:T(8,128)} %ls_hbm.1, f32[40,1024]{1,0:T(8,128)S(1)} %collective-permute-done.right_ref, ...), custom_call_target="tpu_custom_call" | custom-call | flops 8000000000 | tf_op jit(solution)/shard_map/outer_part/pallas_call | solution.py:53
  68.4 0.4 collective-permute-start.8
  68.8 0.0 collective-permute-done.10.near_ref
  68.8 14.2 %middle_part.1 = (f32[1024,512]{1,0:T(8,128)}, f32[1024,512]{1,0:T(8,128)}) custom-call(s32[1]{0:T(128)} %bitcast.f_ref.refs_0_, f32[128,128]{1,0:T(8,128)S(1)} %bitcast.6, f32[5,272,128]{2,1,0:T(8,128)S(1)} %get-tuple-element.42.vm_ref, f32[208,512]{1,0:T(8,128)S(1)} %collective-permute-done.7.early_ref, ...), custom_call_target="tpu_custom_call", output_to_operand_aliasing={{1}: (7, {})} | custom-call | flops 20000000000 | tf_op jit(solution)/shard_map/middle_part/pallas_call | solution.py:53
  83.0 0.0 collective-permute-done.9.far_ref
  83.0 0.0 collective-permute-done.8.theirs_ref
  83.0 1.0 %insert.1 = (f32[1024,512]{1,0:T(8,128)}, f32[1024,512]{1,0:T(8,128)}) custom-call(s32[1]{0:T(128)} %bitcast.f_ref.refs_0_, f32[256,512]{1,0:T(8,128)S(1)} %collective-permute-done.8.theirs_ref, f32[240,512]{1,0:T(8,128)S(1)} %collective-permute-done.9.far_ref, f32[1024,512]{1,0:T(8,128)} %get-tuple-element.46._, ...), custom_call_target="tpu_custom_call", output_to_operand_aliasing={{0}: (3, {}), {1}: (4, {})} | custom-call | flops 1000000000 | tf_op jit(solution)/shard_map/insert/pallas_call | solution.py:53
Async XLA Ops:
  0.6 4.0 %copy-start = (f32[1024,512]{1,0:T(8,128)S(1)}, f32[1024,512]{1,0:T(8,128)}, u32[]{:S(2)}) copy-start(f32[1024,512]{1,0:T(8,128)} %ls_hbm.1) | copy-start | bytes 6291460
  2.5 29.2 %collective-permute-start.5 = (f32[54,8,512]{2,1,0:T(8,128)S(1)}, f32[54,8,512]{2,1,0:T(8,128)S(1)}, u32[]{:S(2)}, u32[]{:S(2)}) collective-permute-start(f32[54,8,512]{2,1,0:T(8,128)S(1)} %send_part.1), channel_id=1, source_target_pairs={{0,64},{64,0},{1,65},{65,1},{2,66},{66,2},{3,67},{67,3},{4,68},{68... | collective-permute-start | bytes 2654216 | tf_op jit(solution)/shard_map/ppermute | solution.py:614
  7.1 8.8 %collective-permute-start = (f32[40,1024]{1,0:T(8,128)S(1)}, f32[40,1024]{1,0:T(8,128)S(1)}, u32[]{:S(2)}, u32[]{:S(2)}) collective-permute-start(f32[40,1024]{1,0:T(8,128)S(1)} %get-tuple-element.26), channel_id=1, source_target_pairs={{0,15},{1,0},{2,1},{3,2},{4,3},{5,4},{6,5},{7,6},{8,7},{9,8},{10,9... | collective-permute-start | bytes 491528 | tf_op jit(solution)/shard_map/ppermute | solution.py:625
  13.4 7.5 %collective-permute-start.1 = (f32[40,1024]{1,0:T(8,128)S(1)}, f32[40,1024]{1,0:T(8,128)S(1)}, u32[]{:S(2)}, u32[]{:S(2)}) collective-permute-start(f32[40,1024]{1,0:T(8,128)S(1)} %get-tuple-element.27), channel_id=1, source_target_pairs={{0,1},{1,2},{2,3},{3,4},{4,5},{5,6},{6,7},{7,8},{8,9},{9,10},{10,1... | collective-permute-start | bytes 491528 | tf_op jit(solution)/shard_map/ppermute | solution.py:626
  21.0 4.9 %collective-permute-start.3 = (f32[24,640]{1,0:T(8,128)S(1)}, f32[24,640]{1,0:T(8,128)S(1)}, u32[]{:S(2)}, u32[]{:S(2)}) collective-permute-start(f32[24,640]{1,0:T(8,128)S(1)} %get-tuple-element.29), channel_id=1, source_target_pairs={{0,112},{16,64},{32,80},{48,96},{64,16},{80,32},{96,48},{112,0},{1... | collective-permute-start | bytes 184328 | tf_op jit(solution)/shard_map/ppermute | solution.py:642
  23.8 6.8 %collective-permute-start.2 = (f32[48,640]{1,0:T(8,128)S(1)}, f32[48,640]{1,0:T(8,128)S(1)}, u32[]{:S(2)}, u32[]{:S(2)}) collective-permute-start(f32[48,640]{1,0:T(8,128)S(1)} %get-tuple-element.28), channel_id=1, source_target_pairs={{0,16},{16,32},{32,48},{48,0},{64,112},{80,64},{96,80},{112,96},{1... | collective-permute-start | bytes 368648 | tf_op jit(solution)/shard_map/ppermute | solution.py:641
  26.0 4.6 %collective-permute-start.4 = (f32[40,640]{1,0:T(8,128)S(1)}, f32[40,640]{1,0:T(8,128)S(1)}, u32[]{:S(2)}, u32[]{:S(2)}) collective-permute-start(f32[40,640]{1,0:T(8,128)S(1)} %get-tuple-element.30), channel_id=1, source_target_pairs={{0,64},{64,0},{1,65},{65,1},{2,66},{66,2},{3,67},{67,3},{4,68},{68... | collective-permute-start | bytes 307208 | tf_op jit(solution)/shard_map/ppermute | solution.py:643
  26.1 10.4 %collective-permute-start.6 = (f32[16,8,512]{2,1,0:T(8,128)S(1)}, f32[16,8,512]{2,1,0:T(8,128)S(1)}, u32[]{:S(2)}, u32[]{:S(2)}) collective-permute-start(f32[16,8,512]{2,1,0:T(8,128)S(1)} %send_rest.1), channel_id=1, source_target_pairs={{0,64},{64,0},{1,65},{65,1},{2,66},{66,2},{3,67},{67,3},{4,68},{68... | collective-permute-start | bytes 786440 | tf_op jit(solution)/shard_map/ppermute | solution.py:651
  40.4 11.3 %collective-permute-start.7 = (f32[208,512]{1,0:T(8,128)S(1)}, f32[208,512]{1,0:T(8,128)S(1)}, u32[]{:S(2)}, u32[]{:S(2)}) collective-permute-start(f32[208,512]{1,0:T(8,128)S(1)} %get-tuple-element.38), channel_id=1, source_target_pairs={{0,64},{64,0},{1,65},{65,1},{2,66},{66,2},{3,67},{67,3},{4,68},{68... | collective-permute-start | bytes 1277960 | tf_op jit(solution)/shard_map/ppermute | solution.py:686
  41.5 18.4 %all-to-all-start = ((f32[128,1,128]{2,1,0:T(1,128)}), f32[128,1,128]{2,1,0:T(1,128)S(1)}, u32[]{:S(2)}, u32[]{:S(2)}) async-start(f32[128,1,128]{2,1,0:T(1,128)} %bitcast.2), calls=%async_computation | async-start | bytes 131072 | tf_op jit(solution)/shard_map/all_to_all | solution.py:687
  50.2 18.6 %collective-permute-start.10 = (f32[104,512]{1,0:T(8,128)S(1)}, f32[104,512]{1,0:T(8,128)S(1)}, u32[]{:S(2)}, u32[]{:S(2)}) collective-permute-start(f32[104,512]{1,0:T(8,128)S(1)} %get-tuple-element.43), channel_id=1, source_target_pairs={{0,64},{64,0},{1,65},{65,1},{2,66},{66,2},{3,67},{67,3},{4,68},{68... | collective-permute-start | bytes 638984 | tf_op jit(solution)/shard_map/ppermute | solution.py:688
  54.9 28.1 %collective-permute-start.9 = (f32[240,512]{1,0:T(8,128)}, f32[240,512]{1,0:T(8,128)S(1)}, u32[]{:S(2)}, u32[]{:S(2)}) collective-permute-start(f32[240,512]{1,0:T(8,128)} %get-tuple-element.41), channel_id=1, source_target_pairs={{0,64},{64,0},{1,65},{65,1},{2,66},{66,2},{3,67},{67,3},{4,68},{68... | collective-permute-start | bytes 1474568 | tf_op jit(solution)/shard_map/ppermute | solution.py:698
  68.4 14.6 %collective-permute-start.8 = (f32[256,512]{1,0:T(8,128)S(1)}, f32[256,512]{1,0:T(8,128)S(1)}, u32[]{:S(2)}, u32[]{:S(2)}) collective-permute-start(f32[256,512]{1,0:T(8,128)S(1)} %get-tuple-element.40.mine_ref), channel_id=1, source_target_pairs={{0,64},{64,0},{1,65},{65,1},{2,66},{66,2},{3,67},{67,3},{4,68},{68... | collective-permute-start | bytes 1572872 | tf_op jit(solution)/shard_map/ppermute | solution.py:718

commit v5 on v4

--- a/solution.py
+++ b/solution.py
@@ -13,9 +13,10 @@
 
 HALO = 24
 SIDE = 20
+SPARE = 4
 EDGE = 12
 STAGED = 16
-OWN_PARTS = (1, 4)
+OWN_PARTS = (33, 128)
 FIRST_PARTS = (27, 35)
 EARLY = 208
 LANES = 128
@@ -65,6 +66,15 @@
     return slice(c * LANES, (c + 1) * LANES)
 
 
+def shares(count, parts):
+    ends = [count * i // parts for i in range(parts + 1)]
+    return [(a, b - a) for a, b in zip(ends, ends[1:])]
+
+
+def swept(ext):
+    return (ext - 2 * SPARE) // 8
+
+
 def blank(nat, f, main):
     for c in range(nat.shape[0]):
         nat[c, pl.ds(aligned(f * main), HALO), :] = jnp.zeros((HALO, LANES), jnp.float32)
@@ -94,17 +104,17 @@
         part = w_ref[0] * buf[0, at : at + rows, :] + w_ref[1] * buf[1, at : at + rows, :]
         put(nat, pl.ds(aligned(f * HALO + at), rows), part)
     for k in range(n):
-        send_ref[k] = spread(nat, nat.shape[1] // 8, k, cols)
+        send_ref[k] = spread(nat, swept(nat.shape[1]), SPARE + k, cols)
 
 
 def send_rest(main, f_ref, p_ref, _, send_ref, nat):
     rows, cols = p_ref.shape
     f = f_ref[0]
-    r = nat.shape[1] // 8
+    r = swept(nat.shape[1])
     blank(nat, 1 - f, main)
     put(nat, pl.ds(aligned(f * HALO), main), p_ref[pl.ds(aligned((1 - f) * (rows - main)), main), :])
     for k in range(send_ref.shape[0]):
-        send_ref[k] = spread(nat, r, r - send_ref.shape[0] + k, cols)
+        send_ref[k] = spread(nat, r, SPARE + r - send_ref.shape[0] + k, cols)
 
 
 def strips(w_hbm, g_ref, ls_ref, p_ref, left_ref, right_ref, buf, w_ref, sems):
@@ -219,14 +229,14 @@
         nat[last, to, :] = pcol[side, :]
         lsx[last, to, :] = lscol[side, :]
 
-    r = ext // 8
+    r = swept(ext)
     for k in range(r):
-        x = spread(lsx, r, k, cols + LANES) * (1.0 / band_cells)
+        x = spread(lsx, r, SPARE + k, cols + LANES) * (1.0 / band_cells)
         u = x * x
         q = 1.0 / (5.0 + 4.0 * u)
         q_ref[k] = q
         rec_ref[k] = (1.0 + u) * q
-        t_ref[k] = spread(nat, r, k, cols + LANES)
+        t_ref[k] = spread(nat, r, SPARE + k, cols + LANES)
 
 
 def wrap(ref, r):
@@ -275,14 +285,14 @@
     f_ref, t_ref, rp1_ref, rp2_ref, q_ref, rec_ref, b0_ref, b1_ref, vs_hbm, early_ref, near_ref, top_ref,
     nat, a_ref, v0, v1, vs_ref, sems,
 ):
-    n, _, cols = rp1_ref.shape
+    begun, _, cols = rp1_ref.shape
     r, _, width = t_ref.shape
-    ext = 8 * r
-    f = f_ref[0]
-    group = r // sems.shape[0]
+    ext = nat.shape[1]
+    f = f_ref[0]
+    groups = shares(r, sems.shape[0])
     copies = [
-        pltpu.make_async_copy(vs_ref.at[pl.ds(i * group, group)], vs_hbm.at[pl.ds(i * group, group)], sems.at[i])
-        for i in range(sems.shape[0])
+        pltpu.make_async_copy(vs_ref.at[pl.ds(at, n)], vs_hbm.at[pl.ds(at, n)], sems.at[i])
+        for i, (at, n) in enumerate(groups)
     ]
     sub = lax.broadcasted_iota(jnp.int32, (8, cols), 0)
     tops = [jnp.zeros((8, cols), jnp.float32)] * 2
@@ -290,28 +300,28 @@
 
     def final(k, value):
         vs_ref[k] = value
-        unspread(nat, r, k, value)
+        unspread(nat, r, SPARE + k, value)
         done.add(k)
-        i = k // group
-        if all(i * group + j in done for j in range(group)):
-            copies[i].start()
+        for i, (at, n) in enumerate(groups):
+            if at <= k < at + n and all(j in done for j in range(at, at + n)):
+                copies[i].start()
         size = jnp.abs(value[:, 0:cols])
-        row = sub * r + k
-        if k < HALO or 7 * r + k >= ext - HALO:
+        row = sub * r + (SPARE + k)
+        if SPARE + k < HALO or SPARE + 7 * r + k >= ext - HALO:
             size = jnp.where((row >= HALO) & (row < ext - HALO), size, 0.0)
         tops[k % 2] = jnp.maximum(tops[k % 2], size)
 
     edge = EXT_SWEEPS + 1
-    for k in (*range(edge), *range(n - edge, n)):
+    for k in (*range(edge), *range(begun - edge, begun)):
         v0[k + 1] = b0_ref[k + 1]
         v1[k + 1] = b1_ref[k + 1]
-    for k in (*range(EXT_SWEEPS), *range(n - EXT_SWEEPS, r)):
-        source = add_part(t_ref[k], rp1_ref[k] if k < n else rp2_ref[k - n])
+    for k in (*range(EXT_SWEEPS), *range(begun - EXT_SWEEPS, r)):
+        source = add_part(t_ref[k], rp1_ref[k] if k < begun else rp2_ref[k - begun])
         a_ref[k] = source * q_ref[k]
-        if k >= n:
+        if k >= begun:
             v0[k + 1] = source
     assert EXT_SWEEPS % 2 == 0
-    for k in range(EXT_SWEEPS, n - EXT_SWEEPS):
+    for k in range(EXT_SWEEPS, begun - EXT_SWEEPS):
         final(k, b0_ref[k + 1])
     wrap(v0, r)
     relax = relaxed(a_ref, rec_ref, width)
@@ -325,7 +335,7 @@
             else:
                 dst[k + 1] = value
 
-        sweep(src, r, body, n - level)
+        sweep(src, r, body, begun - level)
         sweep(src, level, body)
         if level < EXT_SWEEPS:
             wrap(dst, r)
@@ -349,9 +359,7 @@
 def velocity_rows(f_ref, vs_hbm, early_ref, vx_hbm, far_hbm, vel_hbm, vs_ref, nat, sems):
     slabs, ext, _ = nat.shape
     last = slabs - 1
-    r = ext // 8
-    parts = 2
-    group = r // parts
+    r = vs_ref.shape[0]
     used = iter(range(sems.shape[0]))
 
     def begin(src, dst):
@@ -359,13 +367,12 @@
         copy.start()
         return copy
 
-    loads = [
-        begin(vs_hbm.at[pl.ds(i * group, group)], vs_ref.at[pl.ds(i * group, group)]) for i in range(parts)
-    ]
-    for k in range(r):
-        if k % group == 0:
-            loads[k // group].wait()
-        unspread(nat, r, k, vs_ref[k])
+    groups = shares(r, 3)
+    loads = [begin(vs_hbm.at[pl.ds(at, n)], vs_ref.at[pl.ds(at, n)]) for at, n in groups]
+    for load, (at, n) in zip(loads, groups):
+        load.wait()
+        for k in range(at, at + n):
+            unspread(nat, r, SPARE + k, vs_ref[k])
     far = far_hbm.shape[0]
     half = ext - 2 * HALO
     f = f_ref[0]
@@ -513,8 +520,8 @@
 
 
 def middle_part(
-    f_ref, top_ref, vm_ref, early_ref, near_ref, lsn, mine_ref, _, level_ref, vel_ref,
-    nat, vn, p0, p1, h_ref, s_ref, sems,
+    f_ref, top_ref, vm_ref, early_ref, near_ref, lsn, mine_ref, _, level_ref, nat, vel_ref,
+    vn, p0, p1, h_ref, s_ref, sems,
 ):
     rows, cols = level_ref.shape
     f = f_ref[0]
@@ -560,24 +567,30 @@
                 vn[last, first - low : at + LANES - low, :] = block[first - at :, :]
 
     reinit(top_ref, lsn, vn, STAGED - EDGE, r, nat, STAGED - EDGE, p0, p1, h_ref, s_ref, cols + LANES)
-    for c in range(last):
-        ready.append(
-            begin(nat.at[c, pl.ds(STAGED, n), :], level_ref.at[pl.ds(low + STAGED, n), pl.ds(c * LANES, LANES)])
-        )
     for copy in ready:
         copy.wait()
 
 
-def insert(f_ref, theirs_ref, far_ref, _, __, level_ref, vel_ref, sems):
+def insert(f_ref, theirs_ref, far_ref, middle_ref, _, __, level_ref, vel_ref, sems):
     rows = level_ref.shape[0]
     n, far = theirs_ref.shape[0], far_ref.shape[0]
-    f = f_ref[0]
+    slabs = middle_ref.shape[0]
+    f = f_ref[0]
+    mid = rows - 2 * n
     copies = [
         pltpu.make_async_copy(
-            theirs_ref, level_ref.at[pl.ds(aligned((1 - f) * (rows - n)), n), :], sems.at[0]
+            middle_ref.at[c, pl.ds(STAGED, mid), :],
+            level_ref.at[pl.ds(n, mid), pl.ds(c * LANES, LANES)],
+            sems.at[c],
+        )
+        for c in range(slabs)
+    ]
+    copies += [
+        pltpu.make_async_copy(
+            theirs_ref, level_ref.at[pl.ds(aligned((1 - f) * (rows - n)), n), :], sems.at[slabs]
         ),
         pltpu.make_async_copy(
-            far_ref, vel_ref.at[pl.ds(aligned((1 - f) * (rows - far)), far), :], sems.at[1]
+            far_ref, vel_ref.at[pl.ds(aligned((1 - f) * (rows - far)), far), :], sems.at[slabs + 1]
         ),
     ]
     for copy in copies:
@@ -600,7 +613,7 @@
     swap = [(0, 1), (1, 0)]
     main, ext, wide = half + HALO, half + 2 * HALO, cols + LANES
     slabs = wide // LANES
-    r = ext // 8
+    r = swept(ext)
     part = r * FIRST_PARTS[0] // FIRST_PARTS[1]
     weights = pltpu.SMEM(focus_weight.shape, jnp.float32)
 
@@ -676,7 +689,7 @@
         [SMEM] + [VMEM] * 7,
         [
             vmem(slabs, ext, LANES), vmem(r, 8, wide), vmem(r + 2, 8, wide), vmem(r + 2, 8, wide),
-            vmem(r, 8, wide), DMA((7,)),
+            vmem(r, 8, wide), DMA((8,)),
         ],
         "velocity_ended",
         us=5,
@@ -690,7 +703,7 @@
         velocity_rows,
         [(slabs, ext, LANES), (far, cols), (rows, cols)],
         [SMEM, HBM, VMEM],
-        [vmem(r, 8, wide), vmem(slabs, ext, LANES), DMA((2 * slabs + 2,))],
+        [vmem(r, 8, wide), vmem(slabs, ext, LANES), DMA((2 * slabs + 3,))],
         "velocity_rows",
         us=60,
         out_specs=[HBM, HBM, HBM],
@@ -716,28 +729,26 @@
         us=8,
     )(f, tops, level_set, from_right, from_left, got1, vx)
     theirs = lax.ppermute(mine, "focus", swap)
-    level, velocity = call(
+    level, middle_rows, velocity = call(
         middle_part,
-        [(rows, cols), (rows, cols)],
+        [(rows, cols), (slabs - 1, middle, LANES), (rows, cols)],
         [SMEM] + [VMEM] * 6 + [HBM],
-        [vmem(slabs - 1, middle, LANES), vmem(slabs, middle, LANES)]
-        + work(mid)
-        + [DMA((slabs + 1,))],
+        [vmem(slabs, middle, LANES)] + work(mid) + [DMA((2,))],
         "middle_part",
         us=20,
-        out_specs=[HBM, HBM],
-        aliases={7: 1},
+        out_specs=[HBM, VMEM, HBM],
+        aliases={7: 2},
         mib=20,
     )(f, tops, v_mid, got_early, got_near, ls_mid, mine, velocity)
     level, velocity = call(
         insert,
         [(rows, cols), (rows, cols)],
-        [SMEM, VMEM, VMEM, HBM, HBM],
-        [DMA((2,))],
+        [SMEM, VMEM, VMEM, VMEM, HBM, HBM],
+        [DMA((slabs + 1,))],
         "insert",
         out_specs=[HBM, HBM],
-        aliases={3: 0, 4: 1},
-    )(f, theirs, got_far, level, velocity)
+        aliases={4: 0, 5: 1},
+    )(f, theirs, got_far, middle_rows, level, velocity)
     return level, velocity
 
 

time: 84.4 us -> 83.4 us (0.988)
  Pallas kernels: 40.4 us -> 39.5 us
    pallas_call x11, Pallas kernels: 40.4 us -> 39.5 us  [run(): kernel(*(pltpu.with_memory_space_constraint(x, pltpu.HBM) if spec is HBM...]
  transfers between devices with their start and end apart: 12 -> 12, of which waited for: 5 -> 6; matrix products, arithmetic and copies ran while one was open for 0% -> 0% of each run, Pallas kernels for 40% -> 39%
where the time goes in v5:
time: 83.4 us; the launch traced here: 83.2 us
  Pallas kernels  39.5 us (47%)
  starting transfers between devices  26.9 us (32%)
  waiting for transfers between devices  15.8 us (19%)
  between operations  0.91 us (1%)
    pallas_call x11, Pallas kernels, run(): kernel(*(pltpu.with_memory_space_constraint(x, pltpu.HBM) if spec is HBM...  39.5 us
    all_to_all x1, starting transfers between devices, per_device(): tops = lax.all_to_all(top, ('focus', 'gx', 'gy'), 0, 0)  8.41 us
    ppermute x1, starting transfers between devices, per_device(): from_right = lax.ppermute(left, 'gy', shifted(gy, -1))  6.28 us
    ppermute x1, waiting for transfers between devices, per_device(): from_left = lax.ppermute(right, 'gy', shifted(gy, 1))  4.94 us
    all_to_all x1, waiting for transfers between devices, per_device(): tops = lax.all_to_all(top, ('focus', 'gx', 'gy'), 0, 0)  4.28 us
    ppermute x1, waiting for transfers between devices, per_device(): got_fs = lax.ppermute(fs, 'focus', swap)  2.92 us
    ppermute x1, starting transfers between devices, per_device(): got2 = lax.ppermute(m2, ('focus', 'gx'), cross)  2.71 us
    ppermute x1, waiting for transfers between devices, per_device(): from_right = lax.ppermute(left, 'gy', shifted(gy, -1))  2.55 us
  transfers between devices with their start and end apart: 12, of which 6 were waited for; matrix products, arithmetic and copies ran while one was open for 0% of the time, Pallas kernels for 39%

profile of v5, /device:TPU:1, one launch (start us, length us, event | category | flops | bytes accessed | tf_op | source)
XLA Modules:
  0.0 83.2 jit_solution(17497136432632567567)
XLA Ops:
  0.6 0.0 copy-start
  0.6 1.9 %send_part.1 = f32[53,8,512]{2,1,0:T(8,128)S(1)} custom-call(s32[1]{0:T(128)} %bitcast.f_ref.refs_0_, f32[2]{0:T(128)} %w_hbm.3, f32[2,1024,512]{2,1,0:T(8,128)} %g_ref.3), custom_call_target="tpu_custom_call" | custom-call | flops 1000000000 | tf_op jit(solution)/shard_map/send_part/pallas_call | solution.py:54
  2.5 2.1 %collective-permute-start.5 = (f32[53,8,512]{2,1,0:T(8,128)S(1)}, f32[53,8,512]{2,1,0:T(8,128)S(1)}, u32[]{:S(2)}, u32[]{:S(2)}) collective-permute-start(f32[53,8,512]{2,1,0:T(8,128)S(1)} %send_part.1), channel_id=1, source_target_pairs={{0,64},{64,0},{1,65},{65,1},{2,66},{66,2},{3,67},{67,3},{4,68},{68... | collective-permute-start | bytes 2605064 | tf_op jit(solution)/shard_map/ppermute | solution.py:627
  4.6 0.0 copy-done
  4.6 2.5 %strips.1 = (f32[1024,512]{1,0:T(8,128)S(1)}, f32[40,1024]{1,0:T(8,128)S(1)}, f32[40,1024]{1,0:T(8,128)S(1)}) custom-call(f32[2]{0:T(128)} %w_hbm.3, f32[2,1024,512]{2,1,0:T(8,128)} %g_ref.3, f32[1024,512]{1,0:T(8,128)S(1)} %copy-done), custom_call_target="tpu_custom_call" | custom-call | flops 2000000000 | tf_op jit(solution)/shard_map/strips/pallas_call | solution.py:54
  7.1 6.3 %collective-permute-start = (f32[40,1024]{1,0:T(8,128)S(1)}, f32[40,1024]{1,0:T(8,128)S(1)}, u32[]{:S(2)}, u32[]{:S(2)}) collective-permute-start(f32[40,1024]{1,0:T(8,128)S(1)} %get-tuple-element.27), channel_id=1, source_target_pairs={{0,15},{1,0},{2,1},{3,2},{4,3},{5,4},{6,5},{7,6},{8,7},{9,8},{10,9... | collective-permute-start | bytes 491528 | tf_op jit(solution)/shard_map/ppermute | solution.py:638
  13.4 0.0 collective-permute-start.1
  13.4 2.5 %collective-permute-done.right_ref = f32[40,1024]{1,0:T(8,128)S(1)} collective-permute-done((f32[40,1024]{1,0:T(8,128)S(1)}, f32[40,1024]{1,0:T(8,128)S(1)}, u32[]{:S(2)}, u32[]{:S(2)}) %collective-permute-start) | collective-permute-done | bytes 163872 | tf_op jit(solution)/shard_map/ppermute | solution.py:638
  16.0 4.9 %collective-permute-done.1.left_ref = f32[40,1024]{1,0:T(8,128)S(1)} collective-permute-done((f32[40,1024]{1,0:T(8,128)S(1)}, f32[40,1024]{1,0:T(8,128)S(1)}, u32[]{:S(2)}, u32[]{:S(2)}) %collective-permute-start.1) | collective-permute-done | bytes 163872 | tf_op jit(solution)/shard_map/ppermute | solution.py:639
  20.9 0.1 row_messages.1
  21.0 2.7 %collective-permute-start.3 = (f32[24,640]{1,0:T(8,128)S(1)}, f32[24,640]{1,0:T(8,128)S(1)}, u32[]{:S(2)}, u32[]{:S(2)}) collective-permute-start(f32[24,640]{1,0:T(8,128)S(1)} %get-tuple-element.30), channel_id=1, source_target_pairs={{0,112},{16,64},{32,80},{48,96},{64,16},{80,32},{96,48},{112,0},{1... | collective-permute-start | bytes 184328 | tf_op jit(solution)/shard_map/ppermute | solution.py:655
  23.7 2.2 %collective-permute-start.2 = (f32[48,640]{1,0:T(8,128)S(1)}, f32[48,640]{1,0:T(8,128)S(1)}, u32[]{:S(2)}, u32[]{:S(2)}) collective-permute-start(f32[48,640]{1,0:T(8,128)S(1)} %get-tuple-element.29), channel_id=1, source_target_pairs={{0,16},{16,32},{32,48},{48,0},{64,112},{80,64},{96,80},{112,96},{1... | collective-permute-start | bytes 368648 | tf_op jit(solution)/shard_map/ppermute | solution.py:654
  26.0 0.0 collective-permute-start.4
  26.0 0.0 collective-permute-done.3.m2_ref.refs_2_
  26.0 0.1 send_rest.1
  26.1 1.6 %collective-permute-start.6 = (f32[16,8,512]{2,1,0:T(8,128)S(1)}, f32[16,8,512]{2,1,0:T(8,128)S(1)}, u32[]{:S(2)}, u32[]{:S(2)}) collective-permute-start(f32[16,8,512]{2,1,0:T(8,128)S(1)} %send_rest.1), channel_id=1, source_target_pairs={{0,64},{64,0},{1,65},{65,1},{2,66},{66,2},{3,67},{67,3},{4,68},{68... | collective-permute-start | bytes 786440 | tf_op jit(solution)/shard_map/ppermute | solution.py:664
  27.7 2.9 %collective-permute-done.4.fs_ref = f32[40,640]{1,0:T(8,128)S(1)} collective-permute-done((f32[40,640]{1,0:T(8,128)S(1)}, f32[40,640]{1,0:T(8,128)S(1)}, u32[]{:S(2)}, u32[]{:S(2)}) %collective-permute-start.4) | collective-permute-done | bytes 102432 | tf_op jit(solution)/shard_map/ppermute | solution.py:656
  30.6 0.0 collective-permute-done.2.m1_ref
  30.6 1.0 %half_setup.1 = (f32[69,8,640]{2,1,0:T(8,128)S(1)}, f32[69,8,640]{2,1,0:T(8,128)S(1)}, f32[69,8,640]{2,1,0:T(8,128)S(1)}) custom-call(s32[1]{0:T(128)} %bitcast.f_ref.refs_0_, f32[1024,512]{1,0:T(8,128)S(1)} %get-tuple-element.26.p_ref.refs_1_, f32[1024,512]{1,0:T(8,128)S(1)} %copy-done, f32[40,1024]{1,0:T(8,128)S(1)} %collective-permute-done.right_ref, ...), custom_call_target="tpu_custom_call" | custom-call | flops 2000000000 | tf_op jit(solution)/shard_map/half_setup/pallas_call | solution.py:54
  31.6 0.0 collective-permute-done.5.rp1_ref
  31.6 4.0 %velocity_begun.1 = (f32[71,8,640]{2,1,0:T(8,128)S(1)}, f32[71,8,640]{2,1,0:T(8,128)S(1)}) custom-call(f32[69,8,640]{2,1,0:T(8,128)S(1)} %get-tuple-element.32.t_ref, f32[53,8,512]{2,1,0:T(8,128)S(1)} %collective-permute-done.5.rp1_ref, f32[69,8,640]{2,1,0:T(8,128)S(1)} %get-tuple-element.33.q_ref, f32[69,8,640]{2,1,0:T(8,128)S(1)} %get-tuple-element.34.rec_ref), custom_call_target="tpu_custom_call" | custom-call | flops 4000000000 | tf_op jit(solution)/shard_map/velocity_begun/pallas_call | solution.py:54
  35.6 0.9 %collective-permute-done.6.rp2_ref = f32[16,8,512]{2,1,0:T(8,128)S(1)} collective-permute-done((f32[16,8,512]{2,1,0:T(8,128)S(1)}, f32[16,8,512]{2,1,0:T(8,128)S(1)}, u32[]{:S(2)}, u32[]{:S(2)}) %collective-permute-start.6) | collective-permute-done | bytes 262176 | tf_op jit(solution)/shard_map/ppermute | solution.py:664
  36.5 3.8 %velocity_ended.1 = (f32[69,8,640]{2,1,0:T(8,128)}, f32[208,512]{1,0:T(8,128)S(1)}, f32[96,512]{1,0:T(8,128)S(1)}, f32[128,128]{1,0:T(8,128)}) custom-call(s32[1]{0:T(128)} %bitcast.f_ref.refs_0_, f32[69,8,640]{2,1,0:T(8,128)S(1)} %get-tuple-element.32.t_ref, f32[53,8,512]{2,1,0:T(8,128)S(1)} %collective-permute-done.5.rp1_ref, ...), custom_call_target="tpu_custom_call" | custom-call | flops 5000000000 | tf_op jit(solution)/shard_map/velocity_ended/pallas_call | solution.py:54
  40.3 1.1 %collective-permute-start.7 = (f32[208,512]{1,0:T(8,128)S(1)}, f32[208,512]{1,0:T(8,128)S(1)}, u32[]{:S(2)}, u32[]{:S(2)}) collective-permute-start(f32[208,512]{1,0:T(8,128)S(1)} %get-tuple-element.39), channel_id=1, source_target_pairs={{0,64},{64,0},{1,65},{65,1},{2,66},{66,2},{3,67},{67,3},{4,68},{68... | collective-permute-start | bytes 1277960 | tf_op jit(solution)/shard_map/ppermute | solution.py:699
  41.4 8.4 %all-to-all-start = ((f32[128,1,128]{2,1,0:T(1,128)}), f32[128,1,128]{2,1,0:T(1,128)S(1)}, u32[]{:S(2)}, u32[]{:S(2)}) async-start(f32[128,1,128]{2,1,0:T(1,128)} %bitcast.2), calls=%async_computation | async-start | bytes 131072 | tf_op jit(solution)/shard_map/all_to_all | solution.py:700
  49.8 1.5 %collective-permute-start.10 = (f32[96,512]{1,0:T(8,128)S(1)}, f32[96,512]{1,0:T(8,128)S(1)}, u32[]{:S(2)}, u32[]{:S(2)}) collective-permute-start(f32[96,512]{1,0:T(8,128)S(1)} %get-tuple-element.44), channel_id=1, source_target_pairs={{0,64},{64,0},{1,65},{65,1},{2,66},{66,2},{3,67},{67,3},{4,68},{68... | collective-permute-start | bytes 589832 | tf_op jit(solution)/shard_map/ppermute | solution.py:701
  51.3 0.0 collective-permute-done.7.early_ref
  51.3 3.2 %velocity_rows.1 = (f32[5,560,128]{2,1,0:T(8,128)}, f32[248,512]{1,0:T(8,128)}, f32[1024,512]{1,0:T(8,128)}) custom-call(s32[1]{0:T(128)} %bitcast.f_ref.refs_0_, f32[69,8,640]{2,1,0:T(8,128)} %get-tuple-element.38.vs_hbm, f32[208,512]{1,0:T(8,128)S(1)} %collective-permute-done.7.early_ref), custom_call_target="tpu_custom_call" | custom-call | flops 60000002048 | tf_op jit(solution)/shard_map/velocity_rows/pallas_call | solution.py:54
  54.5 0.7 collective-permute-start.9
  55.2 4.3 %all-to-all-done = f32[128,1,128]{2,1,0:T(1,128)S(1)} async-done(((f32[128,1,128]{2,1,0:T(1,128)}), f32[128,1,128]{2,1,0:T(1,128)S(1)}, u32[]{:S(2)}, u32[]{:S(2)}) %all-to-all-start) | async-done | bytes 65568 | tf_op jit(solution)/shard_map/all_to_all | solution.py:700
  59.5 8.7 %outer_part.1 = (f32[264,512]{1,0:T(8,128)S(1)}, f32[5,528,128]{2,1,0:T(8,128)S(1)}, f32[5,264,128]{2,1,0:T(8,128)S(1)}) custom-call(s32[1]{0:T(128)} %bitcast.f_ref.refs_0_, f32[128,128]{1,0:T(8,128)S(1)} %bitcast.5, f32[1024,512]{1,0:T(8,128)} %ls_hbm.1, f32[40,1024]{1,0:T(8,128)S(1)} %collective-permute-done.right_ref, ...), custom_call_target="tpu_custom_call" | custom-call | flops 8000000000 | tf_op jit(solution)/shard_map/outer_part/pallas_call | solution.py:54
  68.1 0.4 collective-permute-start.8
  68.5 0.0 collective-permute-done.10.near_ref
  68.5 12.9 %middle_part.1 = (f32[1024,512]{1,0:T(8,128)}, f32[4,528,128]{2,1,0:T(8,128)S(1)}, f32[1024,512]{1,0:T(8,128)}) custom-call(s32[1]{0:T(128)} %bitcast.f_ref.refs_0_, f32[128,128]{1,0:T(8,128)S(1)} %bitcast.6, f32[5,264,128]{2,1,0:T(8,128)S(1)} %get-tuple-element.43.vm_ref, ...), custom_call_target="tpu_custom_call", output_to_operand_aliasing={{2}: (7, {})} | custom-call | flops 20000000000 | tf_op jit(solution)/shard_map/middle_part/pallas_call | solution.py:54
  81.4 0.0 collective-permute-done.9.far_ref
  81.4 0.2 collective-permute-done.8.theirs_ref
  81.7 1.3 %insert.1 = (f32[1024,512]{1,0:T(8,128)}, f32[1024,512]{1,0:T(8,128)}) custom-call(s32[1]{0:T(128)} %bitcast.f_ref.refs_0_, f32[264,512]{1,0:T(8,128)S(1)} %collective-permute-done.8.theirs_ref, f32[248,512]{1,0:T(8,128)S(1)} %collective-permute-done.9.far_ref, ...), custom_call_target="tpu_custom_call", output_to_operand_aliasing={{0}: (4, {}), {1}: (5, {})} | custom-call | flops 1000000000 | tf_op jit(solution)/shard_map/insert/pallas_call | solution.py:54
Async XLA Ops:
  0.6 4.0 %copy-start = (f32[1024,512]{1,0:T(8,128)S(1)}, f32[1024,512]{1,0:T(8,128)}, u32[]{:S(2)}) copy-start(f32[1024,512]{1,0:T(8,128)} %ls_hbm.1) | copy-start | bytes 6291460
  2.5 29.1 %collective-permute-start.5 = (f32[53,8,512]{2,1,0:T(8,128)S(1)}, f32[53,8,512]{2,1,0:T(8,128)S(1)}, u32[]{:S(2)}, u32[]{:S(2)}) collective-permute-start(f32[53,8,512]{2,1,0:T(8,128)S(1)} %send_part.1), channel_id=1, source_target_pairs={{0,64},{64,0},{1,65},{65,1},{2,66},{66,2},{3,67},{67,3},{4,68},{68... | collective-permute-start | bytes 2605064 | tf_op jit(solution)/shard_map/ppermute | solution.py:627
  7.1 8.8 %collective-permute-start = (f32[40,1024]{1,0:T(8,128)S(1)}, f32[40,1024]{1,0:T(8,128)S(1)}, u32[]{:S(2)}, u32[]{:S(2)}) collective-permute-start(f32[40,1024]{1,0:T(8,128)S(1)} %get-tuple-element.27), channel_id=1, source_target_pairs={{0,15},{1,0},{2,1},{3,2},{4,3},{5,4},{6,5},{7,6},{8,7},{9,8},{10,9... | collective-permute-start | bytes 491528 | tf_op jit(solution)/shard_map/ppermute | solution.py:638
  13.4 7.5 %collective-permute-start.1 = (f32[40,1024]{1,0:T(8,128)S(1)}, f32[40,1024]{1,0:T(8,128)S(1)}, u32[]{:S(2)}, u32[]{:S(2)}) collective-permute-start(f32[40,1024]{1,0:T(8,128)S(1)} %get-tuple-element.28), channel_id=1, source_target_pairs={{0,1},{1,2},{2,3},{3,4},{4,5},{5,6},{6,7},{7,8},{8,9},{9,10},{10,1... | collective-permute-start | bytes 491528 | tf_op jit(solution)/shard_map/ppermute | solution.py:639
  21.0 4.9 %collective-permute-start.3 = (f32[24,640]{1,0:T(8,128)S(1)}, f32[24,640]{1,0:T(8,128)S(1)}, u32[]{:S(2)}, u32[]{:S(2)}) collective-permute-start(f32[24,640]{1,0:T(8,128)S(1)} %get-tuple-element.30), channel_id=1, source_target_pairs={{0,112},{16,64},{32,80},{48,96},{64,16},{80,32},{96,48},{112,0},{1... | collective-permute-start | bytes 184328 | tf_op jit(solution)/shard_map/ppermute | solution.py:655
  23.7 6.8 %collective-permute-start.2 = (f32[48,640]{1,0:T(8,128)S(1)}, f32[48,640]{1,0:T(8,128)S(1)}, u32[]{:S(2)}, u32[]{:S(2)}) collective-permute-start(f32[48,640]{1,0:T(8,128)S(1)} %get-tuple-element.29), channel_id=1, source_target_pairs={{0,16},{16,32},{32,48},{48,0},{64,112},{80,64},{96,80},{112,96},{1... | collective-permute-start | bytes 368648 | tf_op jit(solution)/shard_map/ppermute | solution.py:654
  26.0 4.6 %collective-permute-start.4 = (f32[40,640]{1,0:T(8,128)S(1)}, f32[40,640]{1,0:T(8,128)S(1)}, u32[]{:S(2)}, u32[]{:S(2)}) collective-permute-start(f32[40,640]{1,0:T(8,128)S(1)} %get-tuple-element.31), channel_id=1, source_target_pairs={{0,64},{64,0},{1,65},{65,1},{2,66},{66,2},{3,67},{67,3},{4,68},{68... | collective-permute-start | bytes 307208 | tf_op jit(solution)/shard_map/ppermute | solution.py:656
  26.1 10.4 %collective-permute-start.6 = (f32[16,8,512]{2,1,0:T(8,128)S(1)}, f32[16,8,512]{2,1,0:T(8,128)S(1)}, u32[]{:S(2)}, u32[]{:S(2)}) collective-permute-start(f32[16,8,512]{2,1,0:T(8,128)S(1)} %send_rest.1), channel_id=1, source_target_pairs={{0,64},{64,0},{1,65},{65,1},{2,66},{66,2},{3,67},{67,3},{4,68},{68... | collective-permute-start | bytes 786440 | tf_op jit(solution)/shard_map/ppermute | solution.py:664
  40.3 11.0 %collective-permute-start.7 = (f32[208,512]{1,0:T(8,128)S(1)}, f32[208,512]{1,0:T(8,128)S(1)}, u32[]{:S(2)}, u32[]{:S(2)}) collective-permute-start(f32[208,512]{1,0:T(8,128)S(1)} %get-tuple-element.39), channel_id=1, source_target_pairs={{0,64},{64,0},{1,65},{65,1},{2,66},{66,2},{3,67},{67,3},{4,68},{68... | collective-permute-start | bytes 1277960 | tf_op jit(solution)/shard_map/ppermute | solution.py:699
  41.4 18.1 %all-to-all-start = ((f32[128,1,128]{2,1,0:T(1,128)}), f32[128,1,128]{2,1,0:T(1,128)S(1)}, u32[]{:S(2)}, u32[]{:S(2)}) async-start(f32[128,1,128]{2,1,0:T(1,128)} %bitcast.2), calls=%async_computation | async-start | bytes 131072 | tf_op jit(solution)/shard_map/all_to_all | solution.py:700
  49.8 18.7 %collective-permute-start.10 = (f32[96,512]{1,0:T(8,128)S(1)}, f32[96,512]{1,0:T(8,128)S(1)}, u32[]{:S(2)}, u32[]{:S(2)}) collective-permute-start(f32[96,512]{1,0:T(8,128)S(1)} %get-tuple-element.44), channel_id=1, source_target_pairs={{0,64},{64,0},{1,65},{65,1},{2,66},{66,2},{3,67},{67,3},{4,68},{68... | collective-permute-start | bytes 589832 | tf_op jit(solution)/shard_map/ppermute | solution.py:701
  54.5 26.9 %collective-permute-start.9 = (f32[248,512]{1,0:T(8,128)}, f32[248,512]{1,0:T(8,128)S(1)}, u32[]{:S(2)}, u32[]{:S(2)}) collective-permute-start(f32[248,512]{1,0:T(8,128)} %get-tuple-element.42), channel_id=1, source_target_pairs={{0,64},{64,0},{1,65},{65,1},{2,66},{66,2},{3,67},{67,3},{4,68},{68... | collective-permute-start | bytes 1523720 | tf_op jit(solution)/shard_map/ppermute | solution.py:711
  68.1 13.5 %collective-permute-start.8 = (f32[264,512]{1,0:T(8,128)S(1)}, f32[264,512]{1,0:T(8,128)S(1)}, u32[]{:S(2)}, u32[]{:S(2)}) collective-permute-start(f32[264,512]{1,0:T(8,128)S(1)} %get-tuple-element.41.mine_ref), channel_id=1, source_target_pairs={{0,64},{64,0},{1,65},{65,1},{2,66},{66,2},{3,67},{67,3},{4,68},{68... | collective-permute-start | bytes 1622024 | tf_op jit(solution)/shard_map/ppermute | solution.py:731

commit v6 on v5

--- a/solution.py
+++ b/solution.py
@@ -16,8 +16,8 @@
 SPARE = 4
 EDGE = 12
 STAGED = 16
-OWN_PARTS = (33, 128)
-FIRST_PARTS = (27, 35)
+OWN_PARTS = (1, 4)
+FIRST_PARTS = (28, 35)
 EARLY = 208
 LANES = 128
 TINY = 1e-18
@@ -379,7 +379,7 @@
     at_far = pl.ds(aligned(HALO + f * (half - far)), far)
     lanes = [pl.ds(c * LANES, LANES) for c in range(last)]
     copies = [begin(nat.at[c, at_far, :], far_hbm.at[:, lanes[c]]) for c in range(last)]
-    copies.append(begin(nat, vx_hbm))
+    copies += [begin(nat.at[c], vx_hbm.at[c]) for c in range(slabs)]
     early = early_ref.shape[0]
     theirs = vel_hbm.at[pl.ds(aligned((1 - f) * half + f * (half - early)), early), :]
     copies.append(begin(early_ref, theirs))
@@ -478,20 +478,23 @@
         for c in range(last)
     ]
     from_ext = aligned(f * (vx_hbm.shape[1] - staged))
-    copies.append(pltpu.make_async_copy(vx_hbm.at[:, pl.ds(from_ext, staged), :], vn, sems.at[last]))
+    copies += [
+        pltpu.make_async_copy(vx_hbm.at[c, pl.ds(from_ext, staged), :], vn.at[c], sems.at[last + c])
+        for c in range(last + 1)
+    ]
     for copy in copies:
         copy.start()
     middle, cut = lsm_ref.shape[1], vm_ref.shape[1]
     low = (rows - middle) // 2
     later = [
         pltpu.make_async_copy(
-            ls_hbm.at[pl.ds(low, middle), pl.ds(c * LANES, LANES)], lsm_ref.at[c], sems.at[last + 1 + c]
+            ls_hbm.at[pl.ds(low, middle), pl.ds(c * LANES, LANES)], lsm_ref.at[c], sems.at[2 * last + 1 + c]
         )
         for c in range(last)
     ]
     later.append(
         pltpu.make_async_copy(
-            vx_hbm.at[:, pl.ds(aligned(HALO + (1 - f) * low), cut), :], vm_ref, sems.at[2 * last + 1]
+            vx_hbm.at[:, pl.ds(aligned(HALO + (1 - f) * low), cut), :], vm_ref, sems.at[3 * last + 1]
         )
     )
     put(lsn, pl.ds(aligned(f * inside), HALO), m1_ref[HALO:, :])
@@ -550,21 +553,20 @@
         vn[c, pl.ds(aligned(f * cut), cut), :] = vm_ref[c]
     put(vn, pl.ds(aligned((1 - f) * cut + f * near), early), early_ref[...])
     put(vn, pl.ds(aligned((1 - f) * (cut + early)), near), near_ref[0:near, :])
-    for i in range(half // LANES):
-        at = i * LANES
-        block = turned(near_ref[near : near + SIDE, at : at + LANES], near_ref[near + SIDE :, at : at + LANES])
-
-        @pl.when(f == 0)
-        def _():
+    def block(at):
+        return turned(near_ref[near : near + SIDE, at : at + LANES], near_ref[near + SIDE :, at : at + LANES])
+
+    @pl.when(f == 0)
+    def _():
+        for at in range(0, staged - cut, LANES):
             end = min(at + LANES, staged - cut)
-            if at < end:
-                vn[last, cut + at : cut + end, :] = block[0 : end - at, :]
-
-        @pl.when(f == 1)
-        def _():
+            vn[last, cut + at : cut + end, :] = block(at)[0 : end - at, :]
+
+    @pl.when(f == 1)
+    def _():
+        for at in range(low // LANES * LANES, half, LANES):
             first = max(at, low)
-            if first < at + LANES:
-                vn[last, first - low : at + LANES - low, :] = block[first - at :, :]
+            vn[last, first - low : at + LANES - low, :] = block(at)[first - at :, :]
 
     reinit(top_ref, lsn, vn, STAGED - EDGE, r, nat, STAGED - EDGE, p0, p1, h_ref, s_ref, cols + LANES)
     for copy in ready:
@@ -585,14 +587,15 @@
         )
         for c in range(slabs)
     ]
-    copies += [
-        pltpu.make_async_copy(
-            theirs_ref, level_ref.at[pl.ds(aligned((1 - f) * (rows - n)), n), :], sems.at[slabs]
-        ),
-        pltpu.make_async_copy(
-            far_ref, vel_ref.at[pl.ds(aligned((1 - f) * (rows - far)), far), :], sems.at[slabs + 1]
-        ),
-    ]
+    pieces = [(theirs_ref, level_ref, at, count) for at, count in shares(n // 8, slabs)]
+    pieces += [(far_ref, vel_ref, at, count) for at, count in shares(far // 8, slabs)]
+    for i, (src, dst, at, count) in enumerate(pieces):
+        first = aligned((1 - f) * (rows - src.shape[0]) + at * 8)
+        copies.append(
+            pltpu.make_async_copy(
+                src.at[pl.ds(at * 8, count * 8), :], dst.at[pl.ds(first, count * 8), :], sems.at[slabs + i]
+            )
+        )
     for copy in copies:
         copy.start()
     for copy in copies:
@@ -703,7 +706,7 @@
         velocity_rows,
         [(slabs, ext, LANES), (far, cols), (rows, cols)],
         [SMEM, HBM, VMEM],
-        [vmem(r, 8, wide), vmem(slabs, ext, LANES), DMA((2 * slabs + 3,))],
+        [vmem(r, 8, wide), vmem(slabs, ext, LANES), DMA((3 * slabs + 3,))],
         "velocity_rows",
         us=60,
         out_specs=[HBM, HBM, HBM],
@@ -724,7 +727,7 @@
         [vmem(slabs - 1, own + 2 * STAGED, LANES), vmem(slabs, staged, LANES), vmem(slabs, staged, LANES)]
         + [vmem(-(-(own + HALO) // LANES) * LANES, LANES)]
         + work(own)
-        + [DMA((2 * slabs,))],
+        + [DMA((3 * slabs,))],
         "outer_part",
         us=8,
     )(f, tops, level_set, from_right, from_left, got1, vx)
@@ -744,7 +747,7 @@
         insert,
         [(rows, cols), (rows, cols)],
         [SMEM, VMEM, VMEM, VMEM, HBM, HBM],
-        [DMA((slabs + 1,))],
+        [DMA((3 * (slabs - 1),))],
         "insert",
         out_specs=[HBM, HBM],
         aliases={4: 0, 5: 1},

time: 83.4 us -> 83.2 us (level)
    ppermute x1, waiting for transfers between devices: 0.9 us -> 0.02 us  [per_device(): from_partner2 = lax.ppermute(to_partner2, 'focus', swap)]
  transfers between devices with their start and end apart: 12 -> 12, of which waited for: 6 -> 4; matrix products, arithmetic and copies ran while one was open for 0% -> 0% of each run, Pallas kernels for 39% -> 39%
where the time goes in v6:
time: 83.2 us; the launch traced here: 83 us
  Pallas kernels  39.6 us (48%)
  starting transfers between devices  27.3 us (33%)
  waiting for transfers between devices  15.2 us (18%)
  between operations  0.92 us (1%)
    pallas_call x11, Pallas kernels, run(): kernel(*(pltpu.with_memory_space_constraint(x, pltpu.HBM) if spec is HBM...  39.6 us
    all_to_all x1, starting transfers between devices, per_device(): tops = lax.all_to_all(top, ('focus', 'gx', 'gy'), 0, 0)  8.83 us
    ppermute x1, starting transfers between devices, per_device(): from_right = lax.ppermute(left, 'gy', shifted(gy, -1))  6.28 us
    ppermute x1, waiting for transfers between devices, per_device(): from_left = lax.ppermute(right, 'gy', shifted(gy, 1))  4.94 us
    all_to_all x1, waiting for transfers between devices, per_device(): tops = lax.all_to_all(top, ('focus', 'gx', 'gy'), 0, 0)  4.76 us
    ppermute x1, waiting for transfers between devices, per_device(): got_fs = lax.ppermute(fs, 'focus', swap)  2.92 us
    ppermute x1, starting transfers between devices, per_device(): got2 = lax.ppermute(m2, ('focus', 'gx'), cross)  2.7 us
    ppermute x1, waiting for transfers between devices, per_device(): from_right = lax.ppermute(left, 'gy', shifted(gy, -1))  2.55 us
  transfers between devices with their start and end apart: 12, of which 4 were waited for; matrix products, arithmetic and copies ran while one was open for 0% of the time, Pallas kernels for 39%

profile of v6, /device:TPU:1, one launch (start us, length us, event | category | flops | bytes accessed | tf_op | source)
XLA Modules:
  0.0 83.0 jit_solution(14183912404302622952)
XLA Ops:
  0.6 0.0 copy-start
  0.6 1.9 %send_part.1 = f32[55,8,512]{2,1,0:T(8,128)S(1)} custom-call(s32[1]{0:T(128)} %bitcast.f_ref.refs_0_, f32[2]{0:T(128)} %w_hbm.3, f32[2,1024,512]{2,1,0:T(8,128)} %g_ref.3), custom_call_target="tpu_custom_call" | custom-call | flops 1000000000 | tf_op jit(solution)/shard_map/send_part/pallas_call | solution.py:54
  2.5 2.1 %collective-permute-start.5 = (f32[55,8,512]{2,1,0:T(8,128)S(1)}, f32[55,8,512]{2,1,0:T(8,128)S(1)}, u32[]{:S(2)}, u32[]{:S(2)}) collective-permute-start(f32[55,8,512]{2,1,0:T(8,128)S(1)} %send_part.1), channel_id=1, source_target_pairs={{0,64},{64,0},{1,65},{65,1},{2,66},{66,2},{3,67},{67,3},{4,68},{68... | collective-permute-start | bytes 2703368 | tf_op jit(solution)/shard_map/ppermute | solution.py:630
  4.6 0.0 copy-done
  4.6 2.5 %strips.1 = (f32[1024,512]{1,0:T(8,128)S(1)}, f32[40,1024]{1,0:T(8,128)S(1)}, f32[40,1024]{1,0:T(8,128)S(1)}) custom-call(f32[2]{0:T(128)} %w_hbm.3, f32[2,1024,512]{2,1,0:T(8,128)} %g_ref.3, f32[1024,512]{1,0:T(8,128)S(1)} %copy-done), custom_call_target="tpu_custom_call" | custom-call | flops 2000000000 | tf_op jit(solution)/shard_map/strips/pallas_call | solution.py:54
  7.1 6.3 %collective-permute-start = (f32[40,1024]{1,0:T(8,128)S(1)}, f32[40,1024]{1,0:T(8,128)S(1)}, u32[]{:S(2)}, u32[]{:S(2)}) collective-permute-start(f32[40,1024]{1,0:T(8,128)S(1)} %get-tuple-element.27), channel_id=1, source_target_pairs={{0,15},{1,0},{2,1},{3,2},{4,3},{5,4},{6,5},{7,6},{8,7},{9,8},{10,9... | collective-permute-start | bytes 491528 | tf_op jit(solution)/shard_map/ppermute | solution.py:641
  13.4 0.0 collective-permute-start.1
  13.4 2.5 %collective-permute-done.right_ref = f32[40,1024]{1,0:T(8,128)S(1)} collective-permute-done((f32[40,1024]{1,0:T(8,128)S(1)}, f32[40,1024]{1,0:T(8,128)S(1)}, u32[]{:S(2)}, u32[]{:S(2)}) %collective-permute-start) | collective-permute-done | bytes 163872 | tf_op jit(solution)/shard_map/ppermute | solution.py:641
  16.0 4.9 %collective-permute-done.1.left_ref = f32[40,1024]{1,0:T(8,128)S(1)} collective-permute-done((f32[40,1024]{1,0:T(8,128)S(1)}, f32[40,1024]{1,0:T(8,128)S(1)}, u32[]{:S(2)}, u32[]{:S(2)}) %collective-permute-start.1) | collective-permute-done | bytes 163872 | tf_op jit(solution)/shard_map/ppermute | solution.py:642
  20.9 0.1 row_messages.1
  21.0 2.7 %collective-permute-start.3 = (f32[24,640]{1,0:T(8,128)S(1)}, f32[24,640]{1,0:T(8,128)S(1)}, u32[]{:S(2)}, u32[]{:S(2)}) collective-permute-start(f32[24,640]{1,0:T(8,128)S(1)} %get-tuple-element.30), channel_id=1, source_target_pairs={{0,112},{16,64},{32,80},{48,96},{64,16},{80,32},{96,48},{112,0},{1... | collective-permute-start | bytes 184328 | tf_op jit(solution)/shard_map/ppermute | solution.py:658
  23.7 2.2 %collective-permute-start.2 = (f32[48,640]{1,0:T(8,128)S(1)}, f32[48,640]{1,0:T(8,128)S(1)}, u32[]{:S(2)}, u32[]{:S(2)}) collective-permute-start(f32[48,640]{1,0:T(8,128)S(1)} %get-tuple-element.29), channel_id=1, source_target_pairs={{0,16},{16,32},{32,48},{48,0},{64,112},{80,64},{96,80},{112,96},{1... | collective-permute-start | bytes 368648 | tf_op jit(solution)/shard_map/ppermute | solution.py:657
  26.0 0.0 collective-permute-start.4
  26.0 0.0 collective-permute-done.3.m2_ref.refs_2_
  26.0 0.1 send_rest.1
  26.1 1.6 %collective-permute-start.6 = (f32[14,8,512]{2,1,0:T(8,128)S(1)}, f32[14,8,512]{2,1,0:T(8,128)S(1)}, u32[]{:S(2)}, u32[]{:S(2)}) collective-permute-start(f32[14,8,512]{2,1,0:T(8,128)S(1)} %send_rest.1), channel_id=1, source_target_pairs={{0,64},{64,0},{1,65},{65,1},{2,66},{66,2},{3,67},{67,3},{4,68},{68... | collective-permute-start | bytes 688136 | tf_op jit(solution)/shard_map/ppermute | solution.py:667
  27.7 2.9 %collective-permute-done.4.fs_ref = f32[40,640]{1,0:T(8,128)S(1)} collective-permute-done((f32[40,640]{1,0:T(8,128)S(1)}, f32[40,640]{1,0:T(8,128)S(1)}, u32[]{:S(2)}, u32[]{:S(2)}) %collective-permute-start.4) | collective-permute-done | bytes 102432 | tf_op jit(solution)/shard_map/ppermute | solution.py:659
  30.6 0.0 collective-permute-done.2.m1_ref
  30.6 1.0 %half_setup.1 = (f32[69,8,640]{2,1,0:T(8,128)S(1)}, f32[69,8,640]{2,1,0:T(8,128)S(1)}, f32[69,8,640]{2,1,0:T(8,128)S(1)}) custom-call(s32[1]{0:T(128)} %bitcast.f_ref.refs_0_, f32[1024,512]{1,0:T(8,128)S(1)} %get-tuple-element.26.p_ref.refs_1_, f32[1024,512]{1,0:T(8,128)S(1)} %copy-done, f32[40,1024]{1,0:T(8,128)S(1)} %collective-permute-done.right_ref, ...), custom_call_target="tpu_custom_call" | custom-call | flops 2000000000 | tf_op jit(solution)/shard_map/half_setup/pallas_call | solution.py:54
  31.6 0.0 collective-permute-done.5.rp1_ref
  31.6 4.1 %velocity_begun.1 = (f32[71,8,640]{2,1,0:T(8,128)S(1)}, f32[71,8,640]{2,1,0:T(8,128)S(1)}) custom-call(f32[69,8,640]{2,1,0:T(8,128)S(1)} %get-tuple-element.32.t_ref, f32[55,8,512]{2,1,0:T(8,128)S(1)} %collective-permute-done.5.rp1_ref, f32[69,8,640]{2,1,0:T(8,128)S(1)} %get-tuple-element.33.q_ref, f32[69,8,640]{2,1,0:T(8,128)S(1)} %get-tuple-element.34.rec_ref), custom_call_target="tpu_custom_call" | custom-call | flops 4000000000 | tf_op jit(solution)/shard_map/velocity_begun/pallas_call | solution.py:54
  35.8 0.0 collective-permute-done.6.rp2_ref
  35.8 3.7 %velocity_ended.1 = (f32[69,8,640]{2,1,0:T(8,128)}, f32[208,512]{1,0:T(8,128)S(1)}, f32[104,512]{1,0:T(8,128)S(1)}, f32[128,128]{1,0:T(8,128)}) custom-call(s32[1]{0:T(128)} %bitcast.f_ref.refs_0_, f32[69,8,640]{2,1,0:T(8,128)S(1)} %get-tuple-element.32.t_ref, f32[55,8,512]{2,1,0:T(8,128)S(1)} %collective-permute-done.5.rp1_ref, ...), custom_call_target="tpu_custom_call" | custom-call | flops 5000000000 | tf_op jit(solution)/shard_map/velocity_ended/pallas_call | solution.py:54
  39.6 1.5 %collective-permute-start.7 = (f32[208,512]{1,0:T(8,128)S(1)}, f32[208,512]{1,0:T(8,128)S(1)}, u32[]{:S(2)}, u32[]{:S(2)}) collective-permute-start(f32[208,512]{1,0:T(8,128)S(1)} %get-tuple-element.39), channel_id=1, source_target_pairs={{0,64},{64,0},{1,65},{65,1},{2,66},{66,2},{3,67},{67,3},{4,68},{68... | collective-permute-start | bytes 1277960 | tf_op jit(solution)/shard_map/ppermute | solution.py:702
  41.0 8.8 %all-to-all-start = ((f32[128,1,128]{2,1,0:T(1,128)}), f32[128,1,128]{2,1,0:T(1,128)S(1)}, u32[]{:S(2)}, u32[]{:S(2)}) async-start(f32[128,1,128]{2,1,0:T(1,128)} %bitcast.2), calls=%async_computation | async-start | bytes 131072 | tf_op jit(solution)/shard_map/all_to_all | solution.py:703
  49.9 1.5 %collective-permute-start.10 = (f32[104,512]{1,0:T(8,128)S(1)}, f32[104,512]{1,0:T(8,128)S(1)}, u32[]{:S(2)}, u32[]{:S(2)}) collective-permute-start(f32[104,512]{1,0:T(8,128)S(1)} %get-tuple-element.44), channel_id=1, source_target_pairs={{0,64},{64,0},{1,65},{65,1},{2,66},{66,2},{3,67},{67,3},{4,68},{68... | collective-permute-start | bytes 638984 | tf_op jit(solution)/shard_map/ppermute | solution.py:704
  51.3 0.0 collective-permute-done.7.early_ref
  51.3 3.2 %velocity_rows.1 = (f32[5,560,128]{2,1,0:T(8,128)}, f32[240,512]{1,0:T(8,128)}, f32[1024,512]{1,0:T(8,128)}) custom-call(s32[1]{0:T(128)} %bitcast.f_ref.refs_0_, f32[69,8,640]{2,1,0:T(8,128)} %get-tuple-element.38.vs_hbm, f32[208,512]{1,0:T(8,128)S(1)} %collective-permute-done.7.early_ref), custom_call_target="tpu_custom_call" | custom-call | flops 60000002048 | tf_op jit(solution)/shard_map/velocity_rows/pallas_call | solution.py:54
  54.6 0.2 collective-permute-start.9
  54.7 4.8 %all-to-all-done = f32[128,1,128]{2,1,0:T(1,128)S(1)} async-done(((f32[128,1,128]{2,1,0:T(1,128)}), f32[128,1,128]{2,1,0:T(1,128)S(1)}, u32[]{:S(2)}, u32[]{:S(2)}) %all-to-all-start) | async-done | bytes 65568 | tf_op jit(solution)/shard_map/all_to_all | solution.py:703
  59.5 8.5 %outer_part.1 = (f32[256,512]{1,0:T(8,128)S(1)}, f32[5,544,128]{2,1,0:T(8,128)S(1)}, f32[5,272,128]{2,1,0:T(8,128)S(1)}) custom-call(s32[1]{0:T(128)} %bitcast.f_ref.refs_0_, f32[128,128]{1,0:T(8,128)S(1)} %bitcast.5, f32[1024,512]{1,0:T(8,128)} %ls_hbm.1, f32[40,1024]{1,0:T(8,128)S(1)} %collective-permute-done.right_ref, ...), custom_call_target="tpu_custom_call" | custom-call | flops 8000000000 | tf_op jit(solution)/shard_map/outer_part/pallas_call | solution.py:54
  68.0 0.4 collective-permute-start.8
  68.4 0.0 collective-permute-done.10.near_ref
  68.4 13.0 %middle_part.1 = (f32[1024,512]{1,0:T(8,128)}, f32[4,544,128]{2,1,0:T(8,128)S(1)}, f32[1024,512]{1,0:T(8,128)}) custom-call(s32[1]{0:T(128)} %bitcast.f_ref.refs_0_, f32[128,128]{1,0:T(8,128)S(1)} %bitcast.6, f32[5,272,128]{2,1,0:T(8,128)S(1)} %get-tuple-element.43.vm_ref, ...), custom_call_target="tpu_custom_call", output_to_operand_aliasing={{2}: (7, {})} | custom-call | flops 20000000000 | tf_op jit(solution)/shard_map/middle_part/pallas_call | solution.py:54
  81.4 0.0 collective-permute-done.9.far_ref
  81.4 0.0 collective-permute-done.8.theirs_ref
  81.4 1.4 %insert.1 = (f32[1024,512]{1,0:T(8,128)}, f32[1024,512]{1,0:T(8,128)}) custom-call(s32[1]{0:T(128)} %bitcast.f_ref.refs_0_, f32[256,512]{1,0:T(8,128)S(1)} %collective-permute-done.8.theirs_ref, f32[240,512]{1,0:T(8,128)S(1)} %collective-permute-done.9.far_ref, ...), custom_call_target="tpu_custom_call", output_to_operand_aliasing={{0}: (4, {}), {1}: (5, {})} | custom-call | flops 1000000000 | tf_op jit(solution)/shard_map/insert/pallas_call | solution.py:54
Async XLA Ops:
  0.6 4.0 %copy-start = (f32[1024,512]{1,0:T(8,128)S(1)}, f32[1024,512]{1,0:T(8,128)}, u32[]{:S(2)}) copy-start(f32[1024,512]{1,0:T(8,128)} %ls_hbm.1) | copy-start | bytes 6291460
  2.5 29.1 %collective-permute-start.5 = (f32[55,8,512]{2,1,0:T(8,128)S(1)}, f32[55,8,512]{2,1,0:T(8,128)S(1)}, u32[]{:S(2)}, u32[]{:S(2)}) collective-permute-start(f32[55,8,512]{2,1,0:T(8,128)S(1)} %send_part.1), channel_id=1, source_target_pairs={{0,64},{64,0},{1,65},{65,1},{2,66},{66,2},{3,67},{67,3},{4,68},{68... | collective-permute-start | bytes 2703368 | tf_op jit(solution)/shard_map/ppermute | solution.py:630
  7.1 8.8 %collective-permute-start = (f32[40,1024]{1,0:T(8,128)S(1)}, f32[40,1024]{1,0:T(8,128)S(1)}, u32[]{:S(2)}, u32[]{:S(2)}) collective-permute-start(f32[40,1024]{1,0:T(8,128)S(1)} %get-tuple-element.27), channel_id=1, source_target_pairs={{0,15},{1,0},{2,1},{3,2},{4,3},{5,4},{6,5},{7,6},{8,7},{9,8},{10,9... | collective-permute-start | bytes 491528 | tf_op jit(solution)/shard_map/ppermute | solution.py:641
  13.4 7.5 %collective-permute-start.1 = (f32[40,1024]{1,0:T(8,128)S(1)}, f32[40,1024]{1,0:T(8,128)S(1)}, u32[]{:S(2)}, u32[]{:S(2)}) collective-permute-start(f32[40,1024]{1,0:T(8,128)S(1)} %get-tuple-element.28), channel_id=1, source_target_pairs={{0,1},{1,2},{2,3},{3,4},{4,5},{5,6},{6,7},{7,8},{8,9},{9,10},{10,1... | collective-permute-start | bytes 491528 | tf_op jit(solution)/shard_map/ppermute | solution.py:642
  21.0 4.9 %collective-permute-start.3 = (f32[24,640]{1,0:T(8,128)S(1)}, f32[24,640]{1,0:T(8,128)S(1)}, u32[]{:S(2)}, u32[]{:S(2)}) collective-permute-start(f32[24,640]{1,0:T(8,128)S(1)} %get-tuple-element.30), channel_id=1, source_target_pairs={{0,112},{16,64},{32,80},{48,96},{64,16},{80,32},{96,48},{112,0},{1... | collective-permute-start | bytes 184328 | tf_op jit(solution)/shard_map/ppermute | solution.py:658
  23.7 6.8 %collective-permute-start.2 = (f32[48,640]{1,0:T(8,128)S(1)}, f32[48,640]{1,0:T(8,128)S(1)}, u32[]{:S(2)}, u32[]{:S(2)}) collective-permute-start(f32[48,640]{1,0:T(8,128)S(1)} %get-tuple-element.29), channel_id=1, source_target_pairs={{0,16},{16,32},{32,48},{48,0},{64,112},{80,64},{96,80},{112,96},{1... | collective-permute-start | bytes 368648 | tf_op jit(solution)/shard_map/ppermute | solution.py:657
  26.0 4.6 %collective-permute-start.4 = (f32[40,640]{1,0:T(8,128)S(1)}, f32[40,640]{1,0:T(8,128)S(1)}, u32[]{:S(2)}, u32[]{:S(2)}) collective-permute-start(f32[40,640]{1,0:T(8,128)S(1)} %get-tuple-element.31), channel_id=1, source_target_pairs={{0,64},{64,0},{1,65},{65,1},{2,66},{66,2},{3,67},{67,3},{4,68},{68... | collective-permute-start | bytes 307208 | tf_op jit(solution)/shard_map/ppermute | solution.py:659
  26.1 9.7 %collective-permute-start.6 = (f32[14,8,512]{2,1,0:T(8,128)S(1)}, f32[14,8,512]{2,1,0:T(8,128)S(1)}, u32[]{:S(2)}, u32[]{:S(2)}) collective-permute-start(f32[14,8,512]{2,1,0:T(8,128)S(1)} %send_rest.1), channel_id=1, source_target_pairs={{0,64},{64,0},{1,65},{65,1},{2,66},{66,2},{3,67},{67,3},{4,68},{68... | collective-permute-start | bytes 688136 | tf_op jit(solution)/shard_map/ppermute | solution.py:667
  39.6 11.8 %collective-permute-start.7 = (f32[208,512]{1,0:T(8,128)S(1)}, f32[208,512]{1,0:T(8,128)S(1)}, u32[]{:S(2)}, u32[]{:S(2)}) collective-permute-start(f32[208,512]{1,0:T(8,128)S(1)} %get-tuple-element.39), channel_id=1, source_target_pairs={{0,64},{64,0},{1,65},{65,1},{2,66},{66,2},{3,67},{67,3},{4,68},{68... | collective-permute-start | bytes 1277960 | tf_op jit(solution)/shard_map/ppermute | solution.py:702
  41.0 18.5 %all-to-all-start = ((f32[128,1,128]{2,1,0:T(1,128)}), f32[128,1,128]{2,1,0:T(1,128)S(1)}, u32[]{:S(2)}, u32[]{:S(2)}) async-start(f32[128,1,128]{2,1,0:T(1,128)} %bitcast.2), calls=%async_computation | async-start | bytes 131072 | tf_op jit(solution)/shard_map/all_to_all | solution.py:703
  49.9 18.6 %collective-permute-start.10 = (f32[104,512]{1,0:T(8,128)S(1)}, f32[104,512]{1,0:T(8,128)S(1)}, u32[]{:S(2)}, u32[]{:S(2)}) collective-permute-start(f32[104,512]{1,0:T(8,128)S(1)} %get-tuple-element.44), channel_id=1, source_target_pairs={{0,64},{64,0},{1,65},{65,1},{2,66},{66,2},{3,67},{67,3},{4,68},{68... | collective-permute-start | bytes 638984 | tf_op jit(solution)/shard_map/ppermute | solution.py:704
  54.6 26.9 %collective-permute-start.9 = (f32[240,512]{1,0:T(8,128)}, f32[240,512]{1,0:T(8,128)S(1)}, u32[]{:S(2)}, u32[]{:S(2)}) collective-permute-start(f32[240,512]{1,0:T(8,128)} %get-tuple-element.42), channel_id=1, source_target_pairs={{0,64},{64,0},{1,65},{65,1},{2,66},{66,2},{3,67},{67,3},{4,68},{68... | collective-permute-start | bytes 1474568 | tf_op jit(solution)/shard_map/ppermute | solution.py:714
  68.0 13.4 %collective-permute-start.8 = (f32[256,512]{1,0:T(8,128)S(1)}, f32[256,512]{1,0:T(8,128)S(1)}, u32[]{:S(2)}, u32[]{:S(2)}) collective-permute-start(f32[256,512]{1,0:T(8,128)S(1)} %get-tuple-element.41.mine_ref), channel_id=1, source_target_pairs={{0,64},{64,0},{1,65},{65,1},{2,66},{66,2},{3,67},{67,3},{4,68},{68... | collective-permute-start | bytes 1572872 | tf_op jit(solution)/shard_map/ppermute | solution.py:734

commit v7 on v6

--- a/solution.py
+++ b/solution.py
@@ -367,7 +367,7 @@
         copy.start()
         return copy
 
-    groups = shares(r, 3)
+    groups = shares(r, 6)
     loads = [begin(vs_hbm.at[pl.ds(at, n)], vs_ref.at[pl.ds(at, n)]) for at, n in groups]
     for load, (at, n) in zip(loads, groups):
         load.wait()
@@ -706,7 +706,7 @@
         velocity_rows,
         [(slabs, ext, LANES), (far, cols), (rows, cols)],
         [SMEM, HBM, VMEM],
-        [vmem(r, 8, wide), vmem(slabs, ext, LANES), DMA((3 * slabs + 3,))],
+        [vmem(r, 8, wide), vmem(slabs, ext, LANES), DMA((3 * slabs + 6,))],
         "velocity_rows",
         us=60,
         out_specs=[HBM, HBM, HBM],

time: 83.2 us -> 83.2 us (level)
  no operation moved by 1% of the time
where the time goes in v7:
time: 83.2 us; the launch traced here: 83 us
  Pallas kernels  39.8 us (48%)
  starting transfers between devices  27.3 us (33%)
  waiting for transfers between devices  15.1 us (18%)
  between operations  0.92 us (1%)
    pallas_call x11, Pallas kernels, run(): kernel(*(pltpu.with_memory_space_constraint(x, pltpu.HBM) if spec is HBM...  39.8 us
    all_to_all x1, starting transfers between devices, per_device(): tops = lax.all_to_all(top, ('focus', 'gx', 'gy'), 0, 0)  8.83 us
    ppermute x1, starting transfers between devices, per_device(): from_right = lax.ppermute(left, 'gy', shifted(gy, -1))  6.28 us
    ppermute x1, waiting for transfers between devices, per_device(): from_left = lax.ppermute(right, 'gy', shifted(gy, 1))  4.94 us
    all_to_all x1, waiting for transfers between devices, per_device(): tops = lax.all_to_all(top, ('focus', 'gx', 'gy'), 0, 0)  4.62 us
    ppermute x1, waiting for transfers between devices, per_device(): got_fs = lax.ppermute(fs, 'focus', swap)  2.92 us
    ppermute x1, starting transfers between devices, per_device(): got2 = lax.ppermute(m2, ('focus', 'gx'), cross)  2.7 us
    ppermute x1, waiting for transfers between devices, per_device(): from_right = lax.ppermute(left, 'gy', shifted(gy, -1))  2.55 us
  transfers between devices with their start and end apart: 12, of which 4 were waited for; matrix products, arithmetic and copies ran while one was open for 0% of the time, Pallas kernels for 39%

profile of v7, /device:TPU:1, one launch (start us, length us, event | category | flops | bytes accessed | tf_op | source)
XLA Modules:
  0.0 83.0 jit_solution(17762510550986919186)
XLA Ops:
  0.6 0.0 copy-start
  0.6 1.9 %send_part.1 = f32[55,8,512]{2,1,0:T(8,128)S(1)} custom-call(s32[1]{0:T(128)} %bitcast.f_ref.refs_0_, f32[2]{0:T(128)} %w_hbm.3, f32[2,1024,512]{2,1,0:T(8,128)} %g_ref.3), custom_call_target="tpu_custom_call" | custom-call | flops 1000000000 | tf_op jit(solution)/shard_map/send_part/pallas_call | solution.py:54
  2.5 2.1 %collective-permute-start.5 = (f32[55,8,512]{2,1,0:T(8,128)S(1)}, f32[55,8,512]{2,1,0:T(8,128)S(1)}, u32[]{:S(2)}, u32[]{:S(2)}) collective-permute-start(f32[55,8,512]{2,1,0:T(8,128)S(1)} %send_part.1), channel_id=1, source_target_pairs={{0,64},{64,0},{1,65},{65,1},{2,66},{66,2},{3,67},{67,3},{4,68},{68... | collective-permute-start | bytes 2703368 | tf_op jit(solution)/shard_map/ppermute | solution.py:630
  4.6 0.0 copy-done
  4.6 2.5 %strips.1 = (f32[1024,512]{1,0:T(8,128)S(1)}, f32[40,1024]{1,0:T(8,128)S(1)}, f32[40,1024]{1,0:T(8,128)S(1)}) custom-call(f32[2]{0:T(128)} %w_hbm.3, f32[2,1024,512]{2,1,0:T(8,128)} %g_ref.3, f32[1024,512]{1,0:T(8,128)S(1)} %copy-done), custom_call_target="tpu_custom_call" | custom-call | flops 2000000000 | tf_op jit(solution)/shard_map/strips/pallas_call | solution.py:54
  7.1 6.3 %collective-permute-start = (f32[40,1024]{1,0:T(8,128)S(1)}, f32[40,1024]{1,0:T(8,128)S(1)}, u32[]{:S(2)}, u32[]{:S(2)}) collective-permute-start(f32[40,1024]{1,0:T(8,128)S(1)} %get-tuple-element.27), channel_id=1, source_target_pairs={{0,15},{1,0},{2,1},{3,2},{4,3},{5,4},{6,5},{7,6},{8,7},{9,8},{10,9... | collective-permute-start | bytes 491528 | tf_op jit(solution)/shard_map/ppermute | solution.py:641
  13.4 0.0 collective-permute-start.1
  13.4 2.5 %collective-permute-done.right_ref = f32[40,1024]{1,0:T(8,128)S(1)} collective-permute-done((f32[40,1024]{1,0:T(8,128)S(1)}, f32[40,1024]{1,0:T(8,128)S(1)}, u32[]{:S(2)}, u32[]{:S(2)}) %collective-permute-start) | collective-permute-done | bytes 163872 | tf_op jit(solution)/shard_map/ppermute | solution.py:641
  16.0 4.9 %collective-permute-done.1.left_ref = f32[40,1024]{1,0:T(8,128)S(1)} collective-permute-done((f32[40,1024]{1,0:T(8,128)S(1)}, f32[40,1024]{1,0:T(8,128)S(1)}, u32[]{:S(2)}, u32[]{:S(2)}) %collective-permute-start.1) | collective-permute-done | bytes 163872 | tf_op jit(solution)/shard_map/ppermute | solution.py:642
  20.9 0.1 row_messages.1
  21.0 2.7 %collective-permute-start.3 = (f32[24,640]{1,0:T(8,128)S(1)}, f32[24,640]{1,0:T(8,128)S(1)}, u32[]{:S(2)}, u32[]{:S(2)}) collective-permute-start(f32[24,640]{1,0:T(8,128)S(1)} %get-tuple-element.30), channel_id=1, source_target_pairs={{0,112},{16,64},{32,80},{48,96},{64,16},{80,32},{96,48},{112,0},{1... | collective-permute-start | bytes 184328 | tf_op jit(solution)/shard_map/ppermute | solution.py:658
  23.7 2.2 %collective-permute-start.2 = (f32[48,640]{1,0:T(8,128)S(1)}, f32[48,640]{1,0:T(8,128)S(1)}, u32[]{:S(2)}, u32[]{:S(2)}) collective-permute-start(f32[48,640]{1,0:T(8,128)S(1)} %get-tuple-element.29), channel_id=1, source_target_pairs={{0,16},{16,32},{32,48},{48,0},{64,112},{80,64},{96,80},{112,96},{1... | collective-permute-start | bytes 368648 | tf_op jit(solution)/shard_map/ppermute | solution.py:657
  26.0 0.0 collective-permute-start.4
  26.0 0.0 collective-permute-done.3.m2_ref.refs_2_
  26.0 0.1 send_rest.1
  26.1 1.6 %collective-permute-start.6 = (f32[14,8,512]{2,1,0:T(8,128)S(1)}, f32[14,8,512]{2,1,0:T(8,128)S(1)}, u32[]{:S(2)}, u32[]{:S(2)}) collective-permute-start(f32[14,8,512]{2,1,0:T(8,128)S(1)} %send_rest.1), channel_id=1, source_target_pairs={{0,64},{64,0},{1,65},{65,1},{2,66},{66,2},{3,67},{67,3},{4,68},{68... | collective-permute-start | bytes 688136 | tf_op jit(solution)/shard_map/ppermute | solution.py:667
  27.7 2.9 %collective-permute-done.4.fs_ref = f32[40,640]{1,0:T(8,128)S(1)} collective-permute-done((f32[40,640]{1,0:T(8,128)S(1)}, f32[40,640]{1,0:T(8,128)S(1)}, u32[]{:S(2)}, u32[]{:S(2)}) %collective-permute-start.4) | collective-permute-done | bytes 102432 | tf_op jit(solution)/shard_map/ppermute | solution.py:659
  30.6 0.0 collective-permute-done.2.m1_ref
  30.6 1.0 %half_setup.1 = (f32[69,8,640]{2,1,0:T(8,128)S(1)}, f32[69,8,640]{2,1,0:T(8,128)S(1)}, f32[69,8,640]{2,1,0:T(8,128)S(1)}) custom-call(s32[1]{0:T(128)} %bitcast.f_ref.refs_0_, f32[1024,512]{1,0:T(8,128)S(1)} %get-tuple-element.26.p_ref.refs_1_, f32[1024,512]{1,0:T(8,128)S(1)} %copy-done, f32[40,1024]{1,0:T(8,128)S(1)} %collective-permute-done.right_ref, ...), custom_call_target="tpu_custom_call" | custom-call | flops 2000000000 | tf_op jit(solution)/shard_map/half_setup/pallas_call | solution.py:54
  31.6 0.0 collective-permute-done.5.rp1_ref
  31.6 4.1 %velocity_begun.1 = (f32[71,8,640]{2,1,0:T(8,128)S(1)}, f32[71,8,640]{2,1,0:T(8,128)S(1)}) custom-call(f32[69,8,640]{2,1,0:T(8,128)S(1)} %get-tuple-element.32.t_ref, f32[55,8,512]{2,1,0:T(8,128)S(1)} %collective-permute-done.5.rp1_ref, f32[69,8,640]{2,1,0:T(8,128)S(1)} %get-tuple-element.33.q_ref, f32[69,8,640]{2,1,0:T(8,128)S(1)} %get-tuple-element.34.rec_ref), custom_call_target="tpu_custom_call" | custom-call | flops 4000000000 | tf_op jit(solution)/shard_map/velocity_begun/pallas_call | solution.py:54
  35.8 0.0 collective-permute-done.6.rp2_ref
  35.8 3.7 %velocity_ended.1 = (f32[69,8,640]{2,1,0:T(8,128)}, f32[208,512]{1,0:T(8,128)S(1)}, f32[104,512]{1,0:T(8,128)S(1)}, f32[128,128]{1,0:T(8,128)}) custom-call(s32[1]{0:T(128)} %bitcast.f_ref.refs_0_, f32[69,8,640]{2,1,0:T(8,128)S(1)} %get-tuple-element.32.t_ref, f32[55,8,512]{2,1,0:T(8,128)S(1)} %collective-permute-done.5.rp1_ref, ...), custom_call_target="tpu_custom_call" | custom-call | flops 5000000000 | tf_op jit(solution)/shard_map/velocity_ended/pallas_call | solution.py:54
  39.6 1.5 %collective-permute-start.7 = (f32[208,512]{1,0:T(8,128)S(1)}, f32[208,512]{1,0:T(8,128)S(1)}, u32[]{:S(2)}, u32[]{:S(2)}) collective-permute-start(f32[208,512]{1,0:T(8,128)S(1)} %get-tuple-element.39), channel_id=1, source_target_pairs={{0,64},{64,0},{1,65},{65,1},{2,66},{66,2},{3,67},{67,3},{4,68},{68... | collective-permute-start | bytes 1277960 | tf_op jit(solution)/shard_map/ppermute | solution.py:702
  41.0 8.8 %all-to-all-start = ((f32[128,1,128]{2,1,0:T(1,128)}), f32[128,1,128]{2,1,0:T(1,128)S(1)}, u32[]{:S(2)}, u32[]{:S(2)}) async-start(f32[128,1,128]{2,1,0:T(1,128)} %bitcast.2), calls=%async_computation | async-start | bytes 131072 | tf_op jit(solution)/shard_map/all_to_all | solution.py:703
  49.9 1.5 %collective-permute-start.10 = (f32[104,512]{1,0:T(8,128)S(1)}, f32[104,512]{1,0:T(8,128)S(1)}, u32[]{:S(2)}, u32[]{:S(2)}) collective-permute-start(f32[104,512]{1,0:T(8,128)S(1)} %get-tuple-element.44), channel_id=1, source_target_pairs={{0,64},{64,0},{1,65},{65,1},{2,66},{66,2},{3,67},{67,3},{4,68},{68... | collective-permute-start | bytes 638984 | tf_op jit(solution)/shard_map/ppermute | solution.py:704
  51.3 0.0 collective-permute-done.7.early_ref
  51.3 3.4 %velocity_rows.1 = (f32[5,560,128]{2,1,0:T(8,128)}, f32[240,512]{1,0:T(8,128)}, f32[1024,512]{1,0:T(8,128)}) custom-call(s32[1]{0:T(128)} %bitcast.f_ref.refs_0_, f32[69,8,640]{2,1,0:T(8,128)} %get-tuple-element.38.vs_hbm, f32[208,512]{1,0:T(8,128)S(1)} %collective-permute-done.7.early_ref), custom_call_target="tpu_custom_call" | custom-call | flops 60000002048 | tf_op jit(solution)/shard_map/velocity_rows/pallas_call | solution.py:54
  54.7 0.2 collective-permute-start.9
  54.9 4.6 %all-to-all-done = f32[128,1,128]{2,1,0:T(1,128)S(1)} async-done(((f32[128,1,128]{2,1,0:T(1,128)}), f32[128,1,128]{2,1,0:T(1,128)S(1)}, u32[]{:S(2)}, u32[]{:S(2)}) %all-to-all-start) | async-done | bytes 65568 | tf_op jit(solution)/shard_map/all_to_all | solution.py:703
  59.5 8.5 %outer_part.1 = (f32[256,512]{1,0:T(8,128)S(1)}, f32[5,544,128]{2,1,0:T(8,128)S(1)}, f32[5,272,128]{2,1,0:T(8,128)S(1)}) custom-call(s32[1]{0:T(128)} %bitcast.f_ref.refs_0_, f32[128,128]{1,0:T(8,128)S(1)} %bitcast.5, f32[1024,512]{1,0:T(8,128)} %ls_hbm.1, f32[40,1024]{1,0:T(8,128)S(1)} %collective-permute-done.right_ref, ...), custom_call_target="tpu_custom_call" | custom-call | flops 8000000000 | tf_op jit(solution)/shard_map/outer_part/pallas_call | solution.py:54
  68.0 0.4 collective-permute-start.8
  68.4 0.0 collective-permute-done.10.near_ref
  68.4 13.0 %middle_part.1 = (f32[1024,512]{1,0:T(8,128)}, f32[4,544,128]{2,1,0:T(8,128)S(1)}, f32[1024,512]{1,0:T(8,128)}) custom-call(s32[1]{0:T(128)} %bitcast.f_ref.refs_0_, f32[128,128]{1,0:T(8,128)S(1)} %bitcast.6, f32[5,272,128]{2,1,0:T(8,128)S(1)} %get-tuple-element.43.vm_ref, ...), custom_call_target="tpu_custom_call", output_to_operand_aliasing={{2}: (7, {})} | custom-call | flops 20000000000 | tf_op jit(solution)/shard_map/middle_part/pallas_call | solution.py:54
  81.4 0.0 collective-permute-done.9.far_ref
  81.4 0.0 collective-permute-done.8.theirs_ref
  81.4 1.4 %insert.1 = (f32[1024,512]{1,0:T(8,128)}, f32[1024,512]{1,0:T(8,128)}) custom-call(s32[1]{0:T(128)} %bitcast.f_ref.refs_0_, f32[256,512]{1,0:T(8,128)S(1)} %collective-permute-done.8.theirs_ref, f32[240,512]{1,0:T(8,128)S(1)} %collective-permute-done.9.far_ref, ...), custom_call_target="tpu_custom_call", output_to_operand_aliasing={{0}: (4, {}), {1}: (5, {})} | custom-call | flops 1000000000 | tf_op jit(solution)/shard_map/insert/pallas_call | solution.py:54
Async XLA Ops:
  0.6 4.0 %copy-start = (f32[1024,512]{1,0:T(8,128)S(1)}, f32[1024,512]{1,0:T(8,128)}, u32[]{:S(2)}) copy-start(f32[1024,512]{1,0:T(8,128)} %ls_hbm.1) | copy-start | bytes 6291460
  2.5 29.1 %collective-permute-start.5 = (f32[55,8,512]{2,1,0:T(8,128)S(1)}, f32[55,8,512]{2,1,0:T(8,128)S(1)}, u32[]{:S(2)}, u32[]{:S(2)}) collective-permute-start(f32[55,8,512]{2,1,0:T(8,128)S(1)} %send_part.1), channel_id=1, source_target_pairs={{0,64},{64,0},{1,65},{65,1},{2,66},{66,2},{3,67},{67,3},{4,68},{68... | collective-permute-start | bytes 2703368 | tf_op jit(solution)/shard_map/ppermute | solution.py:630
  7.1 8.8 %collective-permute-start = (f32[40,1024]{1,0:T(8,128)S(1)}, f32[40,1024]{1,0:T(8,128)S(1)}, u32[]{:S(2)}, u32[]{:S(2)}) collective-permute-start(f32[40,1024]{1,0:T(8,128)S(1)} %get-tuple-element.27), channel_id=1, source_target_pairs={{0,15},{1,0},{2,1},{3,2},{4,3},{5,4},{6,5},{7,6},{8,7},{9,8},{10,9... | collective-permute-start | bytes 491528 | tf_op jit(solution)/shard_map/ppermute | solution.py:641
  13.4 7.5 %collective-permute-start.1 = (f32[40,1024]{1,0:T(8,128)S(1)}, f32[40,1024]{1,0:T(8,128)S(1)}, u32[]{:S(2)}, u32[]{:S(2)}) collective-permute-start(f32[40,1024]{1,0:T(8,128)S(1)} %get-tuple-element.28), channel_id=1, source_target_pairs={{0,1},{1,2},{2,3},{3,4},{4,5},{5,6},{6,7},{7,8},{8,9},{9,10},{10,1... | collective-permute-start | bytes 491528 | tf_op jit(solution)/shard_map/ppermute | solution.py:642
  21.0 4.9 %collective-permute-start.3 = (f32[24,640]{1,0:T(8,128)S(1)}, f32[24,640]{1,0:T(8,128)S(1)}, u32[]{:S(2)}, u32[]{:S(2)}) collective-permute-start(f32[24,640]{1,0:T(8,128)S(1)} %get-tuple-element.30), channel_id=1, source_target_pairs={{0,112},{16,64},{32,80},{48,96},{64,16},{80,32},{96,48},{112,0},{1... | collective-permute-start | bytes 184328 | tf_op jit(solution)/shard_map/ppermute | solution.py:658
  23.7 6.8 %collective-permute-start.2 = (f32[48,640]{1,0:T(8,128)S(1)}, f32[48,640]{1,0:T(8,128)S(1)}, u32[]{:S(2)}, u32[]{:S(2)}) collective-permute-start(f32[48,640]{1,0:T(8,128)S(1)} %get-tuple-element.29), channel_id=1, source_target_pairs={{0,16},{16,32},{32,48},{48,0},{64,112},{80,64},{96,80},{112,96},{1... | collective-permute-start | bytes 368648 | tf_op jit(solution)/shard_map/ppermute | solution.py:657
  26.0 4.6 %collective-permute-start.4 = (f32[40,640]{1,0:T(8,128)S(1)}, f32[40,640]{1,0:T(8,128)S(1)}, u32[]{:S(2)}, u32[]{:S(2)}) collective-permute-start(f32[40,640]{1,0:T(8,128)S(1)} %get-tuple-element.31), channel_id=1, source_target_pairs={{0,64},{64,0},{1,65},{65,1},{2,66},{66,2},{3,67},{67,3},{4,68},{68... | collective-permute-start | bytes 307208 | tf_op jit(solution)/shard_map/ppermute | solution.py:659
  26.1 9.7 %collective-permute-start.6 = (f32[14,8,512]{2,1,0:T(8,128)S(1)}, f32[14,8,512]{2,1,0:T(8,128)S(1)}, u32[]{:S(2)}, u32[]{:S(2)}) collective-permute-start(f32[14,8,512]{2,1,0:T(8,128)S(1)} %send_rest.1), channel_id=1, source_target_pairs={{0,64},{64,0},{1,65},{65,1},{2,66},{66,2},{3,67},{67,3},{4,68},{68... | collective-permute-start | bytes 688136 | tf_op jit(solution)/shard_map/ppermute | solution.py:667
  39.6 11.8 %collective-permute-start.7 = (f32[208,512]{1,0:T(8,128)S(1)}, f32[208,512]{1,0:T(8,128)S(1)}, u32[]{:S(2)}, u32[]{:S(2)}) collective-permute-start(f32[208,512]{1,0:T(8,128)S(1)} %get-tuple-element.39), channel_id=1, source_target_pairs={{0,64},{64,0},{1,65},{65,1},{2,66},{66,2},{3,67},{67,3},{4,68},{68... | collective-permute-start | bytes 1277960 | tf_op jit(solution)/shard_map/ppermute | solution.py:702
  41.0 18.5 %all-to-all-start = ((f32[128,1,128]{2,1,0:T(1,128)}), f32[128,1,128]{2,1,0:T(1,128)S(1)}, u32[]{:S(2)}, u32[]{:S(2)}) async-start(f32[128,1,128]{2,1,0:T(1,128)} %bitcast.2), calls=%async_computation | async-start | bytes 131072 | tf_op jit(solution)/shard_map/all_to_all | solution.py:703
  49.9 18.6 %collective-permute-start.10 = (f32[104,512]{1,0:T(8,128)S(1)}, f32[104,512]{1,0:T(8,128)S(1)}, u32[]{:S(2)}, u32[]{:S(2)}) collective-permute-start(f32[104,512]{1,0:T(8,128)S(1)} %get-tuple-element.44), channel_id=1, source_target_pairs={{0,64},{64,0},{1,65},{65,1},{2,66},{66,2},{3,67},{67,3},{4,68},{68... | collective-permute-start | bytes 638984 | tf_op jit(solution)/shard_map/ppermute | solution.py:704
  54.7 26.7 %collective-permute-start.9 = (f32[240,512]{1,0:T(8,128)}, f32[240,512]{1,0:T(8,128)S(1)}, u32[]{:S(2)}, u32[]{:S(2)}) collective-permute-start(f32[240,512]{1,0:T(8,128)} %get-tuple-element.42), channel_id=1, source_target_pairs={{0,64},{64,0},{1,65},{65,1},{2,66},{66,2},{3,67},{67,3},{4,68},{68... | collective-permute-start | bytes 1474568 | tf_op jit(solution)/shard_map/ppermute | solution.py:714
  68.0 13.4 %collective-permute-start.8 = (f32[256,512]{1,0:T(8,128)S(1)}, f32[256,512]{1,0:T(8,128)S(1)}, u32[]{:S(2)}, u32[]{:S(2)}) collective-permute-start(f32[256,512]{1,0:T(8,128)S(1)} %get-tuple-element.41.mine_ref), channel_id=1, source_target_pairs={{0,64},{64,0},{1,65},{65,1},{2,66},{66,2},{3,67},{67,3},{4,68},{68... | collective-permute-start | bytes 1572872 | tf_op jit(solution)/shard_map/ppermute | solution.py:734
